TPU v7x, 128 devices: a whole 4x4x4 slice. The times are simulated.
128 devices in a mesh: dp: 64 (over z, y, x), tp: 2 (over core).
Axes of the slice: x: 4, y: 4, z: 4, core: 2. Of those that a mesh axis runs over, the one named last changes fastest.
Arguments:
- moe_tokens: bfloat16 [8192, 3584], P('dp'), may hold values from -6 to 6
- slot_routes: int32 [8192, 8], P('dp'), may hold values from 0 to 127, all different within a row; in each aligned block of 128 rows (0 to 127, 128 to 255, ...) at most 10 rows name the same one
- route_gates: float32 [8192, 8], P('dp'), may hold values from 0.1 to 0.5
- w_in: bfloat16 [128, 3584, 1024], P('dp', None, 'tp'), may hold values from -0.09375 to 0.09375
- w_up: bfloat16 [128, 3584, 1024], P('dp', None, 'tp'), may hold values from -0.09375 to 0.09375
- w_out: bfloat16 [128, 1024, 3584], P('dp', 'tp'), may hold values from -0.1875 to 0.1875
- query_latent: bfloat16 [64, 128, 512], P('dp'), may hold values from -20 to 20
- query_rope: bfloat16 [64, 128, 64], P('dp'), may hold values from -4 to 4
- cache_latent: bfloat16 [64, 2048, 512], P('dp', 'tp'), may hold values from -5 to 5
- cache_rope: bfloat16 [64, 64, 2048], P('dp', None, 'tp'), may hold values from -4 to 4
- lengths: int32 [64], P('dp'), may hold values from 128 to 2048, as said below
Outputs:
- moe_out: bfloat16 [8192, 3584], P('dp', 'tp')
- attn_out: bfloat16 [64, 128, 512], P('dp')
Inputs may be any that keep to these rules, and one draw needn't show every extreme that they name: `slot_routes`: each row names 8 different slots; within the rows of one dp index (aligned blocks of 128 rows) no slot is named more than 10 times, a bound that some block reaches. `lengths`: some row has all 2048 positions.
All inputs are finite; a program needn't handle non-finite values.
Results may differ from a plain program's by a relative error of at most 0.0057.
Values may be sent and summed in bfloat16 or wider, within the bound.
No kernel may reach another device: no remote copies, remote signals or barrier semaphores. Data moves between devices by JAX's collectives and lax.ppermute only.
A program may use at most 128 MiB of HBM per device.

v0:
```python
import math

import jax
import jax.numpy as jnp
from jax import lax
from jax.sharding import PartitionSpec as P

softmax_scale = 192.0 ** (-0.5) * (0.1 * math.log(40.0) + 1.0) ** 2


def attention(query_latent, query_rope, cache_latent, cache_rope, lengths):
    local_span = cache_latent.shape[1]
    positions = lax.axis_index("tp") * local_span + jnp.arange(local_span, dtype=jnp.int32)
    visible = positions[None, None, :] < lengths[:, None, None]
    scores = (
        jnp.einsum("bhl,btl->bht", query_latent, cache_latent, preferred_element_type=jnp.float32)
        + jnp.einsum("bhr,brt->bht", query_rope, cache_rope, preferred_element_type=jnp.float32)
    ) * softmax_scale
    local_peak = jnp.max(jnp.where(visible, scores, -1e30), axis=2)
    row_peak = lax.pmax(local_peak, "tp")
    weights = jnp.where(visible, jnp.exp(scores - row_peak[:, :, None]), 0.0)
    local_total = jnp.sum(weights, axis=2)
    local_numer = jnp.einsum(
        "bht,btl->bhl",
        weights.astype(jnp.bfloat16),
        cache_latent,
        preferred_element_type=jnp.float32,
    )
    numerator, row_total = lax.psum((local_numer, local_total), "tp")
    return (numerator / row_total[:, :, None]).astype(jnp.bfloat16)


def body(
    moe_tokens,
    slot_routes,
    route_gates,
    w_in,
    w_up,
    w_out,
    query_latent,
    query_rope,
    cache_latent,
    cache_rope,
    lengths,
):
    tok_count, top_count = slot_routes.shape
    dp_count = lax.axis_size("dp")
    slots_local = w_in.shape[0]
    slot_count = slots_local * dp_count
    capacity = (top_count * tok_count + slot_count - 1) // slot_count + 2
    half_width = moe_tokens.shape[1] // lax.axis_size("tp")
    route_slots = slot_routes.reshape(-1)
    route_order = jnp.arange(route_slots.shape[0], dtype=jnp.int32)
    earlier = (route_slots[:, None] == route_slots[None, :]) & (
        route_order[None, :] < route_order[:, None]
    )
    slot_rank = jnp.sum(earlier.astype(jnp.int32), axis=1)
    buffer_index = route_slots * capacity + slot_rank
    buffer_ids = jnp.arange(slot_count * capacity, dtype=jnp.int32)
    placement = jnp.any(
        buffer_ids[:, None, None] == buffer_index.reshape(tok_count, top_count)[None, :, :], axis=2
    ).astype(jnp.bfloat16)
    outbound = jnp.dot(placement, moe_tokens, preferred_element_type=jnp.float32).astype(
        jnp.bfloat16
    )
    outbound = outbound.reshape(dp_count, slots_local, capacity, moe_tokens.shape[1])
    received = lax.all_to_all(outbound, "dp", split_axis=0, concat_axis=0, tiled=True)
    sources, slots_here, item_count, feature_count = received.shape
    slot_rows = jnp.transpose(received, (1, 0, 2, 3)).reshape(
        slots_here, sources * item_count, feature_count
    )
    gate_part = jnp.einsum("snd,sdh->snh", slot_rows, w_in, preferred_element_type=jnp.float32)
    up_part = jnp.einsum("snd,sdh->snh", slot_rows, w_up, preferred_element_type=jnp.float32)
    hidden = (jax.nn.silu(gate_part) * up_part).astype(jnp.bfloat16)
    partial_value = jnp.einsum("snh,shd->snd", hidden, w_out, preferred_element_type=jnp.float32)
    summed = lax.psum(partial_value, "tp").astype(jnp.bfloat16)
    shaped = jnp.transpose(summed.reshape(slots_here, sources, item_count, -1), (1, 0, 2, 3))
    returned = lax.all_to_all(shaped, "dp", split_axis=0, concat_axis=0, tiled=True)
    flat_back = returned.reshape(slot_count * capacity, -1)
    flat_back = lax.dynamic_slice_in_dim(
        flat_back, lax.axis_index("tp") * half_width, half_width, 1
    )
    picked = (
        jnp.take(flat_back, buffer_index, axis=0)
        .astype(jnp.float32)
        .reshape(tok_count, top_count, half_width)
    )
    moe_out = jnp.sum(picked * route_gates[:, :, None], axis=1).astype(jnp.bfloat16)
    attn_out = attention(query_latent, query_rope, cache_latent, cache_rope, lengths)
    return (moe_out, attn_out)


def solution(mesh):
    placed = (
        P("dp", None),
        P("dp", None),
        P("dp", None),
        P("dp", None, "tp"),
        P("dp", None, "tp"),
        P("dp", "tp", None),
        P("dp", None, None),
        P("dp", None, None),
        P("dp", "tp", None),
        P("dp", None, "tp"),
        P("dp"),
    )
    return jax.shard_map(
        body,
        mesh=mesh,
        in_specs=placed,
        out_specs=(P("dp", "tp"), P("dp", None, None)),
        check_vma=False,
    )
```

profile of v0, /device:TPU:1, one launch (start us, length us, event | category | flops | bytes accessed | tf_op | source)
XLA Modules:
  0.0 527.5 jit_solution(16675441144070925909)
XLA Ops:
  7.2 0.0 copy-start
  7.2 0.9 copy.42
  8.1 0.1 reshape.114
  8.1 0.5 convert_reduce_fusion
  8.7 0.1 reduce_sum.34
  8.8 0.7 compare_and_fusion
  9.5 4.6 fusion.4
  14.2 7.2 %convolution_convert_fusion = bf16[1280,3584]{1,0:T(8,128)(2,1)} fusion(pred[1280,128]{1,0:T(8,128)(4,1)S(1)} %fusion.4, bf16[128,3584]{1,0:T(8,128)(2,1)} %param.11), kind=kOutput, calls=%fused_computation.1 | convolution fusion | flops 1178992640 | bytes 10256384 | tf_op jit(solution)/shard_map/dot_general | solution.py:63
  21.4 14.2 %reshape.115 = bf16[64,2,10,3584]{3,2,1,0:T(8,128)(2,1)} reshape(bf16[1280,3584]{1,0:T(8,128)(2,1)} %convolution_convert_fusion) | data formatting | bytes 18350080 | tf_op jit(solution)/shard_map/reshape | solution.py:66
  35.6 17.8 %copy.45 = bf16[64,2,10,3584]{3,1,2,0:T(2,128)(2,1)} copy(bf16[64,2,10,3584]{3,2,1,0:T(8,128)(2,1)} %reshape.115) | data formatting | bytes 18350080 | tf_op jit(solution)/shard_map/reshape | solution.py:66
  53.4 0.0 copy-start.2
  53.4 0.0 copy-start.4
  53.4 0.0 copy-start.1
  53.4 12.3 %all-to-all-start = ((bf16[64,2,10,3584]{3,1,2,0:T(2,128)(2,1)}), bf16[64,2,10,3584]{3,1,2,0:T(2,128)(2,1)}, u32[]{:S(2)}, u32[]{:S(2)}) async-start(bf16[64,2,10,3584]{3,1,2,0:T(2,128)(2,1)} %copy.45), calls=%async_computation | async-start | bytes 18350080 | tf_op jit(solution)/shard_map/all_to_all | solution.py:67
  66.4 0.0 copy-done.2
  66.4 0.0 copy-done.4
  66.4 0.2 fusion.17
  66.7 0.0 copy-done
  66.7 0.0 copy-done.1
  66.7 0.6 select_reduce_fusion
  67.2 3.3 pmax.7
  70.5 0.2 fusion.11
  70.7 119.1 %all-to-all-done = bf16[64,2,10,3584]{3,1,2,0:T(2,128)(2,1)} async-done(((bf16[64,2,10,3584]{3,1,2,0:T(2,128)(2,1)}), bf16[64,2,10,3584]{3,1,2,0:T(2,128)(2,1)}, u32[]{:S(2)}, u32[]{:S(2)}) %all-to-all-start) | async-done | bytes 9175072 | tf_op jit(solution)/shard_map/all_to_all | solution.py:67
  189.9 12.2 %fusion = f32[2,640,512]{2,1,0:T(8,128)} fusion(bf16[2,3584,512]{2,1,0:T(8,128)(2,1)} %param.15, bf16[2,640,3584]{2,0,1:T(2,128)(2,1)} %bitcast.1), kind=kOutput, calls=%fused_computation.2 | convolution fusion | flops 4697620480 | bytes 19136512 | tf_op jit(solution)/shard_map/snd,sdh->snh/dot_general | solution.py:73
  202.1 11.8 %multiply_convert_fusion = bf16[2,640,512]{2,1,0:T(8,128)(2,1)S(1)} fusion(f32[2,640,512]{2,1,0:T(8,128)} %fusion, bf16[2,3584,512]{2,1,0:T(8,128)(2,1)} %param.14, bf16[2,640,3584]{2,0,1:T(2,128)(2,1)} %bitcast.1), kind=kOutput, calls=%fused_computation.13 | convolution fusion | flops 4701552640 | bytes 20447232 | tf_op jit(solution)/shard_map/snd,sdh->snh/dot_general | solution.py:72
  213.9 0.0 slice-done
  213.9 0.0 slice-done.1
  214.0 8.9 %fusion.24 = f32[2,640,3584]{2,1,0:T(8,128)} fusion(bf16[2,640,512]{2,1,0:T(8,128)(2,1)S(1)} %multiply_convert_fusion, bf16[2,512,3584]{2,1,0:T(8,128)(2,1)S(1)} %bitcast.44), kind=kOutput, calls=%fused_computation.40 | convolution fusion | flops 4697620480 | bytes 27000832 | tf_op jit(solution)/shard_map/snh,shd->snd/dot_general | solution.py:75
  222.8 51.9 %all-reduce.5 = (bf16[2,640,3584]{2,1,0:T(8,128)(2,1)}, f32[128]{0:T(128)S(1)}) all-reduce(f32[2,640,3584]{2,1,0:T(8,128)} %fusion.24, f32[128]{0:T(128)S(1)} %fusion.11), channel_id=1, replica_groups=mesh['dp'=64,'tp'=2] {'tp'}, use_global_device_ids=true, to_apply=%region_2.3 | all-reduce | flops 4587648 | bytes 27526144 | tf_op jit(solution)/shard_map/psum | solution.py:76
  274.7 37.9 %copy.48 = bf16[2,640,3584]{2,0,1:T(2,128)(2,1)} copy(bf16[2,640,3584]{2,1,0:T(8,128)(2,1)} %get-tuple-element.2) | data formatting | bytes 18350080 | tf_op jit(solution)/shard_map/convert_element_type | solution.py:76
  312.6 25.9 %all-to-all-start.1 = ((bf16[64,2,10,3584]{3,1,2,0:T(2,128)(2,1)}), bf16[64,2,10,3584]{3,1,2,0:T(2,128)(2,1)}, u32[]{:S(2)}, u32[]{:S(2)}) async-start(bf16[64,2,10,3584]{3,1,2,0:T(2,128)(2,1)} %bitcast.40), calls=%async_computation.1 | async-start | bytes 18350080 | tf_op jit(solution)/shard_map/all_to_all | solution.py:78
  338.5 0.0 all-reduce.4.cloned.1.call-start
  338.6 1.1 convolution_bitcast_fusion
  339.7 0.0 all-reduce.4.cloned.1.call-update
  339.7 0.0 copy-done.3
  339.7 0.1 copy.50
  339.8 0.1 mul.54
  339.9 0.0 copy-done.5
  339.9 0.1 copy.51
  340.0 0.1 copy.44
  340.2 27.5 %all-reduce.4.cloned.1.call-done = f32[1,128,512]{2,1,0:T(8,128)} async-done(((f32[1,128,512]{2,1,0:T(8,128)}), f32[1,128,512]{2,1,0:T(8,128)}) %all-reduce.4.cloned.1.call-update) | async-done | bytes 262160 | tf_op jit(solution)/shard_map/psum | solution.py:29
  367.6 1.7 divide_convert_fusion
  369.3 103.0 %all-to-all-done.1 = bf16[64,2,10,3584]{3,1,2,0:T(2,128)(2,1)} async-done(((bf16[64,2,10,3584]{3,1,2,0:T(2,128)(2,1)}), bf16[64,2,10,3584]{3,1,2,0:T(2,128)(2,1)}, u32[]{:S(2)}, u32[]{:S(2)}) %all-to-all-start.1) | async-done | bytes 9175072 | tf_op jit(solution)/shard_map/all_to_all | solution.py:78
  472.3 12.7 %copy.49 = bf16[64,2,10,3584]{3,2,1,0:T(8,128)(2,1)} copy(bf16[64,2,10,3584]{3,1,2,0:T(2,128)(2,1)} %all-to-all-done.1) | data formatting | bytes 18350080 | tf_op jit(solution)/shard_map/all_to_all | solution.py:78
  485.0 14.6 %reshape.118 = bf16[1280,3584]{1,0:T(8,128)(2,1)} reshape(bf16[64,2,10,3584]{3,2,1,0:T(8,128)(2,1)} %copy.49) | data formatting | bytes 18350080 | tf_op jit(solution)/shard_map/reshape | solution.py:79
  499.6 4.6 constant_dynamic-slice_fusion
  504.3 10.8 %gather_fusion = bf16[1024,1792]{1,0:T(8,128)(2,1)} fusion(bf16[1280,1792]{1,0:T(8,128)(2,1)} %constant_dynamic-slice_fusion, s32[1024]{0:T(1024)S(1)} %broadcast_clamp_fusion), kind=kCustom, calls=%fused_computation | custom fusion | bytes 7344128 | tf_op jit(solution)/shard_map/jit(_take)/gather | solution.py:84
  515.1 5.6 %multiply_reduce_fusion = bf16[128,1792]{1,0:T(8,128)(2,1)} fusion(bf16[1024,1792]{1,0:T(8,128)(2,1)} %gather_fusion, f32[128,8]{1,0:T(8,128)S(1)} %copy.51, pred[128,8]{1,0:T(8,128)(4,1)S(1)} %copy.44), kind=kLoop, calls=%fused_computation.6 | loop fusion | flops 7110656 | bytes 4133888 | tf_op jit(solution)/shard_map/reduce_sum | solution.py:88
  (10 shorter events, 0.1 us)
Async XLA Ops:
  7.2 59.5 %copy-start = (bf16[1,1024,512]{2,1,0:T(8,128)(2,1)S(1)}, bf16[1,1024,512]{2,1,0:T(8,128)(2,1)}, u32[]{:S(2)}) copy-start(bf16[1,1024,512]{2,1,0:T(8,128)(2,1)} %param.19) | copy-start | bytes 3145732
  53.4 13.0 %copy-start.2 = (bf16[1,64,1024]{2,1,0:T(8,128)(2,1)S(1)}, bf16[1,64,1024]{2,1,0:T(8,128)(2,1)}, u32[]{:S(2)}) copy-start(bf16[1,64,1024]{2,1,0:T(8,128)(2,1)} %param.20) | copy-start | bytes 393220
  53.4 13.0 %copy-start.4 = (bf16[1,128,64]{1,2,0:T(8,128)(2,1)S(1)}, bf16[1,128,64]{1,2,0:T(8,128)(2,1)}, u32[]{:S(2)}) copy-start(bf16[1,128,64]{1,2,0:T(8,128)(2,1)} %param.18) | copy-start | bytes 49156
  53.4 13.3 %copy-start.1 = (bf16[1,128,512]{2,1,0:T(8,128)(2,1)S(1)}, bf16[1,128,512]{2,1,0:T(8,128)(2,1)}, u32[]{:S(2)}) copy-start(bf16[1,128,512]{2,1,0:T(8,128)(2,1)} %param.17) | copy-start | bytes 393220
  53.4 136.5 %all-to-all-start = ((bf16[64,2,10,3584]{3,1,2,0:T(2,128)(2,1)}), bf16[64,2,10,3584]{3,1,2,0:T(2,128)(2,1)}, u32[]{:S(2)}, u32[]{:S(2)}) async-start(bf16[64,2,10,3584]{3,1,2,0:T(2,128)(2,1)} %copy.45), calls=%async_computation | async-start | bytes 18350080 | tf_op jit(solution)/shard_map/all_to_all | solution.py:67
  189.9 24.0 %slice-start = ((s8[7340032]{0:T(1024)(128)(4,1)}), s8[4194304]{0:T(1024)(128)(4,1)S(1)}, s32[]{:S(2)}) async-start(s8[7340032]{0:T(1024)(128)(4,1)} %bitcast.43), calls=%async_computation.3 | async-start | bytes 8388608
  202.1 11.8 %slice-start.1 = ((s8[7340032]{0:T(1024)(128)(4,1)}), s8[3145728]{0:T(1024)(128)(4,1)S(1)}, s32[]{:S(2)}) async-start(s8[7340032]{0:T(1024)(128)(4,1)} %bitcast.43), calls=%async_computation.4 | async-start | bytes 6291456
  312.6 27.1 %copy-start.3 = (s32[128,8]{0,1:T(8,128)S(1)}, s32[128,8]{0,1:T(8,128)}, u32[]{:S(2)}) copy-start(s32[128,8]{0,1:T(8,128)} %param.12) | copy-start | bytes 12292
  312.6 27.3 %copy-start.5 = (f32[128,8]{0,1:T(8,128)S(1)}, f32[128,8]{0,1:T(8,128)}, u32[]{:S(2)}) copy-start(f32[128,8]{0,1:T(8,128)} %param.13) | copy-start | bytes 12292
  312.6 159.7 %all-to-all-start.1 = ((bf16[64,2,10,3584]{3,1,2,0:T(2,128)(2,1)}), bf16[64,2,10,3584]{3,1,2,0:T(2,128)(2,1)}, u32[]{:S(2)}, u32[]{:S(2)}) async-start(bf16[64,2,10,3584]{3,1,2,0:T(2,128)(2,1)} %bitcast.40), calls=%async_computation.1 | async-start | bytes 18350080 | tf_op jit(solution)/shard_map/all_to_all | solution.py:78
  338.5 29.1 %all-reduce.4.cloned.1.call-start = ((), (), s32[]{:S(2)}) async-start(), calls=%async_computation.2 | async-start | bytes 524288 | tf_op jit(solution)/shard_map/psum | solution.py:29
Sparse Core Ops, SparseCore 0:
  342.4 25.1 all-reduce.3
where the time goes:
time: 533 us; the launch traced here: 527 us
  waiting for transfers between devices  250 us (47%)
  local copies, waits for them, and re-layouts  114 us (21%)
  blocking collectives  55.2 us (10%)
  matrix products  42 us (8%)
  starting transfers between devices  38.3 us (7%)
  between operations  14.9 us (3%)
  other arithmetic  13.4 us (3%)
    all_to_all x1, waiting for transfers between devices, body(): lax.all_to_all(outbound, 'dp', split_axis=0, concat_axis=0, tiled=True)  119 us
    all_to_all x1, waiting for transfers between devices, body(): lax.all_to_all(shaped, 'dp', split_axis=0, concat_axis=0, tiled=True)  103 us
    psum x1, blocking collectives, body(): summed = lax.psum(partial_value, 'tp').astype(jnp.bfloat16)  51.9 us
    convert_element_type x1, local copies, waits for them, and re-layouts, body(): summed = lax.psum(partial_value, 'tp').astype(jnp.bfloat16)  37.9 us
    reshape x2, local copies, waits for them, and re-layouts, body(): outbound.reshape(dp_count, slots_local, capacity, moe_tokens.shape[1])  31.9 us
    psum x1, waiting for transfers between devices, attention(): numerator, row_total = lax.psum((local_numer, local_total), 'tp')  27.5 us
    all_to_all x1, starting transfers between devices, body(): lax.all_to_all(shaped, 'dp', split_axis=0, concat_axis=0, tiled=True)  25.9 us
    reshape x1, local copies, waits for them, and re-layouts, body(): flat_back = returned.reshape(slot_count * capacity, -1)  14.6 us
  transfers between devices with their start and end apart: 3, of which 3 were waited for; matrix products, arithmetic and copies ran while one was open for 1% of the time, Pallas kernels for 0%

commit v1 on v0

v1 whole, which is shorter than its diff:
```python
import functools
import math

import jax
import jax.numpy as jnp
from jax import lax
from jax.experimental import pallas as pl
from jax.experimental.pallas import tpu as pltpu
from jax.sharding import PartitionSpec as P

softmax_scale = 192.0 ** (-0.5) * (0.1 * math.log(40.0) + 1.0) ** 2

GROUP = 512
BLOCK = 128
TILES = 5
MAIN = 8
REST = 2
CAP = 10
F32 = jnp.float32
BF16 = jnp.bfloat16
SWAP = ((0, 1), (1, 0))


def dot(a, b):
    return jnp.dot(a, b, preferred_element_type=F32)


def dot_nt(a, b):
    return lax.dot_general(a, b, (((1,), (1,)), ((), ())), preferred_element_type=F32)


def iota(shape, dim):
    return lax.broadcasted_iota(jnp.int32, shape, dim)


def rank_code(routes):
    tokens, top = routes.shape
    slots = iota((tokens, 128), 1)
    named = jnp.zeros((tokens, 128), F32)
    for k in range(top):
        named = named + (routes[:, k : k + 1] == slots).astype(F32)
    earlier = (iota((tokens, tokens), 1) < iota((tokens, tokens), 0)).astype(F32).astype(BF16)
    rank = dot(earlier, named.astype(BF16))
    return jnp.where(named > 0.0, rank, -1.0)


def dispatch_kernel(core_ref, routes_ref, tokens_ref, out_ref, main_ref, rest_ref):
    units = out_ref.shape[0] * MAIN

    @pl.when(pl.program_id(0) == 0)
    def _():
        code = rank_code(routes_ref[...]).astype(BF16)
        tokens = code.shape[0]
        unit = iota((units, 128), 0)
        owner = (iota((units, 128), 1) == 2 * (unit >> 3) + core_ref[0]).astype(F32).astype(BF16)
        spread = dot_nt(owner, code)
        unit = iota((units, tokens), 0)
        main_ref[...] = (spread == (unit & 7).astype(F32)).astype(F32).astype(BF16)
        rest = (spread == (MAIN + (unit & 1)).astype(F32)).astype(F32)
        block = (unit >> 1) & 3
        for f in range(4):
            rest_ref[:, f * tokens : (f + 1) * tokens] = jnp.where(block == f, rest, 0.0).astype(BF16)

    rows = tokens_ref[...]
    main = dot(main_ref[...], rows)
    for f in range(4):
        part = main[:, f * BLOCK : (f + 1) * BLOCK]
        out_ref[:, f] = part.reshape(-1, MAIN, BLOCK).astype(BF16)
    stacked = jnp.concatenate([rows[:, f * BLOCK : (f + 1) * BLOCK] for f in range(4)], axis=0)
    rest = dot(rest_ref[...], stacked)
    out_ref[:, 4] = rest.reshape(-1, MAIN, BLOCK).astype(BF16)


def dispatch(core, routes, tokens, dp_count):
    count, features = tokens.shape
    groups = features // GROUP
    units = dp_count * MAIN
    return pl.pallas_call(
        dispatch_kernel,
        grid=(groups,),
        in_specs=[
            pl.BlockSpec(memory_space=pltpu.SMEM),
            pl.BlockSpec(routes.shape, lambda g: (0, 0)),
            pl.BlockSpec((count, GROUP), lambda g: (0, g)),
        ],
        out_specs=pl.BlockSpec((dp_count, TILES, MAIN, BLOCK), lambda g: (0, g, 0, 0)),
        out_shape=jax.ShapeDtypeStruct((dp_count, TILES * groups, MAIN, BLOCK), BF16),
        scratch_shapes=[pltpu.VMEM((units, count), BF16), pltpu.VMEM((units, 4 * count), BF16)],
        compiler_params=pltpu.CompilerParams(vmem_limit_bytes=32 * 1024 * 1024),
        name="dispatch",
    )(core, routes, tokens)


def expert_kernel(
    core_ref,
    message_ref,
    in_own_ref,
    up_own_ref,
    in_far_ref,
    up_far_ref,
    out_own_ref,
    out_far_ref,
    back_ref,
    gate_acc,
    up_acc,
    hidden,
    pick,
    place,
):
    step = pl.program_id(0)
    groups = pl.num_programs(0) // 2
    units = message_ref.shape[0] * MAIN
    rest = message_ref.shape[0] * REST
    width = in_own_ref.shape[2]

    @pl.when(step == 0)
    def _():
        q, u = iota((4 * rest, units), 0), iota((4 * rest, units), 1)
        target = ((q & (rest - 1)) >> 1) * MAIN + (lax.div(q, rest)) * REST + (q & 1)
        pick[...] = (u == target).astype(F32).astype(BF16)
        u, q = iota((units, 4 * rest), 0), iota((units, 4 * rest), 1)
        target = ((q & (rest - 1)) >> 1) * MAIN + (lax.div(q, rest)) * REST + (q & 1)
        place[...] = (u == target).astype(F32).astype(BF16)
        gate_acc[...] = jnp.zeros_like(gate_acc)
        up_acc[...] = jnp.zeros_like(up_acc)

    @pl.when(step < groups)
    def _():
        main = jnp.concatenate(
            [message_ref[:, f].astype(F32).reshape(units, BLOCK).astype(BF16) for f in range(4)], axis=1
        )
        tail = message_ref[:, 4].astype(F32).reshape(units, BLOCK).astype(BF16)
        tail = dot(pick[...], tail).astype(BF16)
        tail = jnp.concatenate([tail[f * rest : (f + 1) * rest] for f in range(4)], axis=1)
        rows = jnp.concatenate([main, tail], axis=0)
        gate_acc[:, :width] += dot(rows, in_own_ref[0])
        up_acc[:, :width] += dot(rows, up_own_ref[0])
        gate_acc[:, width:] += dot(rows, in_far_ref[...])
        up_acc[:, width:] += dot(rows, up_far_ref[...])

    @pl.when(step == groups)
    def _():
        gate = gate_acc[...]
        hidden[...] = (gate / (1.0 + jnp.exp(-gate)) * up_acc[...]).astype(BF16)

    @pl.when(step >= groups)
    def _():
        value = dot(hidden[:, :width], out_own_ref[0]) + dot(hidden[:, width:], out_far_ref[...])
        for f in range(4):
            part = value[:units, f * BLOCK : (f + 1) * BLOCK]
            back_ref[:, f] = part.reshape(-1, MAIN, BLOCK).astype(BF16)
        tail = value[units:].astype(BF16)
        tail = jnp.concatenate([tail[:, f * BLOCK : (f + 1) * BLOCK] for f in range(4)], axis=0)
        back_ref[:, 4] = dot(place[...], tail).reshape(-1, MAIN, BLOCK).astype(BF16)


def experts(core, message, w_in, w_up, w_out, in_far, up_far, out_far):
    dp_count, tiles = message.shape[:2]
    groups = tiles // TILES
    width = w_in.shape[2]
    rows = dp_count * CAP
    units, rest = dp_count * MAIN, dp_count * REST

    def early(i):
        return jnp.minimum(i, groups - 1)

    def late(i):
        return jnp.maximum(i - groups, 0)

    return pl.pallas_call(
        expert_kernel,
        grid_spec=pltpu.PrefetchScalarGridSpec(
            num_scalar_prefetch=1,
            grid=(2 * groups,),
            in_specs=[
                pl.BlockSpec((dp_count, TILES, MAIN, BLOCK), lambda i, c: (0, early(i), 0, 0)),
                pl.BlockSpec((1, GROUP, width), lambda i, c: (c[0], early(i), 0)),
                pl.BlockSpec((1, GROUP, width), lambda i, c: (c[0], early(i), 0)),
                pl.BlockSpec((GROUP, width), lambda i, c: (early(i), 0)),
                pl.BlockSpec((GROUP, width), lambda i, c: (early(i), 0)),
                pl.BlockSpec((1, width, GROUP), lambda i, c: (c[0], 0, late(i))),
                pl.BlockSpec((width, GROUP), lambda i, c: (0, late(i))),
            ],
            out_specs=pl.BlockSpec((dp_count, TILES, MAIN, BLOCK), lambda i, c: (0, late(i), 0, 0)),
            scratch_shapes=[
                pltpu.VMEM((rows, 2 * width), F32),
                pltpu.VMEM((rows, 2 * width), F32),
                pltpu.VMEM((rows, 2 * width), BF16),
                pltpu.VMEM((4 * rest, units), BF16),
                pltpu.VMEM((units, 4 * rest), BF16),
            ],
        ),
        out_shape=jax.ShapeDtypeStruct(message.shape, BF16),
        compiler_params=pltpu.CompilerParams(vmem_limit_bytes=48 * 1024 * 1024),
        cost_estimate=pl.CostEstimate(
            flops=12 * rows * groups * GROUP * width, bytes_accessed=32 * 1024 * 1024, transcendentals=0
        ),
        name="experts",
    )(core, message, w_in, w_up, in_far, up_far, w_out, out_far)


def gates_kernel(core_ref, routes_ref, gates_ref, main_ref, rest_ref):
    routes, gates = routes_ref[...], gates_ref[...]
    tokens, top = routes.shape
    units = main_ref.shape[1]
    code = rank_code(routes).astype(BF16)
    slots = iota((tokens, 128), 1)
    value = jnp.zeros((tokens, 128), F32)
    for k in range(top):
        value = value + jnp.where(routes[:, k : k + 1] == slots, gates[:, k : k + 1], 0.0)
    high = value.astype(BF16)
    low = (value - high.astype(F32)).astype(BF16)
    unit = iota((128, units), 1)
    owner = (iota((128, units), 0) == 2 * (unit >> 3) + core_ref[0]).astype(F32).astype(BF16)
    spread = dot(code, owner)
    unit = iota((tokens, units), 1)
    block = (unit >> 1) & 3
    for part, source in enumerate((high, low)):
        gate = dot(source, owner)
        main = jnp.where(spread == (unit & 7).astype(F32), gate, 0.0)
        main_ref[part * tokens : (part + 1) * tokens] = main.astype(BF16)
        rest = jnp.where(spread == (MAIN + (unit & 1)).astype(F32), gate, 0.0)
        for f in range(4):
            at = (2 * f + part) * tokens
            rest_ref[at : at + tokens] = jnp.where(block == f, rest, 0.0).astype(BF16)


def spread_gates(core, routes, gates, dp_count):
    tokens = routes.shape[0]
    units = dp_count * MAIN
    whole = pl.BlockSpec(memory_space=pltpu.VMEM)
    return pl.pallas_call(
        gates_kernel,
        in_specs=[pl.BlockSpec(memory_space=pltpu.SMEM), whole, whole],
        out_specs=(whole, whole),
        out_shape=(
            jax.ShapeDtypeStruct((2 * tokens, units), BF16),
            jax.ShapeDtypeStruct((8 * tokens, units), BF16),
        ),
        compiler_params=pltpu.CompilerParams(vmem_limit_bytes=32 * 1024 * 1024),
        name="gates",
    )(core, routes, gates)


def combine_kernel(core_ref, back_ref, main_ref, rest_ref, keep_ref, send_ref):
    g = pl.program_id(0)
    units = main_ref.shape[1]
    tokens, half = keep_ref.shape
    blocks = half // BLOCK
    rows = jnp.concatenate(
        [back_ref[:, f].astype(F32).reshape(units, BLOCK).astype(BF16) for f in range(4)], axis=1
    )
    tail = back_ref[:, 4].astype(F32).reshape(units, BLOCK).astype(BF16)
    main = dot(main_ref[...], rows)
    rest = dot(rest_ref[...], tail)
    for f in range(4):
        lanes = slice(f * BLOCK, (f + 1) * BLOCK)
        at = 2 * f * tokens
        value = (
            main[:tokens, lanes]
            + main[tokens:, lanes]
            + rest[at : at + tokens]
            + rest[at + tokens : at + 2 * tokens]
        )
        index = 4 * g + f
        side = (index >= blocks).astype(jnp.int32)
        place = pl.ds(pl.multiple_of((index - side * blocks) * BLOCK, BLOCK), BLOCK)

        @pl.when(side == core_ref[0])
        def _():
            keep_ref[:, place] = value

        @pl.when(side != core_ref[0])
        def _():
            send_ref[:, place] = value


def combine(core, back, main, rest):
    dp_count, tiles = back.shape[:2]
    groups = tiles // TILES
    tokens, half = main.shape[0] // 2, groups * GROUP // 2
    out = jax.ShapeDtypeStruct((tokens, half), F32)
    return pl.pallas_call(
        combine_kernel,
        grid=(groups,),
        in_specs=[
            pl.BlockSpec(memory_space=pltpu.SMEM),
            pl.BlockSpec((dp_count, TILES, MAIN, BLOCK), lambda g: (0, g, 0, 0)),
            pl.BlockSpec(main.shape, lambda g: (0, 0)),
            pl.BlockSpec(rest.shape, lambda g: (0, 0)),
        ],
        out_specs=(pl.BlockSpec((tokens, half), lambda g: (0, 0)),) * 2,
        out_shape=(out, out),
        compiler_params=pltpu.CompilerParams(vmem_limit_bytes=32 * 1024 * 1024),
        name="combine",
    )(core, back, main, rest)


def attention(query_latent, query_rope, cache_latent, cache_rope, lengths):
    local_span = cache_latent.shape[1]
    positions = lax.axis_index("tp") * local_span + jnp.arange(local_span, dtype=jnp.int32)
    visible = positions[None, None, :] < lengths[:, None, None]
    scores = (
        jnp.einsum("bhl,btl->bht", query_latent, cache_latent, preferred_element_type=F32)
        + jnp.einsum("bhr,brt->bht", query_rope, cache_rope, preferred_element_type=F32)
    ) * softmax_scale
    peak = jnp.max(jnp.where(visible, scores, -1e30), axis=2, keepdims=True)
    weights = jnp.where(visible, jnp.exp(scores - peak), 0.0)
    total = jnp.sum(weights, axis=2, keepdims=True)
    numer = jnp.einsum("bht,btl->bhl", weights.astype(BF16), cache_latent, preferred_element_type=F32)
    both = jnp.concatenate(
        [numer, jnp.broadcast_to(total, total.shape[:2] + (64,)), jnp.broadcast_to(peak, peak.shape[:2] + (64,))],
        axis=2,
    )
    far = lax.ppermute(both, "tp", SWAP)
    lat = numer.shape[2]
    far_numer, far_total, far_peak = far[:, :, :lat], far[:, :, lat : lat + 1], far[:, :, lat + 64 : lat + 65]
    top = jnp.maximum(peak, far_peak)
    here, there = jnp.exp(peak - top), jnp.exp(far_peak - top)
    return ((numer * here + far_numer * there) / (total * here + far_total * there)).astype(BF16)


def body(
    moe_tokens,
    slot_routes,
    route_gates,
    w_in,
    w_up,
    w_out,
    query_latent,
    query_rope,
    cache_latent,
    cache_rope,
    lengths,
):
    dp_count = lax.axis_size("dp")
    index = lax.axis_index("tp")
    core = jnp.reshape(index, (1,)).astype(jnp.int32)
    outbound = dispatch(core, slot_routes, moe_tokens, dp_count)
    message = lax.all_to_all(outbound, "dp", split_axis=0, concat_axis=0, tiled=True)

    def swap(weight):
        return lax.ppermute(lax.dynamic_index_in_dim(weight, 1 - index, 0, False), "tp", SWAP)

    in_far, up_far, out_far = swap(w_in), swap(w_up), swap(w_out)
    gates_main, gates_rest = spread_gates(core, slot_routes, route_gates, dp_count)
    back = experts(core, message, w_in, w_up, w_out, in_far, up_far, out_far)
    returned = lax.all_to_all(back, "dp", split_axis=0, concat_axis=0, tiled=True)
    keep, send = combine(core, returned, gates_main, gates_rest)
    moe_out = (keep + lax.ppermute(send, "tp", SWAP)).astype(BF16)
    attn_out = attention(query_latent, query_rope, cache_latent, cache_rope, lengths)
    return (moe_out, attn_out)


def solution(mesh):
    placed = (
        P("dp", None),
        P("dp", None),
        P("dp", None),
        P("dp", None, "tp"),
        P("dp", None, "tp"),
        P("dp", "tp", None),
        P("dp", None, None),
        P("dp", None, None),
        P("dp", "tp", None),
        P("dp", None, "tp"),
        P("dp"),
    )
    return jax.shard_map(
        body,
        mesh=mesh,
        in_specs=placed,
        out_specs=(P("dp", "tp"), P("dp", None, None)),
        check_vma=False,
    )
```

time: 533 us -> 191 us (0.36)
  waiting for transfers between devices: 250 us -> 104 us
  local copies, waits for them, and re-layouts: 114 us -> 17.5 us
  blocking collectives: 55.2 us -> 0 us
  matrix products: 42 us -> 1.37 us
  Pallas kernels: 0 us -> 38.9 us
  between operations: 14.9 us -> 1.49 us
  starting transfers between devices: 38.3 us -> 25.7 us
  other arithmetic: 13.4 us -> 1.19 us
    all_to_all x1, waiting for transfers between devices: 119 us -> 36.9 us  [body(): lax.all_to_all(outbound, 'dp', split_axis=0, concat_axis=0, tiled=True)]
    psum x1 -> x0, blocking collectives: 51.9 us -> none  [body(): summed = lax.psum(partial_value, 'tp').astype(jnp.bfloat16)]
    all_to_all x1, waiting for transfers between devices: 103 us -> 55 us  [body(): lax.all_to_all(back, 'dp', split_axis=0, concat_axis=0, tiled=True)]
    reshape x4 -> x0, local copies, waits for them, and re-layouts: 46.6 us -> none  [the longest x2 31.9 us: body(): outbound.reshape(dp_count, slots_local, capacity, moe_tokens.shape[1])]
    dot_general x5 -> x1, matrix products: 41.2 us -> 0.56 us  [attention(): jnp.einsum('bht,btl->bhl', weights.astype(BF16), cache_latent, preferred_...]
    pallas_call x0 -> x4, Pallas kernels: none -> 38.9 us  [the longest x1 26 us: experts(): pl.pallas_call(expert_kernel, grid_spec=pltpu.PrefetchScalarGridSpec(num_...]
    convert_element_type x1 -> x0, local copies, waits for them, and re-layouts: 37.9 us -> none  [body(): summed = lax.psum(partial_value, 'tp').astype(jnp.bfloat16)]
    psum x1 -> x0, waiting for transfers between devices: 27.5 us -> none  [attention(): numerator, row_total = lax.psum((local_numer, local_total), 'tp')]
  transfers between devices with their start and end apart: 3 -> 7, of which waited for: 3 -> 5; matrix products, arithmetic and copies ran while one was open for 1% -> 5% of each run, Pallas kernels for 0% -> 0%
where the time goes in v1:
time: 191 us; the launch traced here: 190 us
  waiting for transfers between devices  104 us (54%)
  Pallas kernels  38.9 us (20%)
  starting transfers between devices  25.7 us (13%)
  local copies, waits for them, and re-layouts  17.5 us (9%)
    all_to_all x1, waiting for transfers between devices, body(): lax.all_to_all(back, 'dp', split_axis=0, concat_axis=0, tiled=True)  55 us
    all_to_all x1, waiting for transfers between devices, body(): lax.all_to_all(outbound, 'dp', split_axis=0, concat_axis=0, tiled=True)  36.9 us
    pallas_call x1, Pallas kernels, experts(): pl.pallas_call(expert_kernel, grid_spec=pltpu.PrefetchScalarGridSpec(num_...  26 us
    all_to_all x1, starting transfers between devices, body(): lax.all_to_all(outbound, 'dp', split_axis=0, concat_axis=0, tiled=True)  12.2 us
    unnamed x27, local copies, waits for them, and re-layouts  10.7 us
    all_to_all x1, starting transfers between devices, body(): lax.all_to_all(back, 'dp', split_axis=0, concat_axis=0, tiled=True)  10.1 us
    ppermute x3, waiting for transfers between devices, swap(): lax.ppermute(lax.dynamic_index_in_dim(weight, 1 - index, 0, False), 'tp',...  9.52 us
    pallas_call x1, Pallas kernels, combine(): pl.pallas_call(combine_kernel, grid=(groups,), in_specs=[pl.BlockSpec(mem...  8.03 us
  transfers between devices with their start and end apart: 7, of which 5 were waited for; matrix products, arithmetic and copies ran while one was open for 5% of the time, Pallas kernels for 0%

profile of v1, /device:TPU:1, one launch (start us, length us, event | category | flops | bytes accessed | tf_op | source)
XLA Modules:
  0.0 189.9 jit_solution(10438705988247799256)
XLA Ops:
  0.6 0.0 copy-start
  0.6 0.9 copy.25.routes_ref
  1.5 1.2 copy-done.2
  2.7 4.1 %dispatch.1 = bf16[64,35,8,128]{3,2,1,0:T(8,128)(2,1)S(1)} custom-call(s32[1]{0:T(128)} %bitcast.core_ref, s32[128,8]{1,0:T(8,128)S(1)} %copy.25.routes_ref, bf16[128,3584]{1,0:T(8,128)(2,1)S(1)} %copy-done.2), custom_call_target="tpu_custom_call" | custom-call | tf_op jit(solution)/shard_map/dispatch/pallas_call | solution.py:78
  6.8 0.0 copy-start.1
  6.8 2.1 %copy-done.1 = bf16[64,35,8,128]{3,2,1,0:T(8,128)(2,1)} copy-done((bf16[64,35,8,128]{3,2,1,0:T(8,128)(2,1)}, bf16[64,35,8,128]{3,2,1,0:T(8,128)(2,1)S(1)}, u32[]{:S(2)}) %copy-start.1) | copy-done | bytes 4587544
  9.0 12.2 %all-to-all-start = ((bf16[64,35,8,128]{3,2,1,0:T(8,128)(2,1)}), bf16[64,35,8,128]{3,2,1,0:T(8,128)(2,1)}, u32[]{:S(2)}, u32[]{:S(2)}) async-start(bf16[64,35,8,128]{3,2,1,0:T(8,128)(2,1)} %copy-done.1), calls=%async_computation | async-start | bytes 9175040 | tf_op jit(solution)/shard_map/all_to_all | solution.py:340
  21.2 2.3 %dynamic-slice_bitcast_fusion.2 = bf16[3584,512]{1,0:T(8,128)(2,1)S(1)} fusion(bf16[2,3584,512]{2,1,0:T(8,128)(2,1)} %in_own_ref.1, s32[]{:T(128)S(6)} %select_n.16), kind=kLoop, calls=%fused_computation.2 | loop fusion | bytes 7340036 | tf_op jit(solution)/shard_map/jit(dynamic_index_in_dim)/squeeze | solution.py:343
  23.4 1.0 collective-permute-start
  24.5 2.3 %dynamic-slice_bitcast_fusion.1 = bf16[3584,512]{1,0:T(8,128)(2,1)S(1)} fusion(bf16[2,3584,512]{2,1,0:T(8,128)(2,1)} %up_own_ref.1, s32[]{:T(128)S(6)} %select_n.16), kind=kLoop, calls=%fused_computation.1 | loop fusion | bytes 7340036 | tf_op jit(solution)/shard_map/jit(dynamic_index_in_dim)/squeeze | solution.py:343
  26.8 0.1 collective-permute-start.1
  26.9 2.3 %dynamic-slice_bitcast_fusion = bf16[512,3584]{1,0:T(8,128)(2,1)S(1)} fusion(bf16[2,512,3584]{2,1,0:T(8,128)(2,1)} %out_own_ref.1, s32[]{:T(128)S(6)} %select_n.16), kind=kLoop, calls=%fused_computation | loop fusion | bytes 7340036 | tf_op jit(solution)/shard_map/jit(dynamic_index_in_dim)/squeeze | solution.py:343
  29.1 0.6 collective-permute-start.2
  29.7 0.8 collective-permute-done.in_far_ref
  30.5 0.0 copy-start.3
  30.5 1.8 copy-done.3
  32.3 8.7 %collective-permute-done.1.up_far_ref = bf16[3584,512]{1,0:T(8,128)(2,1)S(1)} collective-permute-done((bf16[3584,512]{1,0:T(8,128)(2,1)S(1)}, bf16[3584,512]{1,0:T(8,128)(2,1)S(1)}, u32[]{:S(2)}, u32[]{:S(2)}) %collective-permute-start.1) | collective-permute-done | bytes 3670048 | tf_op jit(solution)/shard_map/ppermute | solution.py:343
  41.0 1.8 copy-done.11
  42.8 0.0 collective-permute-done.2.out_far_ref
  42.8 36.9 %all-to-all-done.message_ref = bf16[64,35,8,128]{3,2,1,0:T(8,128)(2,1)} async-done(((bf16[64,35,8,128]{3,2,1,0:T(8,128)(2,1)}), bf16[64,35,8,128]{3,2,1,0:T(8,128)(2,1)}, u32[]{:S(2)}, u32[]{:S(2)}) %all-to-all-start) | async-done | bytes 4587552 | tf_op jit(solution)/shard_map/all_to_all | solution.py:340
  79.7 2.0 %copy-done.4 = bf16[3584,512]{1,0:T(8,128)(2,1)S(1)} copy-done((bf16[3584,512]{1,0:T(8,128)(2,1)S(1)}, bf16[3584,512]{1,0:T(8,128)(2,1)}, u32[]{:S(2)}) %copy-start.4) | copy-done | bytes 3670040
  81.7 26.0 %experts.1 = bf16[64,35,8,128]{3,2,1,0:T(8,128)(2,1)} custom-call(s32[1]{0:T(128)} %bitcast.core_ref, bf16[64,35,8,128]{3,2,1,0:T(8,128)(2,1)} %all-to-all-done.message_ref, bf16[2,3584,512]{2,1,0:T(8,128)(2,1)} %in_own_ref.1, bf16[2,3584,512]{2,1,0:T(8,128)(2,1)} %up_own_ref.1, bf16[3584,512]{1,0:T(8,128)(2,1)S(1)} %copy-done.4, ...), custom_call_target="tpu_custom_call" | custom-call | flops 14092861440 | bytes 33554432 | tf_op jit(solution)/shard_map/experts/pallas_call | solution.py:170
  107.8 0.0 copy-start.9
  107.8 0.0 copy-start.7
  107.8 10.1 %all-to-all-start.1 = ((bf16[64,35,8,128]{3,2,1,0:T(8,128)(2,1)}), bf16[64,35,8,128]{3,2,1,0:T(8,128)(2,1)}, u32[]{:S(2)}, u32[]{:S(2)}) async-start(bf16[64,35,8,128]{3,2,1,0:T(8,128)(2,1)} %experts.1), calls=%async_computation.1 | async-start | bytes 9175040 | tf_op jit(solution)/shard_map/all_to_all | solution.py:348
  117.9 0.0 copy-done.10
  117.9 0.1 copy.27.gates_ref
  118.0 0.8 gates.1
  119.4 0.0 copy-done.8
  119.4 0.0 copy-done.9
  119.4 0.2 fusion.13
  119.7 0.0 copy-done
  119.7 0.0 copy-done.7
  119.7 0.6 select_reduce_fusion
  120.3 0.0 copy-start.5
  120.3 0.6 fusion.1
  120.9 55.0 %all-to-all-done.1.back_ref = bf16[64,35,8,128]{3,2,1,0:T(8,128)(2,1)} async-done(((bf16[64,35,8,128]{3,2,1,0:T(8,128)(2,1)}), bf16[64,35,8,128]{3,2,1,0:T(8,128)(2,1)}, u32[]{:S(2)}, u32[]{:S(2)}) %all-to-all-start.1) | async-done | bytes 4587552 | tf_op jit(solution)/shard_map/all_to_all | solution.py:348
  175.9 0.0 copy-done.5
  175.9 8.0 %combine.1 = (f32[128,1792]{1,0:T(8,128)S(1)}, f32[128,1792]{1,0:T(8,128)}) custom-call(s32[1]{0:T(128)} %bitcast.core_ref, bf16[64,35,8,128]{3,2,1,0:T(8,128)(2,1)} %all-to-all-done.1.back_ref, bf16[256,512]{1,0:T(8,128)(2,1)S(1)} %get-tuple-element.6.main_ref, bf16[1024,512]{1,0:T(8,128)(2,1)S(1)} %get-tuple-element.7.rest_ref), custom_call_target="tpu_custom_call" | custom-call | tf_op jit(solution)/shard_map/combine/pallas_call | solution.py:283
  183.9 1.7 collective-permute-start.3
  185.6 0.0 copy-done.6
  185.6 0.2 fusion.4
  185.9 0.1 collective-permute-start.4
  186.0 2.2 %collective-permute-done.4 = f32[1,128,640]{1,2,0:T(8,128)S(1)} collective-permute-done((f32[1,128,640]{1,2,0:T(8,128)S(1)}, f32[1,128,640]{1,2,0:T(8,128)S(1)}, u32[]{:S(2)}, u32[]{:S(2)}) %collective-permute-start.4) | collective-permute-done | bytes 327712 | tf_op jit(solution)/shard_map/ppermute | solution.py:315
  188.2 0.1 fusion.11
  188.3 0.8 copy.30
  189.0 0.0 collective-permute-done.3
  189.0 0.9 add_convert_fusion
  (11 shorter events, 0.1 us)
Async XLA Ops:
  0.6 119.1 %copy-start = (bf16[1,1024,512]{2,1,0:T(8,128)(2,1)S(1)}, bf16[1,1024,512]{2,1,0:T(8,128)(2,1)}, u32[]{:S(2)}) copy-start(bf16[1,1024,512]{2,1,0:T(8,128)(2,1)} %param.19) | copy-start | bytes 3145732
  1.5 1.2 copy-start.2
  6.8 2.1 %copy-start.1 = (bf16[64,35,8,128]{3,2,1,0:T(8,128)(2,1)}, bf16[64,35,8,128]{3,2,1,0:T(8,128)(2,1)S(1)}, u32[]{:S(2)}) copy-start(bf16[64,35,8,128]{3,2,1,0:T(8,128)(2,1)S(1)} %dispatch.1) | copy-start | bytes 13762564
  9.0 70.7 %all-to-all-start = ((bf16[64,35,8,128]{3,2,1,0:T(8,128)(2,1)}), bf16[64,35,8,128]{3,2,1,0:T(8,128)(2,1)}, u32[]{:S(2)}, u32[]{:S(2)}) async-start(bf16[64,35,8,128]{3,2,1,0:T(8,128)(2,1)} %copy-done.1), calls=%async_computation | async-start | bytes 9175040 | tf_op jit(solution)/shard_map/all_to_all | solution.py:340
  23.4 7.1 %collective-permute-start = (bf16[3584,512]{1,0:T(8,128)(2,1)S(1)}, bf16[3584,512]{1,0:T(8,128)(2,1)S(1)}, u32[]{:S(2)}, u32[]{:S(2)}) collective-permute-start(bf16[3584,512]{1,0:T(8,128)(2,1)S(1)} %dynamic-slice_bitcast_fusion.2), channel_id=1, source_target_pairs={{0,1},{1,0},{2,3},{3,2},{4,5},{5,4},{6,7},{7,6},{8,9},{9,8},{10,11... | collective-permute-start | bytes 11010056 | tf_op jit(solution)/shard_map/ppermute | solution.py:343
  26.8 14.3 %collective-permute-start.1 = (bf16[3584,512]{1,0:T(8,128)(2,1)S(1)}, bf16[3584,512]{1,0:T(8,128)(2,1)S(1)}, u32[]{:S(2)}, u32[]{:S(2)}) collective-permute-start(bf16[3584,512]{1,0:T(8,128)(2,1)S(1)} %dynamic-slice_bitcast_fusion.1), channel_id=1, source_target_pairs={{0,1},{1,0},{2,3},{3,2},{4,5},{5,4},{6,7},{7,6},{8,9},{9,8},{10,11... | collective-permute-start | bytes 11010056 | tf_op jit(solution)/shard_map/ppermute | solution.py:343
  29.1 13.7 %collective-permute-start.2 = (bf16[512,3584]{1,0:T(8,128)(2,1)S(1)}, bf16[512,3584]{1,0:T(8,128)(2,1)}, u32[]{:S(2)}, u32[]{:S(2)}) collective-permute-start(bf16[512,3584]{1,0:T(8,128)(2,1)S(1)} %dynamic-slice_bitcast_fusion), channel_id=1, source_target_pairs={{0,1},{1,0},{2,3},{3,2},{4,5},{5,4},{6,7},{7,6},{8,9},{9,8},{10,11... | collective-permute-start | bytes 11010056 | tf_op jit(solution)/shard_map/ppermute | solution.py:343
  30.5 1.8 copy-start.3
  41.0 1.8 copy-start.11
  79.7 2.0 %copy-start.4 = (bf16[3584,512]{1,0:T(8,128)(2,1)S(1)}, bf16[3584,512]{1,0:T(8,128)(2,1)}, u32[]{:S(2)}) copy-start(bf16[3584,512]{1,0:T(8,128)(2,1)} %copy-done.3) | copy-start | bytes 11010052
  107.8 10.1 %copy-start.10 = (f32[128,8]{0,1:T(8,128)S(1)}, f32[128,8]{0,1:T(8,128)}, u32[]{:S(2)}) copy-start(f32[128,8]{0,1:T(8,128)} %param.13) | copy-start | bytes 12292
  107.8 11.7 %copy-start.8 = (bf16[1,64,1024]{2,1,0:T(8,128)(2,1)S(1)}, bf16[1,64,1024]{2,1,0:T(8,128)(2,1)}, u32[]{:S(2)}) copy-start(bf16[1,64,1024]{2,1,0:T(8,128)(2,1)} %param.20) | copy-start | bytes 393220
  107.8 11.7 %copy-start.9 = (bf16[1,128,64]{1,2,0:T(8,128)(2,1)S(1)}, bf16[1,128,64]{1,2,0:T(8,128)(2,1)}, u32[]{:S(2)}) copy-start(bf16[1,128,64]{1,2,0:T(8,128)(2,1)} %param.18) | copy-start | bytes 49156
  107.8 11.9 %copy-start.7 = (bf16[1,128,512]{2,1,0:T(8,128)(2,1)S(1)}, bf16[1,128,512]{2,1,0:T(8,128)(2,1)}, u32[]{:S(2)}) copy-start(bf16[1,128,512]{2,1,0:T(8,128)(2,1)} %param.17) | copy-start | bytes 393220
  107.8 68.1 %all-to-all-start.1 = ((bf16[64,35,8,128]{3,2,1,0:T(8,128)(2,1)}), bf16[64,35,8,128]{3,2,1,0:T(8,128)(2,1)}, u32[]{:S(2)}, u32[]{:S(2)}) async-start(bf16[64,35,8,128]{3,2,1,0:T(8,128)(2,1)} %experts.1), calls=%async_computation.1 | async-start | bytes 9175040 | tf_op jit(solution)/shard_map/all_to_all | solution.py:348
  120.3 55.6 %copy-start.5 = (f32[128,1024]{1,0:T(8,128)}, f32[128,1024]{1,0:T(8,128)S(1)}, u32[]{:S(2)}) copy-start(f32[128,1024]{1,0:T(8,128)S(1)} %get-tuple-element.16) | copy-start | bytes 1572868
  175.9 9.7 %copy-start.6 = (f32[128,1024]{1,0:T(8,128)S(1)}, f32[128,1024]{1,0:T(8,128)}, u32[]{:S(2)}) copy-start(f32[128,1024]{1,0:T(8,128)} %copy-done.5) | copy-start | bytes 1572868
  183.9 5.1 %collective-permute-start.3 = (f32[128,1792]{1,0:T(8,128)}, f32[128,1792]{1,0:T(8,128)S(1)}, u32[]{:S(2)}, u32[]{:S(2)}) collective-permute-start(f32[128,1792]{1,0:T(8,128)} %get-tuple-element.9), channel_id=1, source_target_pairs={{0,1},{1,0},{2,3},{3,2},{4,5},{5,4},{6,7},{7,6},{8,9},{9,8},{10,11... | collective-permute-start | bytes 2752520 | tf_op jit(solution)/shard_map/ppermute | solution.py:350
  185.9 2.3 %collective-permute-start.4 = (f32[1,128,640]{1,2,0:T(8,128)S(1)}, f32[1,128,640]{1,2,0:T(8,128)S(1)}, u32[]{:S(2)}, u32[]{:S(2)}) collective-permute-start(f32[1,128,640]{1,2,0:T(8,128)S(1)} %pad_maximum_fusion), channel_id=1, source_target_pairs={{0,1},{1,0},{2,3},{3,2},{4,5},{5,4},{6,7},{7,6},{8,9},{9,8},{10,11... | collective-permute-start | bytes 983048 | tf_op jit(solution)/shard_map/ppermute | solution.py:315

commit v2 on v0

v2 whole, which is shorter than its diff:
```python
import math

import jax
import jax.numpy as jnp
from jax import lax
from jax.experimental import pallas as pl
from jax.experimental.pallas import tpu as pltpu
from jax.sharding import PartitionSpec as P

softmax_scale = 192.0 ** (-0.5) * (0.1 * math.log(40.0) + 1.0) ** 2

GROUP = 512
BLOCK = 128
TILES = 5
MAIN = 8
REST = 2
CAP = 10
F32 = jnp.float32
BF16 = jnp.bfloat16
SWAP = ((0, 1), (1, 0))
HBM = pl.BlockSpec(memory_space=pl.ANY)
VMEM = pl.BlockSpec(memory_space=pltpu.VMEM)
SMEM = pl.BlockSpec(memory_space=pltpu.SMEM)
PARAMS = pltpu.CompilerParams(vmem_limit_bytes=58 * 1024 * 1024)


def dot(a, b):
    return jnp.dot(a, b, preferred_element_type=F32)


def iota(shape, dim):
    return lax.broadcasted_iota(jnp.int32, shape, dim)


def one_hot(a, b):
    return (a == b).astype(F32).astype(BF16)


def tiles_of(ref, group):
    return ref.at[:, pl.ds(group * TILES, TILES)]


def features_of(group):
    return slice(group * GROUP, (group + 1) * GROUP)


def block_of(f):
    return slice(f * BLOCK, (f + 1) * BLOCK)


def unit_of(row, half):
    return ((row & (2 * half - 1)) >> 1) * MAIN + lax.div(row, 2 * half) * REST + (row & 1)


def fill_place(ref, dp_count):
    size = ref.shape[0]
    ref[...] = one_hot(iota((size, size), 0), unit_of(iota((size, size), 1), dp_count // 2))


def fill_pick(ref, dp_count):
    size = ref.shape[0]
    ref[...] = one_hot(iota((size, size), 1), unit_of(iota((size, size), 0), dp_count // 2))


def pack(value, place, ref, group):
    dp_count = ref.shape[0]
    main, half = dp_count * MAIN, dp_count // 2
    for f in range(4):
        ref[:, group * TILES + f] = value[:main, block_of(f)].astype(BF16).reshape(dp_count, MAIN, BLOCK)
    rest = value[main:].astype(BF16)
    sides = [rest[: 2 * half], rest[2 * half :]]
    sides = [jnp.concatenate([side[:, block_of(f)] for f in range(4)], axis=0) for side in sides]
    rest = dot(place, jnp.concatenate(sides, axis=1))
    for h in range(2):
        part = rest[:, block_of(h)].astype(BF16).reshape(half, MAIN, BLOCK)
        ref[h * half : (h + 1) * half, group * TILES + 4] = part


def unpack(ref, pick, group):
    dp_count = ref.shape[0]
    main, half = dp_count * MAIN, dp_count // 2
    rows = [ref[:, group * TILES + f].reshape(main, BLOCK) for f in range(4)]
    rest = ref[:, group * TILES + 4].reshape(main, BLOCK)
    rest = dot(pick, jnp.concatenate([rest[: main // 2], rest[main // 2 :]], axis=1)).astype(BF16)
    rest = [
        jnp.concatenate([rest[2 * half * f : 2 * half * (f + 1), block_of(h)] for f in range(4)], axis=1)
        for h in range(2)
    ]
    return jnp.concatenate([jnp.concatenate(rows, axis=1)] + rest, axis=0)


def row_of(index, dp_count):
    main = dp_count * MAIN
    first = index < main
    after = index - main
    return jnp.where(first, index >> 3, after >> 1), jnp.where(first, index & 7, MAIN + (after & 1))


def rank_code(routes):
    top, tokens = routes.shape
    slots = iota((128, tokens), 0)
    named = jnp.zeros((128, tokens), F32)
    for k in range(top):
        named = named + (routes[k : k + 1] == slots).astype(F32)
    earlier = (iota((tokens, tokens), 0) < iota((tokens, tokens), 1)).astype(F32).astype(BF16)
    rank = dot(named.astype(BF16), earlier)
    return jnp.where(named > 0.0, rank, -1.0)


def dispatch_kernel(core_ref, routes_ref, tokens_ref, out_ref, rows, chosen, place, packed, in_sem, out_sem):
    dp_count = out_ref.shape[0]
    groups = out_ref.shape[1] // TILES
    loads = [
        pltpu.make_async_copy(tokens_ref.at[:, features_of(g)], rows.at[:, features_of(g)], in_sem.at[g])
        for g in range(groups)
    ]
    stores = [
        pltpu.make_async_copy(tiles_of(packed, g), tiles_of(out_ref, g), out_sem.at[g]) for g in range(groups)
    ]
    for load in loads:
        load.start()
    fill_place(place, dp_count)
    code = rank_code(routes_ref[...]).astype(BF16)
    tokens = code.shape[1]
    count = dp_count * CAP
    owner, _ = row_of(iota((count, 128), 0), dp_count)
    spread = dot(one_hot(iota((count, 128), 1), 2 * owner + core_ref[0]), code)
    _, turn = row_of(iota((count, tokens), 0), dp_count)
    chosen[...] = one_hot(spread, turn.astype(F32))
    for g in range(groups):
        loads[g].wait()
        pack(dot(chosen[...], rows[:, features_of(g)]), place[...], packed, g)
        stores[g].start()
    for store in stores:
        store.wait()


def dispatch(core, routes, tokens, dp_count):
    count, features = tokens.shape
    groups = features // GROUP
    shape = (dp_count, TILES * groups, MAIN, BLOCK)
    return pl.pallas_call(
        dispatch_kernel,
        in_specs=[SMEM, VMEM, HBM],
        out_specs=HBM,
        out_shape=jax.ShapeDtypeStruct(shape, BF16),
        scratch_shapes=[
            pltpu.VMEM(tokens.shape, BF16),
            pltpu.VMEM((dp_count * CAP, count), BF16),
            pltpu.VMEM((4 * dp_count, 4 * dp_count), BF16),
            pltpu.VMEM(shape, BF16),
            pltpu.SemaphoreType.DMA((groups,)),
            pltpu.SemaphoreType.DMA((groups,)),
        ],
        compiler_params=PARAMS,
        name="dispatch",
    )(core, routes, tokens)


def stages_of(groups):
    edges = [0, 1] + list(range(3, groups, 2)) + [groups]
    return list(zip(edges[:-1], edges[1:]))


def expert_kernel(
    core_ref,
    message_ref,
    in_own_ref,
    up_own_ref,
    in_far_ref,
    up_far_ref,
    out_own_ref,
    out_far_ref,
    back_ref,
    message,
    rows,
    in_own,
    up_own,
    in_far,
    up_far,
    out_both,
    gate_sum,
    up_sum,
    hidden,
    packed,
    pick,
    place,
    message_sem,
    weight_sem,
    far_sem,
    back_sem,
):
    core = core_ref[0]
    dp_count = message.shape[0]
    groups = message.shape[1] // TILES
    width = in_own.shape[1]
    stages = stages_of(groups)
    copy = pltpu.make_async_copy

    def stage_copies(i):
        first, last = stages[i]
        part = pl.ds(first * GROUP, (last - first) * GROUP)
        parts = pl.ds(first * TILES, (last - first) * TILES)
        return [
            copy(message_ref.at[:, parts], message.at[:, parts], message_sem.at[i]),
            copy(in_own_ref.at[core, part], in_own.at[part], weight_sem.at[2 * i]),
            copy(up_own_ref.at[core, part], up_own.at[part], weight_sem.at[2 * i + 1]),
        ]

    far_copies = [
        copy(in_far_ref, in_far, far_sem.at[0]),
        copy(up_far_ref, up_far, far_sem.at[1]),
        copy(out_own_ref.at[core], out_both.at[pl.ds(0, width)], far_sem.at[2]),
        copy(out_far_ref, out_both.at[pl.ds(width, width)], far_sem.at[3]),
    ]
    staged = [stage_copies(i) for i in range(len(stages))]
    back_copies = [copy(tiles_of(packed, g), tiles_of(back_ref, g), back_sem.at[g]) for g in range(groups)]
    for group in staged[:2]:
        for each in group:
            each.start()
    fill_pick(pick, dp_count)
    fill_place(place, dp_count)

    for i, (first, last) in enumerate(stages):
        for each in staged[i]:
            each.wait()
        if i + 2 < len(stages):
            for each in staged[i + 2]:
                each.start()
        elif i + 2 == len(stages):
            for each in far_copies[:2]:
                each.start()
        else:
            for each in far_copies[2:]:
                each.start()
        for g in range(first, last):
            rows[:, features_of(g)] = unpack(message, pick[...], g)
        part = slice(first * GROUP, last * GROUP)
        gate = dot(rows[:, part], in_own[part])
        up = dot(rows[:, part], up_own[part])
        if i > 0:
            gate = gate + gate_sum[...]
            up = up + up_sum[...]
        if i + 1 < len(stages):
            gate_sum[...] = gate
            up_sum[...] = up
        else:
            hidden[:, :width] = (gate / (1.0 + jnp.exp(-gate)) * up).astype(BF16)
    for each in far_copies[:2]:
        each.wait()
    gate = dot(rows[...], in_far[...])
    up = dot(rows[...], up_far[...])
    hidden[:, width:] = (gate / (1.0 + jnp.exp(-gate)) * up).astype(BF16)
    for each in far_copies[2:]:
        each.wait()
    for g in range(groups):
        pack(dot(hidden[...], out_both[:, features_of(g)]), place[...], packed, g)
        back_copies[g].start()
    for each in back_copies:
        each.wait()


def experts(core, message, w_in, w_up, w_out, in_far, up_far, out_far):
    dp_count, tiles = message.shape[:2]
    groups = tiles // TILES
    features, width = in_far.shape
    count = dp_count * CAP
    stages = len(stages_of(groups))
    weight = pltpu.VMEM((features, width), BF16)
    total = pltpu.VMEM((count, width), F32)
    square = pltpu.VMEM((4 * dp_count, 4 * dp_count), BF16)
    return pl.pallas_call(
        expert_kernel,
        in_specs=[SMEM] + [HBM] * 7,
        out_specs=HBM,
        out_shape=jax.ShapeDtypeStruct(message.shape, BF16),
        scratch_shapes=[
            pltpu.VMEM(message.shape, BF16),
            pltpu.VMEM((count, features), BF16),
            weight,
            weight,
            weight,
            weight,
            pltpu.VMEM((2 * width, features), BF16),
            total,
            total,
            pltpu.VMEM((count, 2 * width), BF16),
            pltpu.VMEM(message.shape, BF16),
            square,
            square,
            pltpu.SemaphoreType.DMA((stages,)),
            pltpu.SemaphoreType.DMA((2 * stages,)),
            pltpu.SemaphoreType.DMA((4,)),
            pltpu.SemaphoreType.DMA((groups,)),
        ],
        compiler_params=PARAMS,
        cost_estimate=pl.CostEstimate(
            flops=12 * count * features * width, bytes_accessed=32 * 1024 * 1024, transcendentals=0
        ),
        name="experts",
    )(core, message, w_in, w_up, in_far, up_far, w_out, out_far)


def gates_kernel(core_ref, routes_ref, gates_ref, out_ref):
    routes, gates = routes_ref[...], gates_ref[...]
    top, tokens = routes.shape
    count = out_ref.shape[1]
    dp_count = count // CAP
    code = rank_code(routes).astype(BF16)
    slots = iota((128, tokens), 0)
    value = jnp.zeros((128, tokens), F32)
    for k in range(top):
        value = value + jnp.where(routes[k : k + 1] == slots, gates[k : k + 1], 0.0)
    high = value.astype(BF16)
    low = (value - high.astype(F32)).astype(BF16)
    owner, _ = row_of(iota((128, count), 1), dp_count)
    owner = one_hot(iota((128, count), 0), 2 * owner + core_ref[0])
    _, turn = row_of(iota((tokens, count), 1), dp_count)
    here = dot(code.T, owner) == turn.astype(F32)
    for part, source in enumerate((high, low)):
        gate = jnp.where(here, dot(source.T, owner), 0.0)
        out_ref[part * tokens : (part + 1) * tokens] = gate.astype(BF16)


def spread_gates(core, routes, gates, dp_count):
    return pl.pallas_call(
        gates_kernel,
        in_specs=[SMEM, VMEM, VMEM],
        out_specs=VMEM,
        out_shape=jax.ShapeDtypeStruct((2 * routes.shape[1], dp_count * CAP), BF16),
        name="gates",
    )(core, routes, gates)


def combine_kernel(core_ref, back_ref, gates_ref, keep_ref, send_ref, message, total, pick, sem, out_sem):
    core = core_ref[0]
    dp_count = message.shape[0]
    groups = message.shape[1] // TILES
    tokens, half = keep_ref.shape
    loads = [
        pltpu.make_async_copy(tiles_of(back_ref, g), tiles_of(message, g), sem.at[g]) for g in range(groups)
    ]

    def store(side):
        part = total.at[:, pl.ds(side * half, half)]
        keep = pltpu.make_async_copy(part, keep_ref, out_sem.at[0])
        send = pltpu.make_async_copy(part, send_ref, out_sem.at[1])
        return keep, send

    for load in loads:
        load.start()
    fill_pick(pick, dp_count)
    side = 0
    for g in range(groups):
        loads[g].wait()
        value = dot(gates_ref[...], unpack(message, pick[...], g))
        total[:, features_of(g)] = value[:tokens] + value[tokens:]
        if (g + 1) * GROUP >= (side + 1) * half:
            keep, send = store(side)

            @pl.when(core == side)
            def _():
                keep.start()

            @pl.when(core != side)
            def _():
                send.start()

            side += 1
    keep, send = store(0)
    keep.wait()
    send.wait()


def combine(core, back, gates):
    dp_count, tiles = back.shape[:2]
    groups = tiles // TILES
    tokens = gates.shape[0] // 2
    out = jax.ShapeDtypeStruct((tokens, groups * GROUP // 2), F32)
    return pl.pallas_call(
        combine_kernel,
        in_specs=[SMEM, HBM, VMEM],
        out_specs=(HBM, HBM),
        out_shape=(out, out),
        scratch_shapes=[
            pltpu.VMEM(back.shape, BF16),
            pltpu.VMEM((tokens, groups * GROUP), F32),
            pltpu.VMEM((4 * dp_count, 4 * dp_count), BF16),
            pltpu.SemaphoreType.DMA((groups,)),
            pltpu.SemaphoreType.DMA((2,)),
        ],
        compiler_params=PARAMS,
        name="combine",
    )(core, back, gates)


def attention(query_latent, query_rope, cache_latent, cache_rope, lengths):
    local_span = cache_latent.shape[1]
    positions = lax.axis_index("tp") * local_span + jnp.arange(local_span, dtype=jnp.int32)
    visible = positions[None, None, :] < lengths[:, None, None]
    scores = (
        jnp.einsum("bhl,btl->bht", query_latent, cache_latent, preferred_element_type=F32)
        + jnp.einsum("bhr,brt->bht", query_rope, cache_rope, preferred_element_type=F32)
    ) * softmax_scale
    peak = jnp.max(jnp.where(visible, scores, -1e30), axis=2, keepdims=True)
    weights = jnp.where(visible, jnp.exp(scores - peak), 0.0)
    total = jnp.sum(weights, axis=2, keepdims=True)
    numer = jnp.einsum("bht,btl->bhl", weights.astype(BF16), cache_latent, preferred_element_type=F32)
    both = jnp.concatenate(
        [numer, jnp.broadcast_to(total, total.shape[:2] + (64,)), jnp.broadcast_to(peak, peak.shape[:2] + (64,))],
        axis=2,
    )
    far = lax.ppermute(both, "tp", SWAP)
    lat = numer.shape[2]
    far_numer, far_total, far_peak = far[:, :, :lat], far[:, :, lat : lat + 1], far[:, :, lat + 64 : lat + 65]
    top = jnp.maximum(peak, far_peak)
    here, there = jnp.exp(peak - top), jnp.exp(far_peak - top)
    return ((numer * here + far_numer * there) / (total * here + far_total * there)).astype(BF16)


def body(
    moe_tokens,
    slot_routes,
    route_gates,
    w_in,
    w_up,
    w_out,
    query_latent,
    query_rope,
    cache_latent,
    cache_rope,
    lengths,
):
    dp_count = lax.axis_size("dp")
    index = lax.axis_index("tp")
    core = jnp.reshape(index, (1,)).astype(jnp.int32)
    routes = slot_routes.T
    outbound = dispatch(core, routes, moe_tokens, dp_count)
    message = lax.all_to_all(outbound, "dp", split_axis=0, concat_axis=0, tiled=True)

    def swap(weight):
        return lax.ppermute(lax.dynamic_index_in_dim(weight, 1 - index, 0, False), "tp", SWAP)

    in_far, up_far, out_far = swap(w_in), swap(w_up), swap(w_out)
    gates = spread_gates(core, routes, route_gates.T, dp_count)
    back = experts(core, message, w_in, w_up, w_out, in_far, up_far, out_far)
    returned = lax.all_to_all(back, "dp", split_axis=0, concat_axis=0, tiled=True)
    keep, send = combine(core, returned, gates)
    moe_out = (keep + lax.ppermute(send, "tp", SWAP)).astype(BF16)
    attn_out = attention(query_latent, query_rope, cache_latent, cache_rope, lengths)
    return (moe_out, attn_out)


def solution(mesh):
    placed = (
        P("dp", None),
        P("dp", None),
        P("dp", None),
        P("dp", None, "tp"),
        P("dp", None, "tp"),
        P("dp", "tp", None),
        P("dp", None, None),
        P("dp", None, None),
        P("dp", "tp", None),
        P("dp", None, "tp"),
        P("dp"),
    )
    return jax.shard_map(
        body,
        mesh=mesh,
        in_specs=placed,
        out_specs=(P("dp", "tp"), P("dp", None, None)),
        check_vma=False,
    )
```

time: 533 us -> 179 us (0.34); the launches traced: 527 us -> 179 us
  waiting for transfers between devices: 250 us -> 104 us
  local copies, waits for them, and re-layouts: 114 us -> 9.45 us
  blocking collectives: 55.2 us -> 0 us
  matrix products: 42 us -> 1.38 us
  Pallas kernels: 0 us -> 34 us
  between operations: 14.9 us -> 1.47 us
  starting transfers between devices: 38.3 us -> 26 us
  other arithmetic: 13.4 us -> 2.37 us
    all_to_all x1, waiting for transfers between devices: 119 us -> 38.5 us  [body(): lax.all_to_all(outbound, 'dp', split_axis=0, concat_axis=0, tiled=True)]
    psum x1 -> x0, blocking collectives: 51.9 us -> none  [body(): summed = lax.psum(partial_value, 'tp').astype(jnp.bfloat16)]
    all_to_all x1, waiting for transfers between devices: 103 us -> 54.1 us  [body(): lax.all_to_all(back, 'dp', split_axis=0, concat_axis=0, tiled=True)]
    reshape x4 -> x0, local copies, waits for them, and re-layouts: 46.6 us -> none  [the longest x2 31.9 us: body(): outbound.reshape(dp_count, slots_local, capacity, moe_tokens.shape[1])]
    dot_general x5 -> x1, matrix products: 41.2 us -> 0.57 us  [attention(): jnp.einsum('bht,btl->bhl', weights.astype(BF16), cache_latent, preferred_...]
    convert_element_type x1 -> x0, local copies, waits for them, and re-layouts: 37.9 us -> none  [body(): summed = lax.psum(partial_value, 'tp').astype(jnp.bfloat16)]
    pallas_call x0 -> x4, Pallas kernels: none -> 34 us  [the longest x1 19.5 us: experts(): pl.pallas_call(expert_kernel, in_specs=[SMEM] + [HBM] * 7, out_specs=HBM,...]
    psum x1 -> x0, waiting for transfers between devices: 27.5 us -> none  [attention(): numerator, row_total = lax.psum((local_numer, local_total), 'tp')]
  transfers between devices with their start and end apart: 3 -> 7, of which waited for: 3 -> 6; matrix products, arithmetic and copies ran while one was open for 1% -> 5% of each run, Pallas kernels for 0% -> 1%
where the time goes in v2:
time: 179 us
  waiting for transfers between devices  104 us (58%)
  Pallas kernels  34 us (19%)
  starting transfers between devices  26 us (15%)
  local copies, waits for them, and re-layouts  9.45 us (5%)
  other arithmetic  2.37 us (1%)
    all_to_all x1, waiting for transfers between devices, body(): lax.all_to_all(back, 'dp', split_axis=0, concat_axis=0, tiled=True)  54.1 us
    all_to_all x1, waiting for transfers between devices, body(): lax.all_to_all(outbound, 'dp', split_axis=0, concat_axis=0, tiled=True)  38.5 us
    pallas_call x1, Pallas kernels, experts(): pl.pallas_call(expert_kernel, in_specs=[SMEM] + [HBM] * 7, out_specs=HBM,...  19.5 us
    all_to_all x1, starting transfers between devices, body(): lax.all_to_all(outbound, 'dp', split_axis=0, concat_axis=0, tiled=True)  12.2 us
    all_to_all x1, starting transfers between devices, body(): lax.all_to_all(back, 'dp', split_axis=0, concat_axis=0, tiled=True)  10.1 us
    ppermute x3, waiting for transfers between devices, swap(): lax.ppermute(lax.dynamic_index_in_dim(weight, 1 - index, 0, False), 'tp',...  9.44 us
    squeeze x3, local copies, waits for them, and re-layouts, swap(): lax.dynamic_index_in_dim(weight, 1 - index, 0, False)  6.83 us
    pallas_call x1, Pallas kernels, dispatch(): pl.pallas_call(dispatch_kernel, in_specs=[SMEM, VMEM, HBM], out_specs=HBM...  6.4 us
  transfers between devices with their start and end apart: 7, of which 6 were waited for; matrix products, arithmetic and copies ran while one was open for 5% of the time, Pallas kernels for 1%

profile of v2, /device:TPU:1, one launch (start us, length us, event | category | flops | bytes accessed | tf_op | source)
XLA Modules:
  0.0 178.9 jit_solution(992981601313333120)
XLA Ops:
  0.6 0.0 copy-start
  0.6 6.4 %dispatch.1 = bf16[64,35,8,128]{3,2,1,0:T(8,128)(2,1)} custom-call(s32[1]{0:T(128)} %bitcast.core_ref, s32[8,128]{1,0:T(8,128)} %bitcast.58, bf16[128,3584]{1,0:T(8,128)(2,1)} %tokens_ref.1), custom_call_target="tpu_custom_call" | custom-call | tf_op jit(solution)/shard_map/dispatch/pallas_call | solution.py:142
  7.1 12.2 %all-to-all-start = ((bf16[64,35,8,128]{3,2,1,0:T(8,128)(2,1)}), bf16[64,35,8,128]{3,2,1,0:T(8,128)(2,1)}, u32[]{:S(2)}, u32[]{:S(2)}) async-start(bf16[64,35,8,128]{3,2,1,0:T(8,128)(2,1)} %dispatch.1), calls=%async_computation | async-start | bytes 9175040 | tf_op jit(solution)/shard_map/all_to_all | solution.py:439
  19.3 2.3 %dynamic-slice_bitcast_fusion.2 = bf16[3584,512]{1,0:T(8,128)(2,1)S(1)} fusion(bf16[2,3584,512]{2,1,0:T(8,128)(2,1)} %in_own_ref.1, s32[]{:T(128)S(6)} %select_n.16), kind=kLoop, calls=%fused_computation.2 | loop fusion | bytes 7340036 | tf_op jit(solution)/shard_map/jit(dynamic_index_in_dim)/squeeze | solution.py:442
  21.6 1.0 collective-permute-start
  22.6 2.3 %dynamic-slice_bitcast_fusion.1 = bf16[3584,512]{1,0:T(8,128)(2,1)S(1)} fusion(bf16[2,3584,512]{2,1,0:T(8,128)(2,1)} %up_own_ref.1, s32[]{:T(128)S(6)} %select_n.16), kind=kLoop, calls=%fused_computation.1 | loop fusion | bytes 7340036 | tf_op jit(solution)/shard_map/jit(dynamic_index_in_dim)/squeeze | solution.py:442
  24.9 0.1 collective-permute-start.1
  25.0 2.3 %dynamic-slice_bitcast_fusion = bf16[512,3584]{1,0:T(8,128)(2,1)S(1)} fusion(bf16[2,512,3584]{2,1,0:T(8,128)(2,1)} %out_own_ref.1, s32[]{:T(128)S(6)} %select_n.16), kind=kLoop, calls=%fused_computation | loop fusion | bytes 7340036 | tf_op jit(solution)/shard_map/jit(dynamic_index_in_dim)/squeeze | solution.py:442
  27.2 0.8 collective-permute-start.2
  28.0 0.6 collective-permute-done.in_far_ref
  28.6 0.0 copy-start.4
  28.6 5.2 %collective-permute-done.1.up_far_ref = bf16[3584,512]{1,0:T(8,128)(2,1)S(1)} collective-permute-done((bf16[3584,512]{1,0:T(8,128)(2,1)S(1)}, bf16[3584,512]{1,0:T(8,128)(2,1)S(1)}, u32[]{:S(2)}, u32[]{:S(2)}) %collective-permute-start.1) | collective-permute-done | bytes 3670048 | tf_op jit(solution)/shard_map/ppermute | solution.py:442
  33.9 0.0 copy-done.4
  33.9 0.0 copy-start.5
  33.9 1.8 %copy-done.5 = bf16[3584,512]{1,0:T(8,128)(2,1)} copy-done((bf16[3584,512]{1,0:T(8,128)(2,1)}, bf16[3584,512]{1,0:T(8,128)(2,1)S(1)}, u32[]{:S(2)}) %copy-start.5) | copy-done | bytes 3670040
  35.7 3.6 %collective-permute-done.2.out_far_ref = bf16[512,3584]{1,0:T(8,128)(2,1)} collective-permute-done((bf16[512,3584]{1,0:T(8,128)(2,1)S(1)}, bf16[512,3584]{1,0:T(8,128)(2,1)}, u32[]{:S(2)}, u32[]{:S(2)}) %collective-permute-start.2) | collective-permute-done | bytes 3670048 | tf_op jit(solution)/shard_map/ppermute | solution.py:442
  39.3 38.5 %all-to-all-done.message_ref = bf16[64,35,8,128]{3,2,1,0:T(8,128)(2,1)} async-done(((bf16[64,35,8,128]{3,2,1,0:T(8,128)(2,1)}), bf16[64,35,8,128]{3,2,1,0:T(8,128)(2,1)}, u32[]{:S(2)}, u32[]{:S(2)}) %all-to-all-start) | async-done | bytes 4587552 | tf_op jit(solution)/shard_map/all_to_all | solution.py:439
  77.7 19.5 %experts.1 = bf16[64,35,8,128]{3,2,1,0:T(8,128)(2,1)} custom-call(s32[1]{0:T(128)} %bitcast.core_ref, bf16[64,35,8,128]{3,2,1,0:T(8,128)(2,1)} %all-to-all-done.message_ref, bf16[2,3584,512]{2,1,0:T(8,128)(2,1)} %in_own_ref.1, bf16[2,3584,512]{2,1,0:T(8,128)(2,1)} %up_own_ref.1, bf16[3584,512]{1,0:T(8,128)(2,1)} %copy-done.4, bf16[3584,512]{1,0:T(8,128)(2,1)} %copy-done.5, ...), custom_call_target="tpu_custom_call" | custom-call | flops 14092861440 | bytes 33554432 | tf_op jit(solution)/shard_map/experts/pallas_call | solution.py:272
  97.3 0.0 copy-start.2
  97.3 0.0 copy-start.3
  97.3 0.0 copy-start.1
  97.3 10.1 %all-to-all-start.1 = ((bf16[64,35,8,128]{3,2,1,0:T(8,128)(2,1)}), bf16[64,35,8,128]{3,2,1,0:T(8,128)(2,1)}, u32[]{:S(2)}, u32[]{:S(2)}) async-start(bf16[64,35,8,128]{3,2,1,0:T(8,128)(2,1)} %experts.1), calls=%async_computation.1 | async-start | bytes 9175040 | tf_op jit(solution)/shard_map/all_to_all | solution.py:447
  107.4 2.0 %gates.1.gates_ref = bf16[256,640]{1,0:T(8,128)(2,1)} custom-call(s32[1]{0:T(128)} %bitcast.core_ref, s32[8,128]{1,0:T(8,128)} %bitcast.59, f32[8,128]{1,0:T(8,128)} %bitcast.60), custom_call_target="tpu_custom_call" | custom-call | tf_op jit(solution)/shard_map/gates/pallas_call | solution.py:326
  110.0 0.0 copy-done.2
  110.1 0.0 copy-done.3
  110.1 0.2 fusion.13
  110.3 0.0 copy-done
  110.3 0.0 copy-done.1
  110.3 0.6 select_reduce_fusion
  110.9 0.6 fusion.1
  111.5 54.1 %all-to-all-done.1.back_ref = bf16[64,35,8,128]{3,2,1,0:T(8,128)(2,1)} async-done(((bf16[64,35,8,128]{3,2,1,0:T(8,128)(2,1)}), bf16[64,35,8,128]{3,2,1,0:T(8,128)(2,1)}, u32[]{:S(2)}, u32[]{:S(2)}) %all-to-all-start.1) | async-done | bytes 4587552 | tf_op jit(solution)/shard_map/all_to_all | solution.py:447
  165.6 6.2 %combine.1 = (f32[128,1792]{1,0:T(8,128)}, f32[128,1792]{1,0:T(8,128)}) custom-call(s32[1]{0:T(128)} %bitcast.core_ref, bf16[64,35,8,128]{3,2,1,0:T(8,128)(2,1)} %all-to-all-done.1.back_ref, bf16[256,640]{1,0:T(8,128)(2,1)} %gates.1.gates_ref), custom_call_target="tpu_custom_call" | custom-call | tf_op jit(solution)/shard_map/combine/pallas_call | solution.py:380
  171.8 1.7 collective-permute-start.3
  173.5 0.2 fusion.4
  173.8 0.1 collective-permute-start.4
  173.9 2.2 %collective-permute-done.4 = f32[1,128,640]{1,2,0:T(8,128)S(1)} collective-permute-done((f32[1,128,640]{1,2,0:T(8,128)S(1)}, f32[1,128,640]{1,2,0:T(8,128)S(1)}, u32[]{:S(2)}, u32[]{:S(2)}) %collective-permute-start.4) | collective-permute-done | bytes 327712 | tf_op jit(solution)/shard_map/ppermute | solution.py:413
  176.1 0.1 fusion.11
  176.1 0.8 copy.21
  176.9 0.0 collective-permute-done.3
  176.9 2.0 %add_convert_fusion = bf16[128,1792]{1,0:T(8,128)(2,1)} fusion(f32[128,1792]{1,0:T(8,128)} %get-tuple-element.4, f32[128,1792]{1,0:T(8,128)S(1)} %collective-permute-done.3), kind=kLoop, calls=%fused_computation.8 | loop fusion | flops 458752 | bytes 2293760 | tf_op jit(solution)/shard_map/convert_element_type | solution.py:449
  (5 shorter events, 0.0 us)
Async XLA Ops:
  0.6 109.7 %copy-start = (bf16[1,1024,512]{2,1,0:T(8,128)(2,1)S(1)}, bf16[1,1024,512]{2,1,0:T(8,128)(2,1)}, u32[]{:S(2)}) copy-start(bf16[1,1024,512]{2,1,0:T(8,128)(2,1)} %param.19) | copy-start | bytes 3145732
  7.1 70.7 %all-to-all-start = ((bf16[64,35,8,128]{3,2,1,0:T(8,128)(2,1)}), bf16[64,35,8,128]{3,2,1,0:T(8,128)(2,1)}, u32[]{:S(2)}, u32[]{:S(2)}) async-start(bf16[64,35,8,128]{3,2,1,0:T(8,128)(2,1)} %dispatch.1), calls=%async_computation | async-start | bytes 9175040 | tf_op jit(solution)/shard_map/all_to_all | solution.py:439
  21.6 7.1 %collective-permute-start = (bf16[3584,512]{1,0:T(8,128)(2,1)S(1)}, bf16[3584,512]{1,0:T(8,128)(2,1)S(1)}, u32[]{:S(2)}, u32[]{:S(2)}) collective-permute-start(bf16[3584,512]{1,0:T(8,128)(2,1)S(1)} %dynamic-slice_bitcast_fusion.2), channel_id=1, source_target_pairs={{0,1},{1,0},{2,3},{3,2},{4,5},{5,4},{6,7},{7,6},{8,9},{9,8},{10,11... | collective-permute-start | bytes 11010056 | tf_op jit(solution)/shard_map/ppermute | solution.py:442
  24.9 9.0 %collective-permute-start.1 = (bf16[3584,512]{1,0:T(8,128)(2,1)S(1)}, bf16[3584,512]{1,0:T(8,128)(2,1)S(1)}, u32[]{:S(2)}, u32[]{:S(2)}) collective-permute-start(bf16[3584,512]{1,0:T(8,128)(2,1)S(1)} %dynamic-slice_bitcast_fusion.1), channel_id=1, source_target_pairs={{0,1},{1,0},{2,3},{3,2},{4,5},{5,4},{6,7},{7,6},{8,9},{9,8},{10,11... | collective-permute-start | bytes 11010056 | tf_op jit(solution)/shard_map/ppermute | solution.py:442
  27.2 12.0 %collective-permute-start.2 = (bf16[512,3584]{1,0:T(8,128)(2,1)S(1)}, bf16[512,3584]{1,0:T(8,128)(2,1)}, u32[]{:S(2)}, u32[]{:S(2)}) collective-permute-start(bf16[512,3584]{1,0:T(8,128)(2,1)S(1)} %dynamic-slice_bitcast_fusion), channel_id=1, source_target_pairs={{0,1},{1,0},{2,3},{3,2},{4,5},{5,4},{6,7},{7,6},{8,9},{9,8},{10,11... | collective-permute-start | bytes 11010056 | tf_op jit(solution)/shard_map/ppermute | solution.py:442
  28.6 5.3 %copy-start.4 = (bf16[3584,512]{1,0:T(8,128)(2,1)}, bf16[3584,512]{1,0:T(8,128)(2,1)S(1)}, u32[]{:S(2)}) copy-start(bf16[3584,512]{1,0:T(8,128)(2,1)S(1)} %collective-permute-done.in_far_ref) | copy-start | bytes 11010052
  33.9 1.8 %copy-start.5 = (bf16[3584,512]{1,0:T(8,128)(2,1)}, bf16[3584,512]{1,0:T(8,128)(2,1)S(1)}, u32[]{:S(2)}) copy-start(bf16[3584,512]{1,0:T(8,128)(2,1)S(1)} %collective-permute-done.1.up_far_ref) | copy-start | bytes 11010052
  97.3 12.8 %copy-start.2 = (bf16[1,64,1024]{2,1,0:T(8,128)(2,1)S(1)}, bf16[1,64,1024]{2,1,0:T(8,128)(2,1)}, u32[]{:S(2)}) copy-start(bf16[1,64,1024]{2,1,0:T(8,128)(2,1)} %param.20) | copy-start | bytes 393220
  97.3 12.8 %copy-start.3 = (bf16[1,128,64]{1,2,0:T(8,128)(2,1)S(1)}, bf16[1,128,64]{1,2,0:T(8,128)(2,1)}, u32[]{:S(2)}) copy-start(bf16[1,128,64]{1,2,0:T(8,128)(2,1)} %param.18) | copy-start | bytes 49156
  97.3 13.0 %copy-start.1 = (bf16[1,128,512]{2,1,0:T(8,128)(2,1)S(1)}, bf16[1,128,512]{2,1,0:T(8,128)(2,1)}, u32[]{:S(2)}) copy-start(bf16[1,128,512]{2,1,0:T(8,128)(2,1)} %param.17) | copy-start | bytes 393220
  97.3 68.3 %all-to-all-start.1 = ((bf16[64,35,8,128]{3,2,1,0:T(8,128)(2,1)}), bf16[64,35,8,128]{3,2,1,0:T(8,128)(2,1)}, u32[]{:S(2)}, u32[]{:S(2)}) async-start(bf16[64,35,8,128]{3,2,1,0:T(8,128)(2,1)} %experts.1), calls=%async_computation.1 | async-start | bytes 9175040 | tf_op jit(solution)/shard_map/all_to_all | solution.py:447
  171.8 5.1 %collective-permute-start.3 = (f32[128,1792]{1,0:T(8,128)}, f32[128,1792]{1,0:T(8,128)S(1)}, u32[]{:S(2)}, u32[]{:S(2)}) collective-permute-start(f32[128,1792]{1,0:T(8,128)} %get-tuple-element.5), channel_id=1, source_target_pairs={{0,1},{1,0},{2,3},{3,2},{4,5},{5,4},{6,7},{7,6},{8,9},{9,8},{10,11... | collective-permute-start | bytes 2752520 | tf_op jit(solution)/shard_map/ppermute | solution.py:449
  173.8 2.3 %collective-permute-start.4 = (f32[1,128,640]{1,2,0:T(8,128)S(1)}, f32[1,128,640]{1,2,0:T(8,128)S(1)}, u32[]{:S(2)}, u32[]{:S(2)}) collective-permute-start(f32[1,128,640]{1,2,0:T(8,128)S(1)} %pad_maximum_fusion), channel_id=1, source_target_pairs={{0,1},{1,0},{2,3},{3,2},{4,5},{5,4},{6,7},{7,6},{8,9},{9,8},{10,11... | collective-permute-start | bytes 983048 | tf_op jit(solution)/shard_map/ppermute | solution.py:413

commit v3 on v2

--- a/solution.py
+++ b/solution.py
@@ -40,6 +40,24 @@
     return ref.at[:, pl.ds(group * TILES, TILES)]
 
 
+def pack_copies(packed, messages, sems, groups):
+    copies = []
+    for g in range(groups):
+        for i, part in enumerate((pl.ds(g * TILES, TILES - 1), pl.ds(g * TILES + TILES - 1, 1))):
+            copies.append(pltpu.make_async_copy(packed.at[:, part], messages.at[:, part], sems.at[2 * g + i]))
+    return copies
+
+
+def start(copies):
+    for each in copies:
+        each.start()
+
+
+def wait(copies):
+    for each in copies:
+        each.wait()
+
+
 def features_of(group):
     return slice(group * GROUP, (group + 1) * GROUP)
 
@@ -62,31 +80,54 @@
     ref[...] = one_hot(iota((size, size), 1), unit_of(iota((size, size), 0), dp_count // 2))
 
 
-def pack(value, place, ref, group):
+def pack(value, ref, group):
     dp_count = ref.shape[0]
     main, half = dp_count * MAIN, dp_count // 2
     for f in range(4):
-        ref[:, group * TILES + f] = value[:main, block_of(f)].astype(BF16).reshape(dp_count, MAIN, BLOCK)
+        part = value[:main, block_of(f)].astype(BF16)
+        ref[:, group * TILES + f] = part.reshape(dp_count, MAIN, BLOCK)
     rest = value[main:].astype(BF16)
     sides = [rest[: 2 * half], rest[2 * half :]]
     sides = [jnp.concatenate([side[:, block_of(f)] for f in range(4)], axis=0) for side in sides]
-    rest = dot(place, jnp.concatenate(sides, axis=1))
+    return jnp.concatenate(sides, axis=1)
+
+
+def place_rest(rest, place, ref, group):
+    half = ref.shape[0] // 2
+    rest = dot(place, rest)
     for h in range(2):
-        part = rest[:, block_of(h)].astype(BF16).reshape(half, MAIN, BLOCK)
-        ref[h * half : (h + 1) * half, group * TILES + 4] = part
-
-
-def unpack(ref, pick, group):
+        part = rest[:, block_of(h)].astype(BF16)
+        ref[h * half : (h + 1) * half, group * TILES + 4] = part.reshape(half, MAIN, BLOCK)
+
+
+def pack_all(groups, value_of, place, packed, copies):
+    rest = None
+    for g in range(groups):
+        value = value_of(g)
+        if rest is not None:
+            place_rest(rest, place, packed, g - 1)
+        rest = pack(value, packed, g)
+        start([copies[2 * g]] + ([copies[2 * g - 1]] if g else []))
+    place_rest(rest, place, packed, groups - 1)
+    start(copies[-1:])
+    wait(copies)
+
+
+def pick_rest(ref, pick, group):
     dp_count = ref.shape[0]
     main, half = dp_count * MAIN, dp_count // 2
-    rows = [ref[:, group * TILES + f].reshape(main, BLOCK) for f in range(4)]
     rest = ref[:, group * TILES + 4].reshape(main, BLOCK)
     rest = dot(pick, jnp.concatenate([rest[: main // 2], rest[main // 2 :]], axis=1)).astype(BF16)
-    rest = [
+    sides = [
         jnp.concatenate([rest[2 * half * f : 2 * half * (f + 1), block_of(h)] for f in range(4)], axis=1)
         for h in range(2)
     ]
-    return jnp.concatenate([jnp.concatenate(rows, axis=1)] + rest, axis=0)
+    return jnp.concatenate(sides, axis=0)
+
+
+def main_rows(ref, group):
+    main = ref.shape[0] * MAIN
+    return jnp.concatenate([ref[:, group * TILES + f].reshape(main, BLOCK) for f in range(4)], axis=1)
 
 
 def row_of(index, dp_count):
@@ -114,11 +155,7 @@
         pltpu.make_async_copy(tokens_ref.at[:, features_of(g)], rows.at[:, features_of(g)], in_sem.at[g])
         for g in range(groups)
     ]
-    stores = [
-        pltpu.make_async_copy(tiles_of(packed, g), tiles_of(out_ref, g), out_sem.at[g]) for g in range(groups)
-    ]
-    for load in loads:
-        load.start()
+    start(loads)
     fill_place(place, dp_count)
     code = rank_code(routes_ref[...]).astype(BF16)
     tokens = code.shape[1]
@@ -127,12 +164,9 @@
     spread = dot(one_hot(iota((count, 128), 1), 2 * owner + core_ref[0]), code)
     _, turn = row_of(iota((count, tokens), 0), dp_count)
     chosen[...] = one_hot(spread, turn.astype(F32))
-    for g in range(groups):
-        loads[g].wait()
-        pack(dot(chosen[...], rows[:, features_of(g)]), place[...], packed, g)
-        stores[g].start()
-    for store in stores:
-        store.wait()
+    wait(loads)
+    stores = pack_copies(packed, out_ref, out_sem, groups)
+    pack_all(groups, lambda g: dot(chosen[...], rows[:, features_of(g)]), place[...], packed, stores)
 
 
 def dispatch(core, routes, tokens, dp_count):
@@ -150,7 +184,7 @@
             pltpu.VMEM((4 * dp_count, 4 * dp_count), BF16),
             pltpu.VMEM(shape, BF16),
             pltpu.SemaphoreType.DMA((groups,)),
-            pltpu.SemaphoreType.DMA((groups,)),
+            pltpu.SemaphoreType.DMA((2 * groups,)),
         ],
         compiler_params=PARAMS,
         name="dispatch",
@@ -200,12 +234,20 @@
     def stage_copies(i):
         first, last = stages[i]
         part = pl.ds(first * GROUP, (last - first) * GROUP)
-        parts = pl.ds(first * TILES, (last - first) * TILES)
         return [
-            copy(message_ref.at[:, parts], message.at[:, parts], message_sem.at[i]),
             copy(in_own_ref.at[core, part], in_own.at[part], weight_sem.at[2 * i]),
             copy(up_own_ref.at[core, part], up_own.at[part], weight_sem.at[2 * i + 1]),
         ]
+
+    def message_copy(i):
+        first, last = stages[i]
+        part = pl.ds(first * TILES, (last - first) * TILES)
+        return copy(message_ref.at[:, part], message.at[:, part], message_sem.at[i])
+
+    def unpack(i):
+        for g in range(*stages[i]):
+            rows[: dp_count * MAIN, features_of(g)] = main_rows(message, g)
+            rows[dp_count * MAIN :, features_of(g)] = pick_rest(message, pick[...], g)
 
     far_copies = [
         copy(in_far_ref, in_far, far_sem.at[0]),
@@ -213,28 +255,22 @@
         copy(out_own_ref.at[core], out_both.at[pl.ds(0, width)], far_sem.at[2]),
         copy(out_far_ref, out_both.at[pl.ds(width, width)], far_sem.at[3]),
     ]
-    staged = [stage_copies(i) for i in range(len(stages))]
-    back_copies = [copy(tiles_of(packed, g), tiles_of(back_ref, g), back_sem.at[g]) for g in range(groups)]
-    for group in staged[:2]:
-        for each in group:
-            each.start()
+    staged = [stage_copies(i) for i in range(len(stages))] + [far_copies[:2], far_copies[2:]]
+    messages = [message_copy(i) for i in range(len(stages))]
+    back_copies = pack_copies(packed, back_ref, back_sem, groups)
+    start([messages[0]] + staged[0] + [messages[1]] + staged[1] + [messages[2]] + staged[2])
     fill_pick(pick, dp_count)
     fill_place(place, dp_count)
+    wait(messages[:1])
+    unpack(0)
 
     for i, (first, last) in enumerate(stages):
-        for each in staged[i]:
-            each.wait()
-        if i + 2 < len(stages):
-            for each in staged[i + 2]:
-                each.start()
-        elif i + 2 == len(stages):
-            for each in far_copies[:2]:
-                each.start()
-        else:
-            for each in far_copies[2:]:
-                each.start()
-        for g in range(first, last):
-            rows[:, features_of(g)] = unpack(message, pick[...], g)
+        wait(staged[i])
+        if i + 3 < len(staged):
+            start(messages[i + 3 : i + 4] + staged[i + 3])
+        if 0 < i < len(stages) - 1:
+            wait([messages[i + 1]])
+            unpack(i + 1)
         part = slice(first * GROUP, last * GROUP)
         gate = dot(rows[:, part], in_own[part])
         up = dot(rows[:, part], up_own[part])
@@ -246,18 +282,15 @@
             up_sum[...] = up
         else:
             hidden[:, :width] = (gate / (1.0 + jnp.exp(-gate)) * up).astype(BF16)
-    for each in far_copies[:2]:
-        each.wait()
+        if i == 0:
+            wait([messages[1]])
+            unpack(1)
+    wait(far_copies[:2])
     gate = dot(rows[...], in_far[...])
     up = dot(rows[...], up_far[...])
     hidden[:, width:] = (gate / (1.0 + jnp.exp(-gate)) * up).astype(BF16)
-    for each in far_copies[2:]:
-        each.wait()
-    for g in range(groups):
-        pack(dot(hidden[...], out_both[:, features_of(g)]), place[...], packed, g)
-        back_copies[g].start()
-    for each in back_copies:
-        each.wait()
+    wait(far_copies[2:])
+    pack_all(groups, lambda g: dot(hidden[...], out_both[:, features_of(g)]), place[...], packed, back_copies)
 
 
 def experts(core, message, w_in, w_up, w_out, in_far, up_far, out_far):
@@ -291,7 +324,7 @@
             pltpu.SemaphoreType.DMA((stages,)),
             pltpu.SemaphoreType.DMA((2 * stages,)),
             pltpu.SemaphoreType.DMA((4,)),
-            pltpu.SemaphoreType.DMA((groups,)),
+            pltpu.SemaphoreType.DMA((2 * groups,)),
         ],
         compiler_params=PARAMS,
         cost_estimate=pl.CostEstimate(
@@ -332,7 +365,7 @@
     )(core, routes, gates)
 
 
-def combine_kernel(core_ref, back_ref, gates_ref, keep_ref, send_ref, message, total, pick, sem, out_sem):
+def combine_kernel(core_ref, back_ref, gates_ref, after_ref, keep_ref, send_ref, message, gates, total, pick, sem):
     core = core_ref[0]
     dp_count = message.shape[0]
     groups = message.shape[1] // TILES
@@ -340,58 +373,52 @@
     loads = [
         pltpu.make_async_copy(tiles_of(back_ref, g), tiles_of(message, g), sem.at[g]) for g in range(groups)
     ]
-
-    def store(side):
-        part = total.at[:, pl.ds(side * half, half)]
-        keep = pltpu.make_async_copy(part, keep_ref, out_sem.at[0])
-        send = pltpu.make_async_copy(part, send_ref, out_sem.at[1])
-        return keep, send
-
-    for load in loads:
-        load.start()
+    gates_load = [pltpu.make_async_copy(gates_ref, gates, sem.at[groups])]
+    start(gates_load + loads)
     fill_pick(pick, dp_count)
+    wait(gates_load + loads[:1])
+    rest = pick_rest(message, pick[...], 0)
     side = 0
     for g in range(groups):
-        loads[g].wait()
-        value = dot(gates_ref[...], unpack(message, pick[...], g))
+        wait(loads[g + 1 : g + 2])
+        value = dot(gates[...], jnp.concatenate([main_rows(message, g), rest], axis=0))
+        if g + 1 < groups:
+            rest = pick_rest(message, pick[...], g + 1)
         total[:, features_of(g)] = value[:tokens] + value[tokens:]
         if (g + 1) * GROUP >= (side + 1) * half:
-            keep, send = store(side)
+            part = slice(side * half, (side + 1) * half)
 
             @pl.when(core == side)
             def _():
-                keep.start()
+                keep_ref[...] = total[:, part]
 
             @pl.when(core != side)
             def _():
-                send.start()
+                send_ref[...] = total[:, part]
 
             side += 1
-    keep, send = store(0)
-    keep.wait()
-    send.wait()
-
-
-def combine(core, back, gates):
+
+
+def combine(core, back, gates, after):
     dp_count, tiles = back.shape[:2]
     groups = tiles // TILES
     tokens = gates.shape[0] // 2
     out = jax.ShapeDtypeStruct((tokens, groups * GROUP // 2), F32)
     return pl.pallas_call(
         combine_kernel,
-        in_specs=[SMEM, HBM, VMEM],
-        out_specs=(HBM, HBM),
+        in_specs=[SMEM, HBM, HBM, HBM],
+        out_specs=(VMEM, VMEM),
         out_shape=(out, out),
         scratch_shapes=[
             pltpu.VMEM(back.shape, BF16),
+            pltpu.VMEM(gates.shape, BF16),
             pltpu.VMEM((tokens, groups * GROUP), F32),
             pltpu.VMEM((4 * dp_count, 4 * dp_count), BF16),
-            pltpu.SemaphoreType.DMA((groups,)),
-            pltpu.SemaphoreType.DMA((2,)),
+            pltpu.SemaphoreType.DMA((groups + 1,)),
         ],
-        compiler_params=PARAMS,
+        compiler_params=pltpu.CompilerParams(vmem_limit_bytes=16 * 1024 * 1024),
         name="combine",
-    )(core, back, gates)
+    )(core, back, gates, after)
 
 
 def attention(query_latent, query_rope, cache_latent, cache_rope, lengths):
@@ -445,9 +472,9 @@
     gates = spread_gates(core, routes, route_gates.T, dp_count)
     back = experts(core, message, w_in, w_up, w_out, in_far, up_far, out_far)
     returned = lax.all_to_all(back, "dp", split_axis=0, concat_axis=0, tiled=True)
-    keep, send = combine(core, returned, gates)
+    attn_out = attention(query_latent, query_rope, cache_latent, cache_rope, lengths)
+    keep, send = combine(core, returned, gates, attn_out)
     moe_out = (keep + lax.ppermute(send, "tp", SWAP)).astype(BF16)
-    attn_out = attention(query_latent, query_rope, cache_latent, cache_rope, lengths)
     return (moe_out, attn_out)
 
 

time: 179 us -> 175 us (0.978)
  Pallas kernels: 34 us -> 30.8 us
  waiting for transfers between devices: 104 us -> 102 us
    ppermute x1, waiting for transfers between devices: 2.19 us -> 0.01 us  [attention(): far = lax.ppermute(both, 'tp', SWAP)]
    ppermute x1, waiting for transfers between devices: 0.01 us -> 2.1 us  [body(): moe_out = (keep + lax.ppermute(send, 'tp', SWAP)).astype(BF16)]
    all_to_all x1, waiting for transfers between devices: 54.1 us -> 52.3 us  [body(): lax.all_to_all(back, 'dp', split_axis=0, concat_axis=0, tiled=True)]
where the time goes in v3:
time: 175 us; the launch traced here: 174 us
  waiting for transfers between devices  102 us (58%)
  Pallas kernels  30.8 us (18%)
  starting transfers between devices  26.7 us (15%)
  local copies, waits for them, and re-layouts  9.99 us (6%)
    all_to_all x1, waiting for transfers between devices, body(): lax.all_to_all(back, 'dp', split_axis=0, concat_axis=0, tiled=True)  52.3 us
    all_to_all x1, waiting for transfers between devices, body(): lax.all_to_all(outbound, 'dp', split_axis=0, concat_axis=0, tiled=True)  38.5 us
    pallas_call x1, Pallas kernels, experts(): pl.pallas_call(expert_kernel, in_specs=[SMEM] + [HBM] * 7, out_specs=HBM,...  19.5 us
    all_to_all x1, starting transfers between devices, body(): lax.all_to_all(outbound, 'dp', split_axis=0, concat_axis=0, tiled=True)  12.2 us
    all_to_all x1, starting transfers between devices, body(): lax.all_to_all(back, 'dp', split_axis=0, concat_axis=0, tiled=True)  10.2 us
    ppermute x3, waiting for transfers between devices, swap(): lax.ppermute(lax.dynamic_index_in_dim(weight, 1 - index, 0, False), 'tp',...  9.48 us
    squeeze x3, local copies, waits for them, and re-layouts, swap(): lax.dynamic_index_in_dim(weight, 1 - index, 0, False)  6.83 us
    pallas_call x1, Pallas kernels, dispatch(): pl.pallas_call(dispatch_kernel, in_specs=[SMEM, VMEM, HBM], out_specs=HBM...  4.95 us
  transfers between devices with their start and end apart: 7, of which 6 were waited for; matrix products, arithmetic and copies ran while one was open for 5% of the time, Pallas kernels for 1%

profile of v3, /device:TPU:1, one launch (start us, length us, event | category | flops | bytes accessed | tf_op | source)
XLA Modules:
  0.0 174.1 jit_solution(3726555100889417696)
XLA Ops:
  0.6 0.0 copy-start
  0.6 5.0 %dispatch.1 = bf16[64,35,8,128]{3,2,1,0:T(8,128)(2,1)} custom-call(s32[1]{0:T(128)} %bitcast.core_ref, s32[8,128]{1,0:T(8,128)} %bitcast.37, bf16[128,3584]{1,0:T(8,128)(2,1)} %tokens_ref.1), custom_call_target="tpu_custom_call" | custom-call | tf_op jit(solution)/shard_map/dispatch/pallas_call | solution.py:176
  5.6 12.2 %all-to-all-start = ((bf16[64,35,8,128]{3,2,1,0:T(8,128)(2,1)}), bf16[64,35,8,128]{3,2,1,0:T(8,128)(2,1)}, u32[]{:S(2)}, u32[]{:S(2)}) async-start(bf16[64,35,8,128]{3,2,1,0:T(8,128)(2,1)} %dispatch.1), calls=%async_computation | async-start | bytes 9175040 | tf_op jit(solution)/shard_map/all_to_all | solution.py:466
  17.8 2.3 %dynamic-slice_bitcast_fusion.2 = bf16[3584,512]{1,0:T(8,128)(2,1)S(1)} fusion(bf16[2,3584,512]{2,1,0:T(8,128)(2,1)} %in_own_ref.1, s32[]{:T(128)S(6)} %select_n.16), kind=kLoop, calls=%fused_computation.2 | loop fusion | bytes 7340036 | tf_op jit(solution)/shard_map/jit(dynamic_index_in_dim)/squeeze | solution.py:469
  20.1 1.0 collective-permute-start
  21.1 2.3 %dynamic-slice_bitcast_fusion.1 = bf16[3584,512]{1,0:T(8,128)(2,1)S(1)} fusion(bf16[2,3584,512]{2,1,0:T(8,128)(2,1)} %up_own_ref.1, s32[]{:T(128)S(6)} %select_n.16), kind=kLoop, calls=%fused_computation.1 | loop fusion | bytes 7340036 | tf_op jit(solution)/shard_map/jit(dynamic_index_in_dim)/squeeze | solution.py:469
  23.4 0.1 collective-permute-start.1
  23.5 2.3 %dynamic-slice_bitcast_fusion = bf16[512,3584]{1,0:T(8,128)(2,1)S(1)} fusion(bf16[2,512,3584]{2,1,0:T(8,128)(2,1)} %out_own_ref.1, s32[]{:T(128)S(6)} %select_n.16), kind=kLoop, calls=%fused_computation | loop fusion | bytes 7340036 | tf_op jit(solution)/shard_map/jit(dynamic_index_in_dim)/squeeze | solution.py:469
  25.8 0.8 collective-permute-start.2
  26.5 0.6 collective-permute-done.in_far_ref
  27.2 0.0 copy-start.6
  27.2 5.2 %collective-permute-done.1.up_far_ref = bf16[3584,512]{1,0:T(8,128)(2,1)S(1)} collective-permute-done((bf16[3584,512]{1,0:T(8,128)(2,1)S(1)}, bf16[3584,512]{1,0:T(8,128)(2,1)S(1)}, u32[]{:S(2)}, u32[]{:S(2)}) %collective-permute-start.1) | collective-permute-done | bytes 3670048 | tf_op jit(solution)/shard_map/ppermute | solution.py:469
  32.4 0.0 copy-done.6
  32.4 0.0 copy-start.7
  32.4 1.8 %copy-done.7 = bf16[3584,512]{1,0:T(8,128)(2,1)} copy-done((bf16[3584,512]{1,0:T(8,128)(2,1)}, bf16[3584,512]{1,0:T(8,128)(2,1)S(1)}, u32[]{:S(2)}) %copy-start.7) | copy-done | bytes 3670040
  34.2 3.6 %collective-permute-done.2.out_far_ref = bf16[512,3584]{1,0:T(8,128)(2,1)} collective-permute-done((bf16[512,3584]{1,0:T(8,128)(2,1)S(1)}, bf16[512,3584]{1,0:T(8,128)(2,1)}, u32[]{:S(2)}, u32[]{:S(2)}) %collective-permute-start.2) | collective-permute-done | bytes 3670048 | tf_op jit(solution)/shard_map/ppermute | solution.py:469
  37.8 38.5 %all-to-all-done.message_ref = bf16[64,35,8,128]{3,2,1,0:T(8,128)(2,1)} async-done(((bf16[64,35,8,128]{3,2,1,0:T(8,128)(2,1)}), bf16[64,35,8,128]{3,2,1,0:T(8,128)(2,1)}, u32[]{:S(2)}, u32[]{:S(2)}) %all-to-all-start) | async-done | bytes 4587552 | tf_op jit(solution)/shard_map/all_to_all | solution.py:466
  76.3 19.5 %experts.1 = bf16[64,35,8,128]{3,2,1,0:T(8,128)(2,1)} custom-call(s32[1]{0:T(128)} %bitcast.core_ref, bf16[64,35,8,128]{3,2,1,0:T(8,128)(2,1)} %all-to-all-done.message_ref, bf16[2,3584,512]{2,1,0:T(8,128)(2,1)} %in_own_ref.1, bf16[2,3584,512]{2,1,0:T(8,128)(2,1)} %up_own_ref.1, bf16[3584,512]{1,0:T(8,128)(2,1)} %copy-done.6, bf16[3584,512]{1,0:T(8,128)(2,1)} %copy-done.7, ...), custom_call_target="tpu_custom_call" | custom-call | flops 14092861440 | bytes 33554432 | tf_op jit(solution)/shard_map/experts/pallas_call | solution.py:305
  95.8 0.0 copy-start.4
  95.8 0.0 copy-start.5
  95.9 0.0 copy-start.3
  95.9 10.2 %all-to-all-start.1 = ((bf16[64,35,8,128]{3,2,1,0:T(8,128)(2,1)}), bf16[64,35,8,128]{3,2,1,0:T(8,128)(2,1)}, u32[]{:S(2)}, u32[]{:S(2)}) async-start(bf16[64,35,8,128]{3,2,1,0:T(8,128)(2,1)} %experts.1), calls=%async_computation.1 | async-start | bytes 9175040 | tf_op jit(solution)/shard_map/all_to_all | solution.py:474
  106.8 0.0 copy-done.4
  106.8 0.0 copy-done.5
  106.8 0.2 fusion.13
  107.0 0.0 copy-done
  107.0 0.0 copy-done.3
  107.1 0.6 select_reduce_fusion
  107.6 0.2 fusion.4
  107.9 0.4 fusion.1
  108.2 0.1 broadcast_in_dim.41
  108.3 0.1 broadcast_in_dim.40
  108.4 0.1 pad_maximum_fusion
  108.5 0.9 collective-permute-start.3
  109.4 1.9 %gates.1.gates_ref = bf16[256,640]{1,0:T(8,128)(2,1)} custom-call(s32[1]{0:T(128)} %bitcast.core_ref, s32[8,128]{1,0:T(8,128)} %bitcast.38, f32[8,128]{1,0:T(8,128)} %bitcast.41), custom_call_target="tpu_custom_call" | custom-call | tf_op jit(solution)/shard_map/gates/pallas_call | solution.py:359
  111.3 0.1 copy.20
  111.4 0.1 copy.21
  111.6 0.0 collective-permute-done.3
  111.6 0.2 fusion.21
  111.8 0.1 fusion.11.after_ref
  111.9 0.0 copy-start.2
  111.9 52.3 %all-to-all-done.1.back_ref = bf16[64,35,8,128]{3,2,1,0:T(8,128)(2,1)} async-done(((bf16[64,35,8,128]{3,2,1,0:T(8,128)(2,1)}), bf16[64,35,8,128]{3,2,1,0:T(8,128)(2,1)}, u32[]{:S(2)}, u32[]{:S(2)}) %all-to-all-start.1) | async-done | bytes 4587552 | tf_op jit(solution)/shard_map/all_to_all | solution.py:474
  164.3 1.0 copy-done.1
  165.2 4.4 %combine.1 = (f32[128,1792]{1,0:T(8,128)S(1)}, f32[128,1792]{1,0:T(8,128)S(1)}) custom-call(s32[1]{0:T(128)} %bitcast.core_ref, bf16[64,35,8,128]{3,2,1,0:T(8,128)(2,1)} %all-to-all-done.1.back_ref, bf16[256,640]{1,0:T(8,128)(2,1)S(1)} %copy-done.1, bf16[1,128,512]{2,1,0:T(8,128)(2,1)S(1)} %fusion.11.after_ref), custom_call_target="tpu_custom_call" | custom-call | tf_op jit(solution)/shard_map/combine/pallas_call | solution.py:407
  169.6 1.5 collective-permute-start.4
  171.1 2.1 %collective-permute-done.4 = f32[128,1792]{1,0:T(8,128)S(1)} collective-permute-done((f32[128,1792]{1,0:T(8,128)S(1)}, f32[128,1792]{1,0:T(8,128)S(1)}, u32[]{:S(2)}, u32[]{:S(2)}) %collective-permute-start.4) | collective-permute-done | bytes 917536 | tf_op jit(solution)/shard_map/ppermute | solution.py:477
  173.2 0.9 add_convert_fusion
  174.1 0.0 copy-done.2
  (2 shorter events, 0.0 us)
Async XLA Ops:
  0.6 106.4 %copy-start = (bf16[1,1024,512]{2,1,0:T(8,128)(2,1)S(1)}, bf16[1,1024,512]{2,1,0:T(8,128)(2,1)}, u32[]{:S(2)}) copy-start(bf16[1,1024,512]{2,1,0:T(8,128)(2,1)} %param.19) | copy-start | bytes 3145732
  5.6 70.7 %all-to-all-start = ((bf16[64,35,8,128]{3,2,1,0:T(8,128)(2,1)}), bf16[64,35,8,128]{3,2,1,0:T(8,128)(2,1)}, u32[]{:S(2)}, u32[]{:S(2)}) async-start(bf16[64,35,8,128]{3,2,1,0:T(8,128)(2,1)} %dispatch.1), calls=%async_computation | async-start | bytes 9175040 | tf_op jit(solution)/shard_map/all_to_all | solution.py:466
  20.1 7.1 %collective-permute-start = (bf16[3584,512]{1,0:T(8,128)(2,1)S(1)}, bf16[3584,512]{1,0:T(8,128)(2,1)S(1)}, u32[]{:S(2)}, u32[]{:S(2)}) collective-permute-start(bf16[3584,512]{1,0:T(8,128)(2,1)S(1)} %dynamic-slice_bitcast_fusion.2), channel_id=1, source_target_pairs={{0,1},{1,0},{2,3},{3,2},{4,5},{5,4},{6,7},{7,6},{8,9},{9,8},{10,11... | collective-permute-start | bytes 11010056 | tf_op jit(solution)/shard_map/ppermute | solution.py:469
  23.4 9.0 %collective-permute-start.1 = (bf16[3584,512]{1,0:T(8,128)(2,1)S(1)}, bf16[3584,512]{1,0:T(8,128)(2,1)S(1)}, u32[]{:S(2)}, u32[]{:S(2)}) collective-permute-start(bf16[3584,512]{1,0:T(8,128)(2,1)S(1)} %dynamic-slice_bitcast_fusion.1), channel_id=1, source_target_pairs={{0,1},{1,0},{2,3},{3,2},{4,5},{5,4},{6,7},{7,6},{8,9},{9,8},{10,11... | collective-permute-start | bytes 11010056 | tf_op jit(solution)/shard_map/ppermute | solution.py:469
  25.8 12.0 %collective-permute-start.2 = (bf16[512,3584]{1,0:T(8,128)(2,1)S(1)}, bf16[512,3584]{1,0:T(8,128)(2,1)}, u32[]{:S(2)}, u32[]{:S(2)}) collective-permute-start(bf16[512,3584]{1,0:T(8,128)(2,1)S(1)} %dynamic-slice_bitcast_fusion), channel_id=1, source_target_pairs={{0,1},{1,0},{2,3},{3,2},{4,5},{5,4},{6,7},{7,6},{8,9},{9,8},{10,11... | collective-permute-start | bytes 11010056 | tf_op jit(solution)/shard_map/ppermute | solution.py:469
  27.2 5.3 %copy-start.6 = (bf16[3584,512]{1,0:T(8,128)(2,1)}, bf16[3584,512]{1,0:T(8,128)(2,1)S(1)}, u32[]{:S(2)}) copy-start(bf16[3584,512]{1,0:T(8,128)(2,1)S(1)} %collective-permute-done.in_far_ref) | copy-start | bytes 11010052
  32.4 1.8 %copy-start.7 = (bf16[3584,512]{1,0:T(8,128)(2,1)}, bf16[3584,512]{1,0:T(8,128)(2,1)S(1)}, u32[]{:S(2)}) copy-start(bf16[3584,512]{1,0:T(8,128)(2,1)S(1)} %collective-permute-done.1.up_far_ref) | copy-start | bytes 11010052
  95.8 10.9 %copy-start.4 = (bf16[1,64,1024]{2,1,0:T(8,128)(2,1)S(1)}, bf16[1,64,1024]{2,1,0:T(8,128)(2,1)}, u32[]{:S(2)}) copy-start(bf16[1,64,1024]{2,1,0:T(8,128)(2,1)} %param.20) | copy-start | bytes 393220
  95.8 10.9 %copy-start.5 = (bf16[1,128,64]{1,2,0:T(8,128)(2,1)S(1)}, bf16[1,128,64]{1,2,0:T(8,128)(2,1)}, u32[]{:S(2)}) copy-start(bf16[1,128,64]{1,2,0:T(8,128)(2,1)} %param.18) | copy-start | bytes 49156
  95.9 11.2 %copy-start.3 = (bf16[1,128,512]{2,1,0:T(8,128)(2,1)S(1)}, bf16[1,128,512]{2,1,0:T(8,128)(2,1)}, u32[]{:S(2)}) copy-start(bf16[1,128,512]{2,1,0:T(8,128)(2,1)} %param.17) | copy-start | bytes 393220
  95.9 68.4 %all-to-all-start.1 = ((bf16[64,35,8,128]{3,2,1,0:T(8,128)(2,1)}), bf16[64,35,8,128]{3,2,1,0:T(8,128)(2,1)}, u32[]{:S(2)}, u32[]{:S(2)}) async-start(bf16[64,35,8,128]{3,2,1,0:T(8,128)(2,1)} %experts.1), calls=%async_computation.1 | async-start | bytes 9175040 | tf_op jit(solution)/shard_map/all_to_all | solution.py:474
  108.5 3.0 %collective-permute-start.3 = (f32[1,128,640]{2,1,0:T(8,128)S(1)}, f32[1,128,640]{2,1,0:T(8,128)S(1)}, u32[]{:S(2)}, u32[]{:S(2)}) collective-permute-start(f32[1,128,640]{2,1,0:T(8,128)S(1)} %pad_maximum_fusion), channel_id=1, source_target_pairs={{0,1},{1,0},{2,3},{3,2},{4,5},{5,4},{6,7},{7,6},{8,9},{9,8},{10,11... | collective-permute-start | bytes 983048 | tf_op jit(solution)/shard_map/ppermute | solution.py:440
  111.9 62.2 %copy-start.2 = (bf16[1,128,512]{2,1,0:T(8,128)(2,1)}, bf16[1,128,512]{2,1,0:T(8,128)(2,1)S(1)}, u32[]{:S(2)}) copy-start(bf16[1,128,512]{2,1,0:T(8,128)(2,1)S(1)} %fusion.11.after_ref) | copy-start | bytes 393220
  164.3 1.0 copy-start.1
  169.6 3.6 %collective-permute-start.4 = (f32[128,1792]{1,0:T(8,128)S(1)}, f32[128,1792]{1,0:T(8,128)S(1)}, u32[]{:S(2)}, u32[]{:S(2)}) collective-permute-start(f32[128,1792]{1,0:T(8,128)S(1)} %get-tuple-element.5), channel_id=1, source_target_pairs={{0,1},{1,0},{2,3},{3,2},{4,5},{5,4},{6,7},{7,6},{8,9},{9,8},{10,11... | collective-permute-start | bytes 2752520 | tf_op jit(solution)/shard_map/ppermute | solution.py:477

commit v4 on v3

--- a/solution.py
+++ b/solution.py
@@ -148,16 +148,20 @@
     return jnp.where(named > 0.0, rank, -1.0)
 
 
-def dispatch_kernel(core_ref, routes_ref, tokens_ref, out_ref, rows, chosen, place, packed, in_sem, out_sem):
+def dispatch_kernel(
+    core_ref, routes_ref, tokens_ref, out_ref, routes, rows, chosen, place, packed, in_sem, out_sem
+):
     dp_count = out_ref.shape[0]
     groups = out_ref.shape[1] // TILES
     loads = [
         pltpu.make_async_copy(tokens_ref.at[:, features_of(g)], rows.at[:, features_of(g)], in_sem.at[g])
         for g in range(groups)
     ]
-    start(loads)
+    routes_load = pltpu.make_async_copy(routes_ref, routes, in_sem.at[groups])
+    start([routes_load] + loads)
     fill_place(place, dp_count)
-    code = rank_code(routes_ref[...]).astype(BF16)
+    wait([routes_load])
+    code = rank_code(routes[...]).astype(BF16)
     tokens = code.shape[1]
     count = dp_count * CAP
     owner, _ = row_of(iota((count, 128), 0), dp_count)
@@ -175,15 +179,16 @@
     shape = (dp_count, TILES * groups, MAIN, BLOCK)
     return pl.pallas_call(
         dispatch_kernel,
-        in_specs=[SMEM, VMEM, HBM],
+        in_specs=[SMEM, HBM, HBM],
         out_specs=HBM,
         out_shape=jax.ShapeDtypeStruct(shape, BF16),
         scratch_shapes=[
+            pltpu.VMEM(routes.shape, jnp.int32),
             pltpu.VMEM(tokens.shape, BF16),
             pltpu.VMEM((dp_count * CAP, count), BF16),
             pltpu.VMEM((4 * dp_count, 4 * dp_count), BF16),
             pltpu.VMEM(shape, BF16),
-            pltpu.SemaphoreType.DMA((groups,)),
+            pltpu.SemaphoreType.DMA((groups + 1,)),
             pltpu.SemaphoreType.DMA((2 * groups,)),
         ],
         compiler_params=PARAMS,
@@ -258,7 +263,7 @@
     staged = [stage_copies(i) for i in range(len(stages))] + [far_copies[:2], far_copies[2:]]
     messages = [message_copy(i) for i in range(len(stages))]
     back_copies = pack_copies(packed, back_ref, back_sem, groups)
-    start([messages[0]] + staged[0] + [messages[1]] + staged[1] + [messages[2]] + staged[2])
+    start(messages + staged[0] + staged[1] + staged[2])
     fill_pick(pick, dp_count)
     fill_place(place, dp_count)
     wait(messages[:1])
@@ -267,7 +272,7 @@
     for i, (first, last) in enumerate(stages):
         wait(staged[i])
         if i + 3 < len(staged):
-            start(messages[i + 3 : i + 4] + staged[i + 3])
+            start(staged[i + 3])
         if 0 < i < len(stages) - 1:
             wait([messages[i + 1]])
             unpack(i + 1)
@@ -334,8 +339,7 @@
     )(core, message, w_in, w_up, in_far, up_far, w_out, out_far)
 
 
-def gates_kernel(core_ref, routes_ref, gates_ref, out_ref):
-    routes, gates = routes_ref[...], gates_ref[...]
+def spread_gates(core, routes, gates, out_ref):
     top, tokens = routes.shape
     count = out_ref.shape[1]
     dp_count = count // CAP
@@ -347,7 +351,7 @@
     high = value.astype(BF16)
     low = (value - high.astype(F32)).astype(BF16)
     owner, _ = row_of(iota((128, count), 1), dp_count)
-    owner = one_hot(iota((128, count), 0), 2 * owner + core_ref[0])
+    owner = one_hot(iota((128, count), 0), 2 * owner + core)
     _, turn = row_of(iota((tokens, count), 1), dp_count)
     here = dot(code.T, owner) == turn.astype(F32)
     for part, source in enumerate((high, low)):
@@ -355,17 +359,22 @@
         out_ref[part * tokens : (part + 1) * tokens] = gate.astype(BF16)
 
 
-def spread_gates(core, routes, gates, dp_count):
-    return pl.pallas_call(
-        gates_kernel,
-        in_specs=[SMEM, VMEM, VMEM],
-        out_specs=VMEM,
-        out_shape=jax.ShapeDtypeStruct((2 * routes.shape[1], dp_count * CAP), BF16),
-        name="gates",
-    )(core, routes, gates)
-
-
-def combine_kernel(core_ref, back_ref, gates_ref, after_ref, keep_ref, send_ref, message, gates, total, pick, sem):
+def combine_kernel(
+    core_ref,
+    back_ref,
+    routes_ref,
+    gates_ref,
+    after_ref,
+    keep_ref,
+    send_ref,
+    message,
+    routes,
+    gates,
+    spread,
+    total,
+    pick,
+    sem,
+):
     core = core_ref[0]
     dp_count = message.shape[0]
     groups = message.shape[1] // TILES
@@ -373,15 +382,20 @@
     loads = [
         pltpu.make_async_copy(tiles_of(back_ref, g), tiles_of(message, g), sem.at[g]) for g in range(groups)
     ]
-    gates_load = [pltpu.make_async_copy(gates_ref, gates, sem.at[groups])]
-    start(gates_load + loads)
+    first = [
+        pltpu.make_async_copy(routes_ref, routes, sem.at[groups]),
+        pltpu.make_async_copy(gates_ref, gates, sem.at[groups + 1]),
+    ]
+    start(first + loads)
     fill_pick(pick, dp_count)
-    wait(gates_load + loads[:1])
+    wait(first)
+    spread_gates(core, routes[...], gates[...], spread)
+    wait(loads[:1])
     rest = pick_rest(message, pick[...], 0)
     side = 0
     for g in range(groups):
         wait(loads[g + 1 : g + 2])
-        value = dot(gates[...], jnp.concatenate([main_rows(message, g), rest], axis=0))
+        value = dot(spread[...], jnp.concatenate([main_rows(message, g), rest], axis=0))
         if g + 1 < groups:
             rest = pick_rest(message, pick[...], g + 1)
         total[:, features_of(g)] = value[:tokens] + value[tokens:]
@@ -399,26 +413,28 @@
             side += 1
 
 
-def combine(core, back, gates, after):
+def combine(core, back, routes, gates, after):
     dp_count, tiles = back.shape[:2]
     groups = tiles // TILES
-    tokens = gates.shape[0] // 2
+    tokens = routes.shape[1]
     out = jax.ShapeDtypeStruct((tokens, groups * GROUP // 2), F32)
     return pl.pallas_call(
         combine_kernel,
-        in_specs=[SMEM, HBM, HBM, HBM],
+        in_specs=[SMEM, HBM, HBM, HBM, HBM],
         out_specs=(VMEM, VMEM),
         out_shape=(out, out),
         scratch_shapes=[
             pltpu.VMEM(back.shape, BF16),
-            pltpu.VMEM(gates.shape, BF16),
+            pltpu.VMEM(routes.shape, jnp.int32),
+            pltpu.VMEM(gates.shape, F32),
+            pltpu.VMEM((2 * tokens, dp_count * CAP), BF16),
             pltpu.VMEM((tokens, groups * GROUP), F32),
             pltpu.VMEM((4 * dp_count, 4 * dp_count), BF16),
-            pltpu.SemaphoreType.DMA((groups + 1,)),
+            pltpu.SemaphoreType.DMA((groups + 2,)),
         ],
         compiler_params=pltpu.CompilerParams(vmem_limit_bytes=16 * 1024 * 1024),
         name="combine",
-    )(core, back, gates, after)
+    )(core, back, routes, gates, after)
 
 
 def attention(query_latent, query_rope, cache_latent, cache_rope, lengths):
@@ -469,11 +485,10 @@
         return lax.ppermute(lax.dynamic_index_in_dim(weight, 1 - index, 0, False), "tp", SWAP)
 
     in_far, up_far, out_far = swap(w_in), swap(w_up), swap(w_out)
-    gates = spread_gates(core, routes, route_gates.T, dp_count)
     back = experts(core, message, w_in, w_up, w_out, in_far, up_far, out_far)
     returned = lax.all_to_all(back, "dp", split_axis=0, concat_axis=0, tiled=True)
     attn_out = attention(query_latent, query_rope, cache_latent, cache_rope, lengths)
-    keep, send = combine(core, returned, gates, attn_out)
+    keep, send = combine(core, returned, routes, route_gates.T, attn_out)
     moe_out = (keep + lax.ppermute(send, "tp", SWAP)).astype(BF16)
     return (moe_out, attn_out)
 

time: 175 us -> 172 us (0.983)
  Pallas kernels: 30.8 us -> 27.7 us
  waiting for transfers between devices: 102 us -> 104 us
    pallas_call x3 -> x2, Pallas kernels: 11.3 us -> 8.53 us  [the longest x1 4.31 us: combine(): pl.pallas_call(combine_kernel, in_specs=[SMEM, HBM, HBM, HBM, HBM], out_s...]
  transfers between devices with their start and end apart: 7 -> 7, of which waited for: 6 -> 7; matrix products, arithmetic and copies ran while one was open for 5% -> 5% of each run, Pallas kernels for 1% -> 0%
where the time goes in v4:
time: 172 us
  waiting for transfers between devices  104 us (60%)
  Pallas kernels  27.7 us (16%)
  starting transfers between devices  27 us (16%)
  local copies, waits for them, and re-layouts  9.03 us (5%)
    all_to_all x1, waiting for transfers between devices, body(): lax.all_to_all(back, 'dp', split_axis=0, concat_axis=0, tiled=True)  52.9 us
    all_to_all x1, waiting for transfers between devices, body(): lax.all_to_all(outbound, 'dp', split_axis=0, concat_axis=0, tiled=True)  38.5 us
    pallas_call x1, Pallas kernels, experts(): pl.pallas_call(expert_kernel, in_specs=[SMEM] + [HBM] * 7, out_specs=HBM,...  19.1 us
    all_to_all x1, starting transfers between devices, body(): lax.all_to_all(outbound, 'dp', split_axis=0, concat_axis=0, tiled=True)  12.2 us
    all_to_all x1, starting transfers between devices, body(): lax.all_to_all(back, 'dp', split_axis=0, concat_axis=0, tiled=True)  10.4 us
    ppermute x3, waiting for transfers between devices, swap(): lax.ppermute(lax.dynamic_index_in_dim(weight, 1 - index, 0, False), 'tp',...  9.48 us
    squeeze x3, local copies, waits for them, and re-layouts, swap(): lax.dynamic_index_in_dim(weight, 1 - index, 0, False)  6.83 us
    pallas_call x1, Pallas kernels, combine(): pl.pallas_call(combine_kernel, in_specs=[SMEM, HBM, HBM, HBM, HBM], out_s...  4.31 us
  transfers between devices with their start and end apart: 7, of which 7 were waited for; matrix products, arithmetic and copies ran while one was open for 5% of the time, Pallas kernels for 0%

profile of v4, /device:TPU:1, one launch (start us, length us, event | category | flops | bytes accessed | tf_op | source)
XLA Modules:
  0.0 171.9 jit_solution(11451212644873430137)
XLA Ops:
  0.6 0.0 copy-start
  0.6 4.2 %dispatch.1 = bf16[64,35,8,128]{3,2,1,0:T(8,128)(2,1)} custom-call(s32[1]{0:T(128)} %bitcast.core_ref, s32[8,128]{1,0:T(8,128)} %bitcast.36, bf16[128,3584]{1,0:T(8,128)(2,1)} %tokens_ref.1), custom_call_target="tpu_custom_call" | custom-call | tf_op jit(solution)/shard_map/dispatch/pallas_call | solution.py:180
  4.9 12.2 %all-to-all-start = ((bf16[64,35,8,128]{3,2,1,0:T(8,128)(2,1)}), bf16[64,35,8,128]{3,2,1,0:T(8,128)(2,1)}, u32[]{:S(2)}, u32[]{:S(2)}) async-start(bf16[64,35,8,128]{3,2,1,0:T(8,128)(2,1)} %dispatch.1), calls=%async_computation | async-start | bytes 9175040 | tf_op jit(solution)/shard_map/all_to_all | solution.py:482
  17.1 2.3 %dynamic-slice_bitcast_fusion.2 = bf16[3584,512]{1,0:T(8,128)(2,1)S(1)} fusion(bf16[2,3584,512]{2,1,0:T(8,128)(2,1)} %in_own_ref.1, s32[]{:T(128)S(6)} %select_n.16), kind=kLoop, calls=%fused_computation.2 | loop fusion | bytes 7340036 | tf_op jit(solution)/shard_map/jit(dynamic_index_in_dim)/squeeze | solution.py:485
  19.4 1.0 collective-permute-start
  20.4 2.3 %dynamic-slice_bitcast_fusion.1 = bf16[3584,512]{1,0:T(8,128)(2,1)S(1)} fusion(bf16[2,3584,512]{2,1,0:T(8,128)(2,1)} %up_own_ref.1, s32[]{:T(128)S(6)} %select_n.16), kind=kLoop, calls=%fused_computation.1 | loop fusion | bytes 7340036 | tf_op jit(solution)/shard_map/jit(dynamic_index_in_dim)/squeeze | solution.py:485
  22.7 0.1 collective-permute-start.1
  22.8 2.3 %dynamic-slice_bitcast_fusion = bf16[512,3584]{1,0:T(8,128)(2,1)S(1)} fusion(bf16[2,512,3584]{2,1,0:T(8,128)(2,1)} %out_own_ref.1, s32[]{:T(128)S(6)} %select_n.16), kind=kLoop, calls=%fused_computation | loop fusion | bytes 7340036 | tf_op jit(solution)/shard_map/jit(dynamic_index_in_dim)/squeeze | solution.py:485
  25.1 0.8 collective-permute-start.2
  25.8 0.6 collective-permute-done.in_far_ref
  26.5 5.2 %collective-permute-done.1.up_far_ref = bf16[3584,512]{1,0:T(8,128)(2,1)S(1)} collective-permute-done((bf16[3584,512]{1,0:T(8,128)(2,1)S(1)}, bf16[3584,512]{1,0:T(8,128)(2,1)S(1)}, u32[]{:S(2)}, u32[]{:S(2)}) %collective-permute-start.1) | collective-permute-done | bytes 3670048 | tf_op jit(solution)/shard_map/ppermute | solution.py:485
  31.7 0.0 copy-done.7
  31.7 1.8 %copy-done.8 = bf16[3584,512]{1,0:T(8,128)(2,1)} copy-done((bf16[3584,512]{1,0:T(8,128)(2,1)}, bf16[3584,512]{1,0:T(8,128)(2,1)S(1)}, u32[]{:S(2)}) %copy-start.8) | copy-done | bytes 3670040
  33.5 3.6 %collective-permute-done.2.out_far_ref = bf16[512,3584]{1,0:T(8,128)(2,1)} collective-permute-done((bf16[512,3584]{1,0:T(8,128)(2,1)S(1)}, bf16[512,3584]{1,0:T(8,128)(2,1)}, u32[]{:S(2)}, u32[]{:S(2)}) %collective-permute-start.2) | collective-permute-done | bytes 3670048 | tf_op jit(solution)/shard_map/ppermute | solution.py:485
  37.1 38.5 %all-to-all-done.message_ref = bf16[64,35,8,128]{3,2,1,0:T(8,128)(2,1)} async-done(((bf16[64,35,8,128]{3,2,1,0:T(8,128)(2,1)}), bf16[64,35,8,128]{3,2,1,0:T(8,128)(2,1)}, u32[]{:S(2)}, u32[]{:S(2)}) %all-to-all-start) | async-done | bytes 4587552 | tf_op jit(solution)/shard_map/all_to_all | solution.py:482
  75.5 19.1 %experts.1 = bf16[64,35,8,128]{3,2,1,0:T(8,128)(2,1)} custom-call(s32[1]{0:T(128)} %bitcast.core_ref, bf16[64,35,8,128]{3,2,1,0:T(8,128)(2,1)} %all-to-all-done.message_ref, bf16[2,3584,512]{2,1,0:T(8,128)(2,1)} %in_own_ref.1, bf16[2,3584,512]{2,1,0:T(8,128)(2,1)} %up_own_ref.1, bf16[3584,512]{1,0:T(8,128)(2,1)} %copy-done.7, bf16[3584,512]{1,0:T(8,128)(2,1)} %copy-done.8, ...), custom_call_target="tpu_custom_call" | custom-call | flops 14092861440 | bytes 33554432 | tf_op jit(solution)/shard_map/experts/pallas_call | solution.py:310
  94.7 0.0 copy-start.5
  94.7 0.0 copy-start.6
  94.7 0.0 copy-start.4
  94.7 10.4 %all-to-all-start.1 = ((bf16[64,35,8,128]{3,2,1,0:T(8,128)(2,1)}), bf16[64,35,8,128]{3,2,1,0:T(8,128)(2,1)}, u32[]{:S(2)}, u32[]{:S(2)}) async-start(bf16[64,35,8,128]{3,2,1,0:T(8,128)(2,1)} %experts.1), calls=%async_computation.1 | async-start | bytes 9175040 | tf_op jit(solution)/shard_map/all_to_all | solution.py:489
  105.1 0.0 copy-start.2
  105.1 0.0 copy-start.3
  105.8 0.0 copy-done.5
  105.8 0.0 copy-done.6
  105.8 0.2 fusion.13
  106.1 0.0 copy-done
  106.1 0.0 copy-done.4
  106.1 0.6 select_reduce_fusion
  106.6 0.2 fusion.4
  106.9 0.4 fusion.1
  107.3 0.1 broadcast_in_dim.41
  107.3 0.1 broadcast_in_dim.40
  107.4 0.1 pad_maximum_fusion
  107.5 0.8 collective-permute-start.3
  108.4 0.1 copy.20
  108.5 0.1 copy.21
  108.6 1.0 collective-permute-done.3
  109.6 0.2 fusion.21
  109.8 0.1 fusion.11.after_ref
  110.0 0.0 copy-start.1
  110.0 52.9 %all-to-all-done.1.back_ref = bf16[64,35,8,128]{3,2,1,0:T(8,128)(2,1)} async-done(((bf16[64,35,8,128]{3,2,1,0:T(8,128)(2,1)}), bf16[64,35,8,128]{3,2,1,0:T(8,128)(2,1)}, u32[]{:S(2)}, u32[]{:S(2)}) %all-to-all-start.1) | async-done | bytes 4587552 | tf_op jit(solution)/shard_map/all_to_all | solution.py:489
  162.9 0.0 copy-done.2
  162.9 0.0 copy-done.3
  162.9 4.3 %combine.1 = (f32[128,1792]{1,0:T(8,128)S(1)}, f32[128,1792]{1,0:T(8,128)S(1)}) custom-call(s32[1]{0:T(128)} %bitcast.core_ref, bf16[64,35,8,128]{3,2,1,0:T(8,128)(2,1)} %all-to-all-done.1.back_ref, s32[8,128]{1,0:T(8,128)S(1)} %bitcast.37, f32[8,128]{1,0:T(8,128)S(1)} %bitcast.38, bf16[1,128,512]{2,1,0:T(8,128)(2,1)S(1)} %fusion.11.after_ref), custom_call_target="tpu_custom_call" | custom-call | tf_op jit(solution)/shard_map/combine/pallas_call | solution.py:421
  167.2 1.7 %collective-permute-start.4 = (f32[128,1792]{1,0:T(8,128)S(1)}, f32[128,1792]{1,0:T(8,128)S(1)}, u32[]{:S(2)}, u32[]{:S(2)}) collective-permute-start(f32[128,1792]{1,0:T(8,128)S(1)} %get-tuple-element.5), channel_id=1, source_target_pairs={{0,1},{1,0},{2,3},{3,2},{4,5},{5,4},{6,7},{7,6},{8,9},{9,8},{10,11... | collective-permute-start | bytes 2752520 | tf_op jit(solution)/shard_map/ppermute | solution.py:492
  168.9 2.1 %collective-permute-done.4 = f32[128,1792]{1,0:T(8,128)S(1)} collective-permute-done((f32[128,1792]{1,0:T(8,128)S(1)}, f32[128,1792]{1,0:T(8,128)S(1)}, u32[]{:S(2)}, u32[]{:S(2)}) %collective-permute-start.4) | collective-permute-done | bytes 917536 | tf_op jit(solution)/shard_map/ppermute | solution.py:492
  171.0 0.9 add_convert_fusion
  171.9 0.0 copy-done.1
  (3 shorter events, 0.0 us)
Async XLA Ops:
  0.6 105.4 %copy-start = (bf16[1,1024,512]{2,1,0:T(8,128)(2,1)S(1)}, bf16[1,1024,512]{2,1,0:T(8,128)(2,1)}, u32[]{:S(2)}) copy-start(bf16[1,1024,512]{2,1,0:T(8,128)(2,1)} %param.19) | copy-start | bytes 3145732
  4.9 70.7 %all-to-all-start = ((bf16[64,35,8,128]{3,2,1,0:T(8,128)(2,1)}), bf16[64,35,8,128]{3,2,1,0:T(8,128)(2,1)}, u32[]{:S(2)}, u32[]{:S(2)}) async-start(bf16[64,35,8,128]{3,2,1,0:T(8,128)(2,1)} %dispatch.1), calls=%async_computation | async-start | bytes 9175040 | tf_op jit(solution)/shard_map/all_to_all | solution.py:482
  19.4 7.1 %collective-permute-start = (bf16[3584,512]{1,0:T(8,128)(2,1)S(1)}, bf16[3584,512]{1,0:T(8,128)(2,1)S(1)}, u32[]{:S(2)}, u32[]{:S(2)}) collective-permute-start(bf16[3584,512]{1,0:T(8,128)(2,1)S(1)} %dynamic-slice_bitcast_fusion.2), channel_id=1, source_target_pairs={{0,1},{1,0},{2,3},{3,2},{4,5},{5,4},{6,7},{7,6},{8,9},{9,8},{10,11... | collective-permute-start | bytes 11010056 | tf_op jit(solution)/shard_map/ppermute | solution.py:485
  22.7 9.0 %collective-permute-start.1 = (bf16[3584,512]{1,0:T(8,128)(2,1)S(1)}, bf16[3584,512]{1,0:T(8,128)(2,1)S(1)}, u32[]{:S(2)}, u32[]{:S(2)}) collective-permute-start(bf16[3584,512]{1,0:T(8,128)(2,1)S(1)} %dynamic-slice_bitcast_fusion.1), channel_id=1, source_target_pairs={{0,1},{1,0},{2,3},{3,2},{4,5},{5,4},{6,7},{7,6},{8,9},{9,8},{10,11... | collective-permute-start | bytes 11010056 | tf_op jit(solution)/shard_map/ppermute | solution.py:485
  25.1 12.0 %collective-permute-start.2 = (bf16[512,3584]{1,0:T(8,128)(2,1)S(1)}, bf16[512,3584]{1,0:T(8,128)(2,1)}, u32[]{:S(2)}, u32[]{:S(2)}) collective-permute-start(bf16[512,3584]{1,0:T(8,128)(2,1)S(1)} %dynamic-slice_bitcast_fusion), channel_id=1, source_target_pairs={{0,1},{1,0},{2,3},{3,2},{4,5},{5,4},{6,7},{7,6},{8,9},{9,8},{10,11... | collective-permute-start | bytes 11010056 | tf_op jit(solution)/shard_map/ppermute | solution.py:485
  26.5 5.3 %copy-start.7 = (bf16[3584,512]{1,0:T(8,128)(2,1)}, bf16[3584,512]{1,0:T(8,128)(2,1)S(1)}, u32[]{:S(2)}) copy-start(bf16[3584,512]{1,0:T(8,128)(2,1)S(1)} %collective-permute-done.in_far_ref) | copy-start | bytes 11010052
  31.7 1.8 %copy-start.8 = (bf16[3584,512]{1,0:T(8,128)(2,1)}, bf16[3584,512]{1,0:T(8,128)(2,1)S(1)}, u32[]{:S(2)}) copy-start(bf16[3584,512]{1,0:T(8,128)(2,1)S(1)} %collective-permute-done.1.up_far_ref) | copy-start | bytes 11010052
  94.7 11.1 %copy-start.5 = (bf16[1,64,1024]{2,1,0:T(8,128)(2,1)S(1)}, bf16[1,64,1024]{2,1,0:T(8,128)(2,1)}, u32[]{:S(2)}) copy-start(bf16[1,64,1024]{2,1,0:T(8,128)(2,1)} %param.20) | copy-start | bytes 393220
  94.7 11.1 %copy-start.6 = (bf16[1,128,64]{1,2,0:T(8,128)(2,1)S(1)}, bf16[1,128,64]{1,2,0:T(8,128)(2,1)}, u32[]{:S(2)}) copy-start(bf16[1,128,64]{1,2,0:T(8,128)(2,1)} %param.18) | copy-start | bytes 49156
  94.7 11.4 %copy-start.4 = (bf16[1,128,512]{2,1,0:T(8,128)(2,1)S(1)}, bf16[1,128,512]{2,1,0:T(8,128)(2,1)}, u32[]{:S(2)}) copy-start(bf16[1,128,512]{2,1,0:T(8,128)(2,1)} %param.17) | copy-start | bytes 393220
  94.7 68.1 %all-to-all-start.1 = ((bf16[64,35,8,128]{3,2,1,0:T(8,128)(2,1)}), bf16[64,35,8,128]{3,2,1,0:T(8,128)(2,1)}, u32[]{:S(2)}, u32[]{:S(2)}) async-start(bf16[64,35,8,128]{3,2,1,0:T(8,128)(2,1)} %experts.1), calls=%async_computation.1 | async-start | bytes 9175040 | tf_op jit(solution)/shard_map/all_to_all | solution.py:489
  105.1 57.8 %copy-start.2 = (s32[128,8]{0,1:T(8,128)S(1)}, s32[128,8]{0,1:T(8,128)}, u32[]{:S(2)}) copy-start(s32[128,8]{0,1:T(8,128)} %param.12) | copy-start | bytes 12292
  105.1 57.8 %copy-start.3 = (f32[128,8]{0,1:T(8,128)S(1)}, f32[128,8]{0,1:T(8,128)}, u32[]{:S(2)}) copy-start(f32[128,8]{0,1:T(8,128)} %param.13) | copy-start | bytes 12292
  107.5 2.1 %collective-permute-start.3 = (f32[1,128,640]{2,1,0:T(8,128)S(1)}, f32[1,128,640]{2,1,0:T(8,128)S(1)}, u32[]{:S(2)}, u32[]{:S(2)}) collective-permute-start(f32[1,128,640]{2,1,0:T(8,128)S(1)} %pad_maximum_fusion), channel_id=1, source_target_pairs={{0,1},{1,0},{2,3},{3,2},{4,5},{5,4},{6,7},{7,6},{8,9},{9,8},{10,11... | collective-permute-start | bytes 983048 | tf_op jit(solution)/shard_map/ppermute | solution.py:456
  110.0 61.9 %copy-start.1 = (bf16[1,128,512]{2,1,0:T(8,128)(2,1)}, bf16[1,128,512]{2,1,0:T(8,128)(2,1)S(1)}, u32[]{:S(2)}) copy-start(bf16[1,128,512]{2,1,0:T(8,128)(2,1)S(1)} %fusion.11.after_ref) | copy-start | bytes 393220
  167.2 3.8 %collective-permute-start.4 = (f32[128,1792]{1,0:T(8,128)S(1)}, f32[128,1792]{1,0:T(8,128)S(1)}, u32[]{:S(2)}, u32[]{:S(2)}) collective-permute-start(f32[128,1792]{1,0:T(8,128)S(1)} %get-tuple-element.5), channel_id=1, source_target_pairs={{0,1},{1,0},{2,3},{3,2},{4,5},{5,4},{6,7},{7,6},{8,9},{9,8},{10,11... | collective-permute-start | bytes 2752520 | tf_op jit(solution)/shard_map/ppermute | solution.py:492

commit v5 on v4

--- a/solution.py
+++ b/solution.py
@@ -36,14 +36,25 @@
     return (a == b).astype(F32).astype(BF16)
 
 
-def tiles_of(ref, group):
-    return ref.at[:, pl.ds(group * TILES, TILES)]
+def groups_of(features):
+    blocks = features // BLOCK
+    return [(at * BLOCK, min(4, blocks - at), at // 4 * TILES) for at in range(0, blocks, 4)]
+
+
+def tiles_in(features):
+    return sum(blocks + 1 for _, blocks, _ in groups_of(features))
+
+
+def back_groups(features):
+    half = features // 2
+    shift = tiles_in(half)
+    return [(h * half + at, blocks, h * shift + t) for h in range(2) for at, blocks, t in groups_of(half)]
 
 
 def pack_copies(packed, messages, sems, groups):
     copies = []
-    for g in range(groups):
-        for i, part in enumerate((pl.ds(g * TILES, TILES - 1), pl.ds(g * TILES + TILES - 1, 1))):
+    for g, (_, blocks, tile) in enumerate(groups):
+        for i, part in enumerate((pl.ds(tile, blocks), pl.ds(tile + blocks, 1))):
             copies.append(pltpu.make_async_copy(packed.at[:, part], messages.at[:, part], sems.at[2 * g + i]))
     return copies
 
@@ -80,43 +91,45 @@
     ref[...] = one_hot(iota((size, size), 1), unit_of(iota((size, size), 0), dp_count // 2))
 
 
-def pack(value, ref, group):
+def pack(value, ref, tile):
     dp_count = ref.shape[0]
+    blocks = value.shape[1] // BLOCK
     main, half = dp_count * MAIN, dp_count // 2
-    for f in range(4):
+    for f in range(blocks):
         part = value[:main, block_of(f)].astype(BF16)
-        ref[:, group * TILES + f] = part.reshape(dp_count, MAIN, BLOCK)
+        ref[:, tile + f] = part.reshape(dp_count, MAIN, BLOCK)
     rest = value[main:].astype(BF16)
+    empty = [jnp.zeros((2 * half, BLOCK), BF16)] * (4 - blocks)
     sides = [rest[: 2 * half], rest[2 * half :]]
-    sides = [jnp.concatenate([side[:, block_of(f)] for f in range(4)], axis=0) for side in sides]
+    sides = [jnp.concatenate([side[:, block_of(f)] for f in range(blocks)] + empty, axis=0) for side in sides]
     return jnp.concatenate(sides, axis=1)
 
 
-def place_rest(rest, place, ref, group):
+def place_rest(rest, place, ref, tile):
     half = ref.shape[0] // 2
     rest = dot(place, rest)
     for h in range(2):
         part = rest[:, block_of(h)].astype(BF16)
-        ref[h * half : (h + 1) * half, group * TILES + 4] = part.reshape(half, MAIN, BLOCK)
+        ref[h * half : (h + 1) * half, tile] = part.reshape(half, MAIN, BLOCK)
 
 
 def pack_all(groups, value_of, place, packed, copies):
-    rest = None
-    for g in range(groups):
-        value = value_of(g)
-        if rest is not None:
-            place_rest(rest, place, packed, g - 1)
-        rest = pack(value, packed, g)
+    rest, last = None, 0
+    for g, (at, blocks, tile) in enumerate(groups):
+        value = value_of(slice(at, at + blocks * BLOCK))
+        if g:
+            place_rest(rest, place, packed, last)
+        rest, last = pack(value, packed, tile), tile + blocks
         start([copies[2 * g]] + ([copies[2 * g - 1]] if g else []))
-    place_rest(rest, place, packed, groups - 1)
+    place_rest(rest, place, packed, last)
     start(copies[-1:])
     wait(copies)
 
 
-def pick_rest(ref, pick, group):
+def pick_rest(ref, pick, tile):
     dp_count = ref.shape[0]
     main, half = dp_count * MAIN, dp_count // 2
-    rest = ref[:, group * TILES + 4].reshape(main, BLOCK)
+    rest = ref[:, tile].reshape(main, BLOCK)
     rest = dot(pick, jnp.concatenate([rest[: main // 2], rest[main // 2 :]], axis=1)).astype(BF16)
     sides = [
         jnp.concatenate([rest[2 * half * f : 2 * half * (f + 1), block_of(h)] for f in range(4)], axis=1)
@@ -125,9 +138,9 @@
     return jnp.concatenate(sides, axis=0)
 
 
-def main_rows(ref, group):
+def main_rows(ref, tile, blocks):
     main = ref.shape[0] * MAIN
-    return jnp.concatenate([ref[:, group * TILES + f].reshape(main, BLOCK) for f in range(4)], axis=1)
+    return jnp.concatenate([ref[:, tile + f].reshape(main, BLOCK) for f in range(blocks)], axis=1)
 
 
 def row_of(index, dp_count):
@@ -169,8 +182,9 @@
     _, turn = row_of(iota((count, tokens), 0), dp_count)
     chosen[...] = one_hot(spread, turn.astype(F32))
     wait(loads)
-    stores = pack_copies(packed, out_ref, out_sem, groups)
-    pack_all(groups, lambda g: dot(chosen[...], rows[:, features_of(g)]), place[...], packed, stores)
+    parts = groups_of(rows.shape[1])
+    stores = pack_copies(packed, out_ref, out_sem, parts)
+    pack_all(parts, lambda part: dot(chosen[...], rows[:, part]), place[...], packed, stores)
 
 
 def dispatch(core, routes, tokens, dp_count):
@@ -251,8 +265,8 @@
 
     def unpack(i):
         for g in range(*stages[i]):
-            rows[: dp_count * MAIN, features_of(g)] = main_rows(message, g)
-            rows[dp_count * MAIN :, features_of(g)] = pick_rest(message, pick[...], g)
+            rows[: dp_count * MAIN, features_of(g)] = main_rows(message, g * TILES, 4)
+            rows[dp_count * MAIN :, features_of(g)] = pick_rest(message, pick[...], g * TILES + 4)
 
     far_copies = [
         copy(in_far_ref, in_far, far_sem.at[0]),
@@ -262,7 +276,8 @@
     ]
     staged = [stage_copies(i) for i in range(len(stages))] + [far_copies[:2], far_copies[2:]]
     messages = [message_copy(i) for i in range(len(stages))]
-    back_copies = pack_copies(packed, back_ref, back_sem, groups)
+    parts = back_groups(rows.shape[1])
+    back_copies = pack_copies(packed, back_ref, back_sem, parts)
     start(messages + staged[0] + staged[1] + staged[2])
     fill_pick(pick, dp_count)
     fill_place(place, dp_count)
@@ -295,7 +310,7 @@
     up = dot(rows[...], up_far[...])
     hidden[:, width:] = (gate / (1.0 + jnp.exp(-gate)) * up).astype(BF16)
     wait(far_copies[2:])
-    pack_all(groups, lambda g: dot(hidden[...], out_both[:, features_of(g)]), place[...], packed, back_copies)
+    pack_all(parts, lambda part: dot(hidden[...], out_both[:, part]), place[...], packed, back_copies)
 
 
 def experts(core, message, w_in, w_up, w_out, in_far, up_far, out_far):
@@ -304,6 +319,7 @@
     features, width = in_far.shape
     count = dp_count * CAP
     stages = len(stages_of(groups))
+    back = (dp_count, 2 * tiles_in(features // 2), MAIN, BLOCK)
     weight = pltpu.VMEM((features, width), BF16)
     total = pltpu.VMEM((count, width), F32)
     square = pltpu.VMEM((4 * dp_count, 4 * dp_count), BF16)
@@ -311,7 +327,7 @@
         expert_kernel,
         in_specs=[SMEM] + [HBM] * 7,
         out_specs=HBM,
-        out_shape=jax.ShapeDtypeStruct(message.shape, BF16),
+        out_shape=jax.ShapeDtypeStruct(back, BF16),
         scratch_shapes=[
             pltpu.VMEM(message.shape, BF16),
             pltpu.VMEM((count, features), BF16),
@@ -323,13 +339,13 @@
             total,
             total,
             pltpu.VMEM((count, 2 * width), BF16),
-            pltpu.VMEM(message.shape, BF16),
+            pltpu.VMEM(back, BF16),
             square,
             square,
             pltpu.SemaphoreType.DMA((stages,)),
             pltpu.SemaphoreType.DMA((2 * stages,)),
             pltpu.SemaphoreType.DMA((4,)),
-            pltpu.SemaphoreType.DMA((2 * groups,)),
+            pltpu.SemaphoreType.DMA((2 * len(back_groups(features)),)),
         ],
         compiler_params=PARAMS,
         cost_estimate=pl.CostEstimate(
@@ -339,9 +355,8 @@
     )(core, message, w_in, w_up, in_far, up_far, w_out, out_far)
 
 
-def spread_gates(core, routes, gates, out_ref):
+def spread_gates(core, routes, gates, count):
     top, tokens = routes.shape
-    count = out_ref.shape[1]
     dp_count = count // CAP
     code = rank_code(routes).astype(BF16)
     slots = iota((128, tokens), 0)
@@ -354,87 +369,78 @@
     owner = one_hot(iota((128, count), 0), 2 * owner + core)
     _, turn = row_of(iota((tokens, count), 1), dp_count)
     here = dot(code.T, owner) == turn.astype(F32)
-    for part, source in enumerate((high, low)):
-        gate = jnp.where(here, dot(source.T, owner), 0.0)
-        out_ref[part * tokens : (part + 1) * tokens] = gate.astype(BF16)
+    parts = [jnp.where(here, dot(source.T, owner), 0.0) for source in (high, low)]
+    return jnp.concatenate(parts, axis=0).astype(BF16)
 
 
 def combine_kernel(
-    core_ref,
-    back_ref,
-    routes_ref,
-    gates_ref,
-    after_ref,
-    keep_ref,
-    send_ref,
-    message,
-    routes,
-    gates,
-    spread,
-    total,
-    pick,
-    sem,
+    back_ref, routes_ref, gates_ref, after_ref, out_ref, message, routes, gates, spread, total, pick, sem, out_sem
 ):
-    core = core_ref[0]
     dp_count = message.shape[0]
-    groups = message.shape[1] // TILES
-    tokens, half = keep_ref.shape
-    loads = [
-        pltpu.make_async_copy(tiles_of(back_ref, g), tiles_of(message, g), sem.at[g]) for g in range(groups)
-    ]
+    tiles = message.shape[1] // 2
+    count = dp_count * CAP
+    tokens = total.shape[0]
+    parts = groups_of(total.shape[1])
+    loads, stores = [], []
+    for g, (at, blocks, tile) in enumerate(parts):
+        lanes = slice(at, at + blocks * BLOCK)
+        stores.append(pltpu.make_async_copy(total.at[:, lanes], out_ref.at[:, lanes], out_sem.at[g]))
+        for core in range(2):
+            part = pl.ds(core * tiles + tile, blocks + 1)
+            loads.append(pltpu.make_async_copy(back_ref.at[:, part], message.at[:, part], sem.at[2 * g + core]))
     first = [
-        pltpu.make_async_copy(routes_ref, routes, sem.at[groups]),
-        pltpu.make_async_copy(gates_ref, gates, sem.at[groups + 1]),
+        pltpu.make_async_copy(routes_ref, routes, sem.at[len(loads)]),
+        pltpu.make_async_copy(gates_ref, gates, sem.at[len(loads) + 1]),
     ]
     start(first + loads)
     fill_pick(pick, dp_count)
     wait(first)
-    spread_gates(core, routes[...], gates[...], spread)
-    wait(loads[:1])
-    rest = pick_rest(message, pick[...], 0)
-    side = 0
-    for g in range(groups):
-        wait(loads[g + 1 : g + 2])
-        value = dot(spread[...], jnp.concatenate([main_rows(message, g), rest], axis=0))
-        if g + 1 < groups:
-            rest = pick_rest(message, pick[...], g + 1)
-        total[:, features_of(g)] = value[:tokens] + value[tokens:]
-        if (g + 1) * GROUP >= (side + 1) * half:
-            part = slice(side * half, (side + 1) * half)
-
-            @pl.when(core == side)
-            def _():
-                keep_ref[...] = total[:, part]
-
-            @pl.when(core != side)
-            def _():
-                send_ref[...] = total[:, part]
-
-            side += 1
-
-
-def combine(core, back, routes, gates, after):
-    dp_count, tiles = back.shape[:2]
-    groups = tiles // TILES
+    for core in range(2):
+        spread[:, core * count : (core + 1) * count] = spread_gates(core, routes[...], gates[...], count)
+
+    def picked(g):
+        _, blocks, tile = parts[g]
+        return [pick_rest(message, pick[...], core * tiles + tile + blocks) for core in range(2)]
+
+    wait(loads[:2])
+    rest = picked(0)
+    for g, (at, blocks, tile) in enumerate(parts):
+        wait(loads[2 * g + 2 : 2 * g + 4])
+        rows = []
+        for core in range(2):
+            rows += [main_rows(message, core * tiles + tile, blocks), rest[core][:, : blocks * BLOCK]]
+        value = dot(spread[...], jnp.concatenate(rows, axis=0))
+        if g + 1 < len(parts):
+            rest = picked(g + 1)
+        total[:, at : at + blocks * BLOCK] = (value[:tokens] + value[tokens:]).astype(BF16)
+        start(stores[g : g + 1])
+    wait(stores)
+
+
+def combine(back, routes, gates, after):
+    dp_count, tiles = back.shape[0], back.shape[1]
     tokens = routes.shape[1]
-    out = jax.ShapeDtypeStruct((tokens, groups * GROUP // 2), F32)
+    blocks = tiles // 2 - -(-(tiles // 2) // TILES)
+    parts = len(groups_of(blocks * BLOCK))
+    out = jax.ShapeDtypeStruct((tokens, blocks * BLOCK), BF16)
     return pl.pallas_call(
         combine_kernel,
-        in_specs=[SMEM, HBM, HBM, HBM, HBM],
-        out_specs=(VMEM, VMEM),
-        out_shape=(out, out),
+        in_specs=[HBM, HBM, HBM, HBM],
+        out_specs=HBM,
+        out_shape=out,
         scratch_shapes=[
             pltpu.VMEM(back.shape, BF16),
             pltpu.VMEM(routes.shape, jnp.int32),
             pltpu.VMEM(gates.shape, F32),
-            pltpu.VMEM((2 * tokens, dp_count * CAP), BF16),
-            pltpu.VMEM((tokens, groups * GROUP), F32),
+            pltpu.VMEM((2 * tokens, 2 * dp_count * CAP), BF16),
+            pltpu.VMEM(out.shape, BF16),
             pltpu.VMEM((4 * dp_count, 4 * dp_count), BF16),
-            pltpu.SemaphoreType.DMA((groups + 2,)),
+            pltpu.SemaphoreType.DMA((2 * parts + 2,)),
+            pltpu.SemaphoreType.DMA((parts,)),
         ],
-        compiler_params=pltpu.CompilerParams(vmem_limit_bytes=16 * 1024 * 1024),
+        compiler_params=PARAMS,
         name="combine",
-    )(core, back, routes, gates, after)
+    )(back, routes, gates, after)
 
 
 def attention(query_latent, query_rope, cache_latent, cache_rope, lengths):
@@ -486,10 +492,11 @@
 
     in_far, up_far, out_far = swap(w_in), swap(w_up), swap(w_out)
     back = experts(core, message, w_in, w_up, w_out, in_far, up_far, out_far)
-    returned = lax.all_to_all(back, "dp", split_axis=0, concat_axis=0, tiled=True)
+    parts = back.shape
+    back = back.reshape(2 * parts[0], parts[1] // 2, MAIN, BLOCK)
+    returned = lax.all_to_all(back, ("dp", "tp"), split_axis=0, concat_axis=0, tiled=True)
     attn_out = attention(query_latent, query_rope, cache_latent, cache_rope, lengths)
-    keep, send = combine(core, returned, routes, route_gates.T, attn_out)
-    moe_out = (keep + lax.ppermute(send, "tp", SWAP)).astype(BF16)
+    moe_out = combine(returned.reshape(parts), routes, route_gates.T, attn_out)
     return (moe_out, attn_out)
 
 

time: 172 us -> 168 us (0.977)
  waiting for transfers between devices: 104 us -> 101 us
  starting transfers between devices: 27 us -> 24.7 us
    ppermute x1 -> x0, waiting for transfers between devices: 2.1 us -> none  [body(): moe_out = (keep + lax.ppermute(send, 'tp', SWAP)).astype(BF16)]
    ppermute x1 -> x0, starting transfers between devices: 1.73 us -> none  [body(): moe_out = (keep + lax.ppermute(send, 'tp', SWAP)).astype(BF16)]
  transfers between devices with their start and end apart: 7 -> 6, of which waited for: 7 -> 6; matrix products, arithmetic and copies ran while one was open for 5% -> 6% of each run, Pallas kernels for 0% -> 0%
where the time goes in v5:
time: 168 us
  waiting for transfers between devices  101 us (60%)
  Pallas kernels  28.4 us (17%)
  starting transfers between devices  24.7 us (15%)
  local copies, waits for them, and re-layouts  9.03 us (5%)
    all_to_all x1, waiting for transfers between devices, body(): lax.all_to_all(back, ('dp', 'tp'), split_axis=0, concat_axis=0, tiled=True)  52.4 us
    all_to_all x1, waiting for transfers between devices, body(): lax.all_to_all(outbound, 'dp', split_axis=0, concat_axis=0, tiled=True)  38.5 us
    pallas_call x1, Pallas kernels, experts(): pl.pallas_call(expert_kernel, in_specs=[SMEM] + [HBM] * 7, out_specs=HBM,...  19.4 us
    all_to_all x1, starting transfers between devices, body(): lax.all_to_all(outbound, 'dp', split_axis=0, concat_axis=0, tiled=True)  12.2 us
    ppermute x3, waiting for transfers between devices, swap(): lax.ppermute(lax.dynamic_index_in_dim(weight, 1 - index, 0, False), 'tp',...  9.46 us
    all_to_all x1, starting transfers between devices, body(): lax.all_to_all(back, ('dp', 'tp'), split_axis=0, concat_axis=0, tiled=True)  9.37 us
    squeeze x3, local copies, waits for them, and re-layouts, swap(): lax.dynamic_index_in_dim(weight, 1 - index, 0, False)  6.83 us
    pallas_call x1, Pallas kernels, combine(): pl.pallas_call(combine_kernel, in_specs=[HBM, HBM, HBM, HBM], out_specs=H...  4.79 us
  transfers between devices with their start and end apart: 6, of which 6 were waited for; matrix products, arithmetic and copies ran while one was open for 6% of the time, Pallas kernels for 0%

profile of v5, /device:TPU:1, one launch (start us, length us, event | category | flops | bytes accessed | tf_op | source)
XLA Modules:
  0.0 167.6 jit_solution(237187593977340745)
XLA Ops:
  0.6 0.0 copy-start
  0.6 4.2 %dispatch.1 = bf16[64,35,8,128]{3,2,1,0:T(8,128)(2,1)} custom-call(s32[1]{0:T(128)} %bitcast.core_ref, s32[8,128]{1,0:T(8,128)} %bitcast.40, bf16[128,3584]{1,0:T(8,128)(2,1)} %tokens_ref.1), custom_call_target="tpu_custom_call" | custom-call | tf_op jit(solution)/shard_map/dispatch/pallas_call | solution.py:194
  4.8 12.2 %all-to-all-start = ((bf16[64,35,8,128]{3,2,1,0:T(8,128)(2,1)}), bf16[64,35,8,128]{3,2,1,0:T(8,128)(2,1)}, u32[]{:S(2)}, u32[]{:S(2)}) async-start(bf16[64,35,8,128]{3,2,1,0:T(8,128)(2,1)} %dispatch.1), calls=%async_computation | async-start | bytes 9175040 | tf_op jit(solution)/shard_map/all_to_all | solution.py:488
  17.0 2.3 %dynamic-slice_bitcast_fusion.2 = bf16[3584,512]{1,0:T(8,128)(2,1)S(1)} fusion(bf16[2,3584,512]{2,1,0:T(8,128)(2,1)} %in_own_ref.1, s32[]{:T(128)S(6)} %select_n.16), kind=kLoop, calls=%fused_computation.2 | loop fusion | bytes 7340036 | tf_op jit(solution)/shard_map/jit(dynamic_index_in_dim)/squeeze | solution.py:491
  19.3 1.0 collective-permute-start
  20.4 2.3 %dynamic-slice_bitcast_fusion.1 = bf16[3584,512]{1,0:T(8,128)(2,1)S(1)} fusion(bf16[2,3584,512]{2,1,0:T(8,128)(2,1)} %up_own_ref.1, s32[]{:T(128)S(6)} %select_n.16), kind=kLoop, calls=%fused_computation.1 | loop fusion | bytes 7340036 | tf_op jit(solution)/shard_map/jit(dynamic_index_in_dim)/squeeze | solution.py:491
  22.7 0.1 collective-permute-start.1
  22.8 2.3 %dynamic-slice_bitcast_fusion = bf16[512,3584]{1,0:T(8,128)(2,1)S(1)} fusion(bf16[2,512,3584]{2,1,0:T(8,128)(2,1)} %out_own_ref.1, s32[]{:T(128)S(6)} %select_n.16), kind=kLoop, calls=%fused_computation | loop fusion | bytes 7340036 | tf_op jit(solution)/shard_map/jit(dynamic_index_in_dim)/squeeze | solution.py:491
  25.0 0.8 collective-permute-start.2
  25.8 0.6 collective-permute-done.in_far_ref
  26.4 0.0 copy-start.4
  26.4 5.2 %collective-permute-done.1.up_far_ref = bf16[3584,512]{1,0:T(8,128)(2,1)S(1)} collective-permute-done((bf16[3584,512]{1,0:T(8,128)(2,1)S(1)}, bf16[3584,512]{1,0:T(8,128)(2,1)S(1)}, u32[]{:S(2)}, u32[]{:S(2)}) %collective-permute-start.1) | collective-permute-done | bytes 3670048 | tf_op jit(solution)/shard_map/ppermute | solution.py:491
  31.7 0.0 copy-done.4
  31.7 0.0 copy-start.5
  31.7 1.8 %copy-done.5 = bf16[3584,512]{1,0:T(8,128)(2,1)} copy-done((bf16[3584,512]{1,0:T(8,128)(2,1)}, bf16[3584,512]{1,0:T(8,128)(2,1)S(1)}, u32[]{:S(2)}) %copy-start.5) | copy-done | bytes 3670040
  33.5 3.6 %collective-permute-done.2.out_far_ref = bf16[512,3584]{1,0:T(8,128)(2,1)} collective-permute-done((bf16[512,3584]{1,0:T(8,128)(2,1)S(1)}, bf16[512,3584]{1,0:T(8,128)(2,1)}, u32[]{:S(2)}, u32[]{:S(2)}) %collective-permute-start.2) | collective-permute-done | bytes 3670048 | tf_op jit(solution)/shard_map/ppermute | solution.py:491
  37.0 38.5 %all-to-all-done.message_ref = bf16[64,35,8,128]{3,2,1,0:T(8,128)(2,1)} async-done(((bf16[64,35,8,128]{3,2,1,0:T(8,128)(2,1)}), bf16[64,35,8,128]{3,2,1,0:T(8,128)(2,1)}, u32[]{:S(2)}, u32[]{:S(2)}) %all-to-all-start) | async-done | bytes 4587552 | tf_op jit(solution)/shard_map/all_to_all | solution.py:488
  75.5 19.4 %experts.1 = bf16[64,36,8,128]{3,2,1,0:T(8,128)(2,1)} custom-call(s32[1]{0:T(128)} %bitcast.core_ref, bf16[64,35,8,128]{3,2,1,0:T(8,128)(2,1)} %all-to-all-done.message_ref, bf16[2,3584,512]{2,1,0:T(8,128)(2,1)} %in_own_ref.1, bf16[2,3584,512]{2,1,0:T(8,128)(2,1)} %up_own_ref.1, bf16[3584,512]{1,0:T(8,128)(2,1)} %copy-done.4, bf16[3584,512]{1,0:T(8,128)(2,1)} %copy-done.5, ...), custom_call_target="tpu_custom_call" | custom-call | flops 14092861440 | bytes 33554432 | tf_op jit(solution)/shard_map/experts/pallas_call | solution.py:326
  95.0 0.0 copy-start.2
  95.0 0.0 copy-start.3
  95.0 0.0 copy-start.1
  95.0 9.4 %all-to-all-start.1 = ((bf16[128,18,8,128]{3,2,1,0:T(8,128)(2,1)}), bf16[128,18,8,128]{3,2,1,0:T(8,128)(2,1)}, u32[]{:S(2)}, u32[]{:S(2)}) async-start(bf16[128,18,8,128]{3,2,1,0:T(8,128)(2,1)} %bitcast.38), calls=%async_computation.1 | async-start | bytes 9437184 | tf_op jit(solution)/shard_map/all_to_all | solution.py:497
  105.0 0.0 copy-done.2
  105.0 0.0 copy-done.3
  105.1 0.2 fusion.13
  105.3 0.0 copy-done
  105.3 0.0 copy-done.1
  105.3 0.6 select_reduce_fusion
  105.9 0.2 fusion.4
  106.1 0.4 fusion.1
  106.5 0.1 broadcast_in_dim.41
  106.6 0.1 broadcast_in_dim.40
  106.7 0.1 pad_maximum_fusion
  106.8 1.2 collective-permute-start.3
  108.0 0.1 copy.20
  108.1 0.1 copy.21
  108.2 1.0 collective-permute-done.3
  109.2 0.2 fusion.21
  109.5 0.8 fusion.11.after_ref
  110.2 52.4 %all-to-all-done.1 = bf16[128,18,8,128]{3,2,1,0:T(8,128)(2,1)} async-done(((bf16[128,18,8,128]{3,2,1,0:T(8,128)(2,1)}), bf16[128,18,8,128]{3,2,1,0:T(8,128)(2,1)}, u32[]{:S(2)}, u32[]{:S(2)}) %all-to-all-start.1) | async-done | bytes 4718624 | tf_op jit(solution)/shard_map/all_to_all | solution.py:497
  162.6 4.8 %combine.1 = bf16[128,1792]{1,0:T(8,128)(2,1)} custom-call(bf16[64,36,8,128]{3,2,1,0:T(8,128)(2,1)} %bitcast.6.back_ref, s32[8,128]{1,0:T(8,128)} %bitcast.41, f32[8,128]{1,0:T(8,128)} %bitcast.44, bf16[1,128,512]{2,1,0:T(8,128)(2,1)} %fusion.11.after_ref), custom_call_target="tpu_custom_call" | custom-call | tf_op jit(solution)/shard_map/combine/pallas_call | solution.py:426
  (1 shorter events, 0.0 us)
Async XLA Ops:
  0.6 104.7 %copy-start = (bf16[1,1024,512]{2,1,0:T(8,128)(2,1)S(1)}, bf16[1,1024,512]{2,1,0:T(8,128)(2,1)}, u32[]{:S(2)}) copy-start(bf16[1,1024,512]{2,1,0:T(8,128)(2,1)} %param.19) | copy-start | bytes 3145732
  4.8 70.7 %all-to-all-start = ((bf16[64,35,8,128]{3,2,1,0:T(8,128)(2,1)}), bf16[64,35,8,128]{3,2,1,0:T(8,128)(2,1)}, u32[]{:S(2)}, u32[]{:S(2)}) async-start(bf16[64,35,8,128]{3,2,1,0:T(8,128)(2,1)} %dispatch.1), calls=%async_computation | async-start | bytes 9175040 | tf_op jit(solution)/shard_map/all_to_all | solution.py:488
  19.3 7.1 %collective-permute-start = (bf16[3584,512]{1,0:T(8,128)(2,1)S(1)}, bf16[3584,512]{1,0:T(8,128)(2,1)S(1)}, u32[]{:S(2)}, u32[]{:S(2)}) collective-permute-start(bf16[3584,512]{1,0:T(8,128)(2,1)S(1)} %dynamic-slice_bitcast_fusion.2), channel_id=1, source_target_pairs={{0,1},{1,0},{2,3},{3,2},{4,5},{5,4},{6,7},{7,6},{8,9},{9,8},{10,11... | collective-permute-start | bytes 11010056 | tf_op jit(solution)/shard_map/ppermute | solution.py:491
  22.7 9.0 %collective-permute-start.1 = (bf16[3584,512]{1,0:T(8,128)(2,1)S(1)}, bf16[3584,512]{1,0:T(8,128)(2,1)S(1)}, u32[]{:S(2)}, u32[]{:S(2)}) collective-permute-start(bf16[3584,512]{1,0:T(8,128)(2,1)S(1)} %dynamic-slice_bitcast_fusion.1), channel_id=1, source_target_pairs={{0,1},{1,0},{2,3},{3,2},{4,5},{5,4},{6,7},{7,6},{8,9},{9,8},{10,11... | collective-permute-start | bytes 11010056 | tf_op jit(solution)/shard_map/ppermute | solution.py:491
  25.0 12.0 %collective-permute-start.2 = (bf16[512,3584]{1,0:T(8,128)(2,1)S(1)}, bf16[512,3584]{1,0:T(8,128)(2,1)}, u32[]{:S(2)}, u32[]{:S(2)}) collective-permute-start(bf16[512,3584]{1,0:T(8,128)(2,1)S(1)} %dynamic-slice_bitcast_fusion), channel_id=1, source_target_pairs={{0,1},{1,0},{2,3},{3,2},{4,5},{5,4},{6,7},{7,6},{8,9},{9,8},{10,11... | collective-permute-start | bytes 11010056 | tf_op jit(solution)/shard_map/ppermute | solution.py:491
  26.4 5.3 %copy-start.4 = (bf16[3584,512]{1,0:T(8,128)(2,1)}, bf16[3584,512]{1,0:T(8,128)(2,1)S(1)}, u32[]{:S(2)}) copy-start(bf16[3584,512]{1,0:T(8,128)(2,1)S(1)} %collective-permute-done.in_far_ref) | copy-start | bytes 11010052
  31.7 1.8 %copy-start.5 = (bf16[3584,512]{1,0:T(8,128)(2,1)}, bf16[3584,512]{1,0:T(8,128)(2,1)S(1)}, u32[]{:S(2)}) copy-start(bf16[3584,512]{1,0:T(8,128)(2,1)S(1)} %collective-permute-done.1.up_far_ref) | copy-start | bytes 11010052
  95.0 10.1 %copy-start.2 = (bf16[1,64,1024]{2,1,0:T(8,128)(2,1)S(1)}, bf16[1,64,1024]{2,1,0:T(8,128)(2,1)}, u32[]{:S(2)}) copy-start(bf16[1,64,1024]{2,1,0:T(8,128)(2,1)} %param.20) | copy-start | bytes 393220
  95.0 10.1 %copy-start.3 = (bf16[1,128,64]{1,2,0:T(8,128)(2,1)S(1)}, bf16[1,128,64]{1,2,0:T(8,128)(2,1)}, u32[]{:S(2)}) copy-start(bf16[1,128,64]{1,2,0:T(8,128)(2,1)} %param.18) | copy-start | bytes 49156
  95.0 10.3 %copy-start.1 = (bf16[1,128,512]{2,1,0:T(8,128)(2,1)S(1)}, bf16[1,128,512]{2,1,0:T(8,128)(2,1)}, u32[]{:S(2)}) copy-start(bf16[1,128,512]{2,1,0:T(8,128)(2,1)} %param.17) | copy-start | bytes 393220
  95.0 67.6 %all-to-all-start.1 = ((bf16[128,18,8,128]{3,2,1,0:T(8,128)(2,1)}), bf16[128,18,8,128]{3,2,1,0:T(8,128)(2,1)}, u32[]{:S(2)}, u32[]{:S(2)}) async-start(bf16[128,18,8,128]{3,2,1,0:T(8,128)(2,1)} %bitcast.38), calls=%async_computation.1 | async-start | bytes 9437184 | tf_op jit(solution)/shard_map/all_to_all | solution.py:497
  106.8 2.5 %collective-permute-start.3 = (f32[1,128,640]{2,1,0:T(8,128)S(1)}, f32[1,128,640]{2,1,0:T(8,128)S(1)}, u32[]{:S(2)}, u32[]{:S(2)}) collective-permute-start(f32[1,128,640]{2,1,0:T(8,128)S(1)} %pad_maximum_fusion), channel_id=1, source_target_pairs={{0,1},{1,0},{2,3},{3,2},{4,5},{5,4},{6,7},{7,6},{8,9},{9,8},{10,11... | collective-permute-start | bytes 983048 | tf_op jit(solution)/shard_map/ppermute | solution.py:462

commit v6 on v5

--- a/solution.py
+++ b/solution.py
@@ -373,12 +373,26 @@
     return jnp.concatenate(parts, axis=0).astype(BF16)
 
 
-def combine_kernel(
-    back_ref, routes_ref, gates_ref, after_ref, out_ref, message, routes, gates, spread, total, pick, sem, out_sem
-):
+def gates_kernel(routes_ref, gates_ref, out_ref):
+    count = out_ref.shape[1] // 2
+    for core in range(2):
+        out_ref[:, core * count : (core + 1) * count] = spread_gates(core, routes_ref[...], gates_ref[...], count)
+
+
+def gate_matrix(routes, gates, dp_count):
+    return pl.pallas_call(
+        gates_kernel,
+        in_specs=[VMEM, VMEM],
+        out_specs=VMEM,
+        out_shape=jax.ShapeDtypeStruct((2 * routes.shape[1], 2 * dp_count * CAP), BF16),
+        compiler_params=PARAMS,
+        name="gates",
+    )(routes, gates)
+
+
+def combine_kernel(back_ref, gates_ref, after_ref, out_ref, message, spread, total, pick, sem, out_sem):
     dp_count = message.shape[0]
     tiles = message.shape[1] // 2
-    count = dp_count * CAP
     tokens = total.shape[0]
     parts = groups_of(total.shape[1])
     loads, stores = [], []
@@ -388,15 +402,9 @@
         for core in range(2):
             part = pl.ds(core * tiles + tile, blocks + 1)
             loads.append(pltpu.make_async_copy(back_ref.at[:, part], message.at[:, part], sem.at[2 * g + core]))
-    first = [
-        pltpu.make_async_copy(routes_ref, routes, sem.at[len(loads)]),
-        pltpu.make_async_copy(gates_ref, gates, sem.at[len(loads) + 1]),
-    ]
-    start(first + loads)
+    gates_load = pltpu.make_async_copy(gates_ref, spread, sem.at[len(loads)])
+    start(loads[:2] + [gates_load] + loads[2:])
     fill_pick(pick, dp_count)
-    wait(first)
-    for core in range(2):
-        spread[:, core * count : (core + 1) * count] = spread_gates(core, routes[...], gates[...], count)
 
     def picked(g):
         _, blocks, tile = parts[g]
@@ -404,6 +412,7 @@
 
     wait(loads[:2])
     rest = picked(0)
+    wait([gates_load])
     for g, (at, blocks, tile) in enumerate(parts):
         wait(loads[2 * g + 2 : 2 * g + 4])
         rows = []
@@ -417,30 +426,28 @@
     wait(stores)
 
 
-def combine(back, routes, gates, after):
+def combine(back, gates, after):
     dp_count, tiles = back.shape[0], back.shape[1]
-    tokens = routes.shape[1]
+    tokens = gates.shape[0] // 2
     blocks = tiles // 2 - -(-(tiles // 2) // TILES)
     parts = len(groups_of(blocks * BLOCK))
     out = jax.ShapeDtypeStruct((tokens, blocks * BLOCK), BF16)
     return pl.pallas_call(
         combine_kernel,
-        in_specs=[HBM, HBM, HBM, HBM],
+        in_specs=[HBM, HBM, HBM],
         out_specs=HBM,
         out_shape=out,
         scratch_shapes=[
             pltpu.VMEM(back.shape, BF16),
-            pltpu.VMEM(routes.shape, jnp.int32),
-            pltpu.VMEM(gates.shape, F32),
-            pltpu.VMEM((2 * tokens, 2 * dp_count * CAP), BF16),
+            pltpu.VMEM(gates.shape, BF16),
             pltpu.VMEM(out.shape, BF16),
             pltpu.VMEM((4 * dp_count, 4 * dp_count), BF16),
-            pltpu.SemaphoreType.DMA((2 * parts + 2,)),
+            pltpu.SemaphoreType.DMA((2 * parts + 1,)),
             pltpu.SemaphoreType.DMA((parts,)),
         ],
         compiler_params=PARAMS,
         name="combine",
-    )(back, routes, gates, after)
+    )(back, gates, after)
 
 
 def attention(query_latent, query_rope, cache_latent, cache_rope, lengths):
@@ -496,7 +503,8 @@
     back = back.reshape(2 * parts[0], parts[1] // 2, MAIN, BLOCK)
     returned = lax.all_to_all(back, ("dp", "tp"), split_axis=0, concat_axis=0, tiled=True)
     attn_out = attention(query_latent, query_rope, cache_latent, cache_rope, lengths)
-    moe_out = combine(returned.reshape(parts), routes, route_gates.T, attn_out)
+    gates = gate_matrix(routes, route_gates.T, dp_count)
+    moe_out = combine(returned.reshape(parts), gates, attn_out)
     return (moe_out, attn_out)
 
 

time: 168 us -> 168 us (level)
  Pallas kernels: 28.4 us -> 30.8 us
  waiting for transfers between devices: 101 us -> 98.9 us
    pallas_call x1 -> x2, Pallas kernels: 4.79 us -> 7.25 us  [the longest x1 4.8 us: combine(): pl.pallas_call(combine_kernel, in_specs=[HBM, HBM, HBM], out_specs=HBM, o...]
  transfers between devices with their start and end apart: 6 -> 6, of which waited for: 6 -> 5; matrix products, arithmetic and copies ran while one was open for 6% -> 6% of each run, Pallas kernels for 0% -> 1%
where the time goes in v6:
time: 168 us
  waiting for transfers between devices  98.9 us (59%)
  Pallas kernels  30.8 us (18%)
  starting transfers between devices  24.7 us (15%)
  local copies, waits for them, and re-layouts  9.03 us (5%)
    all_to_all x1, waiting for transfers between devices, body(): lax.all_to_all(back, ('dp', 'tp'), split_axis=0, concat_axis=0, tiled=True)  50.9 us
    all_to_all x1, waiting for transfers between devices, body(): lax.all_to_all(outbound, 'dp', split_axis=0, concat_axis=0, tiled=True)  38.5 us
    pallas_call x1, Pallas kernels, experts(): pl.pallas_call(expert_kernel, in_specs=[SMEM] + [HBM] * 7, out_specs=HBM,...  19.4 us
    all_to_all x1, starting transfers between devices, body(): lax.all_to_all(outbound, 'dp', split_axis=0, concat_axis=0, tiled=True)  12.2 us
    ppermute x3, waiting for transfers between devices, swap(): lax.ppermute(lax.dynamic_index_in_dim(weight, 1 - index, 0, False), 'tp',...  9.46 us
    all_to_all x1, starting transfers between devices, body(): lax.all_to_all(back, ('dp', 'tp'), split_axis=0, concat_axis=0, tiled=True)  9.37 us
    squeeze x3, local copies, waits for them, and re-layouts, swap(): lax.dynamic_index_in_dim(weight, 1 - index, 0, False)  6.83 us
    pallas_call x1, Pallas kernels, combine(): pl.pallas_call(combine_kernel, in_specs=[HBM, HBM, HBM], out_specs=HBM, o...  4.8 us
  transfers between devices with their start and end apart: 6, of which 5 were waited for; matrix products, arithmetic and copies ran while one was open for 6% of the time, Pallas kernels for 1%

profile of v6, /device:TPU:1, one launch (start us, length us, event | category | flops | bytes accessed | tf_op | source)
XLA Modules:
  0.0 167.6 jit_solution(5275228741674450460)
XLA Ops:
  0.6 0.0 copy-start
  0.6 4.2 %dispatch.1 = bf16[64,35,8,128]{3,2,1,0:T(8,128)(2,1)} custom-call(s32[1]{0:T(128)} %bitcast.core_ref, s32[8,128]{1,0:T(8,128)} %bitcast.40, bf16[128,3584]{1,0:T(8,128)(2,1)} %tokens_ref.1), custom_call_target="tpu_custom_call" | custom-call | tf_op jit(solution)/shard_map/dispatch/pallas_call | solution.py:194
  4.8 12.2 %all-to-all-start = ((bf16[64,35,8,128]{3,2,1,0:T(8,128)(2,1)}), bf16[64,35,8,128]{3,2,1,0:T(8,128)(2,1)}, u32[]{:S(2)}, u32[]{:S(2)}) async-start(bf16[64,35,8,128]{3,2,1,0:T(8,128)(2,1)} %dispatch.1), calls=%async_computation | async-start | bytes 9175040 | tf_op jit(solution)/shard_map/all_to_all | solution.py:495
  17.0 2.3 %dynamic-slice_bitcast_fusion.2 = bf16[3584,512]{1,0:T(8,128)(2,1)S(1)} fusion(bf16[2,3584,512]{2,1,0:T(8,128)(2,1)} %in_own_ref.1, s32[]{:T(128)S(6)} %select_n.16), kind=kLoop, calls=%fused_computation.2 | loop fusion | bytes 7340036 | tf_op jit(solution)/shard_map/jit(dynamic_index_in_dim)/squeeze | solution.py:498
  19.3 1.0 collective-permute-start
  20.4 2.3 %dynamic-slice_bitcast_fusion.1 = bf16[3584,512]{1,0:T(8,128)(2,1)S(1)} fusion(bf16[2,3584,512]{2,1,0:T(8,128)(2,1)} %up_own_ref.1, s32[]{:T(128)S(6)} %select_n.16), kind=kLoop, calls=%fused_computation.1 | loop fusion | bytes 7340036 | tf_op jit(solution)/shard_map/jit(dynamic_index_in_dim)/squeeze | solution.py:498
  22.7 0.1 collective-permute-start.1
  22.8 2.3 %dynamic-slice_bitcast_fusion = bf16[512,3584]{1,0:T(8,128)(2,1)S(1)} fusion(bf16[2,512,3584]{2,1,0:T(8,128)(2,1)} %out_own_ref.1, s32[]{:T(128)S(6)} %select_n.16), kind=kLoop, calls=%fused_computation | loop fusion | bytes 7340036 | tf_op jit(solution)/shard_map/jit(dynamic_index_in_dim)/squeeze | solution.py:498
  25.0 0.8 collective-permute-start.2
  25.8 0.6 collective-permute-done.in_far_ref
  26.4 0.0 copy-start.4
  26.4 5.2 %collective-permute-done.1.up_far_ref = bf16[3584,512]{1,0:T(8,128)(2,1)S(1)} collective-permute-done((bf16[3584,512]{1,0:T(8,128)(2,1)S(1)}, bf16[3584,512]{1,0:T(8,128)(2,1)S(1)}, u32[]{:S(2)}, u32[]{:S(2)}) %collective-permute-start.1) | collective-permute-done | bytes 3670048 | tf_op jit(solution)/shard_map/ppermute | solution.py:498
  31.7 0.0 copy-done.4
  31.7 0.0 copy-start.5
  31.7 1.8 %copy-done.5 = bf16[3584,512]{1,0:T(8,128)(2,1)} copy-done((bf16[3584,512]{1,0:T(8,128)(2,1)}, bf16[3584,512]{1,0:T(8,128)(2,1)S(1)}, u32[]{:S(2)}) %copy-start.5) | copy-done | bytes 3670040
  33.5 3.6 %collective-permute-done.2.out_far_ref = bf16[512,3584]{1,0:T(8,128)(2,1)} collective-permute-done((bf16[512,3584]{1,0:T(8,128)(2,1)S(1)}, bf16[512,3584]{1,0:T(8,128)(2,1)}, u32[]{:S(2)}, u32[]{:S(2)}) %collective-permute-start.2) | collective-permute-done | bytes 3670048 | tf_op jit(solution)/shard_map/ppermute | solution.py:498
  37.0 38.5 %all-to-all-done.message_ref = bf16[64,35,8,128]{3,2,1,0:T(8,128)(2,1)} async-done(((bf16[64,35,8,128]{3,2,1,0:T(8,128)(2,1)}), bf16[64,35,8,128]{3,2,1,0:T(8,128)(2,1)}, u32[]{:S(2)}, u32[]{:S(2)}) %all-to-all-start) | async-done | bytes 4587552 | tf_op jit(solution)/shard_map/all_to_all | solution.py:495
  75.5 19.4 %experts.1 = bf16[64,36,8,128]{3,2,1,0:T(8,128)(2,1)} custom-call(s32[1]{0:T(128)} %bitcast.core_ref, bf16[64,35,8,128]{3,2,1,0:T(8,128)(2,1)} %all-to-all-done.message_ref, bf16[2,3584,512]{2,1,0:T(8,128)(2,1)} %in_own_ref.1, bf16[2,3584,512]{2,1,0:T(8,128)(2,1)} %up_own_ref.1, bf16[3584,512]{1,0:T(8,128)(2,1)} %copy-done.4, bf16[3584,512]{1,0:T(8,128)(2,1)} %copy-done.5, ...), custom_call_target="tpu_custom_call" | custom-call | flops 14092861440 | bytes 33554432 | tf_op jit(solution)/shard_map/experts/pallas_call | solution.py:326
  95.0 0.0 copy-start.2
  95.0 0.0 copy-start.3
  95.0 0.0 copy-start.1
  95.0 9.4 %all-to-all-start.1 = ((bf16[128,18,8,128]{3,2,1,0:T(8,128)(2,1)}), bf16[128,18,8,128]{3,2,1,0:T(8,128)(2,1)}, u32[]{:S(2)}, u32[]{:S(2)}) async-start(bf16[128,18,8,128]{3,2,1,0:T(8,128)(2,1)} %bitcast.38), calls=%async_computation.1 | async-start | bytes 9437184 | tf_op jit(solution)/shard_map/all_to_all | solution.py:504
  105.0 0.0 copy-done.2
  105.0 0.0 copy-done.3
  105.1 0.2 fusion.13
  105.3 0.0 copy-done
  105.3 0.0 copy-done.1
  105.3 0.6 select_reduce_fusion
  105.9 0.2 fusion.4
  106.1 0.4 fusion.1
  106.5 0.1 broadcast_in_dim.41
  106.6 0.1 broadcast_in_dim.40
  106.7 0.1 pad_maximum_fusion
  106.8 1.2 collective-permute-start.3
  108.0 2.4 %gates.1.gates_ref = bf16[256,1280]{1,0:T(8,128)(2,1)} custom-call(s32[8,128]{1,0:T(8,128)} %bitcast.41, f32[8,128]{1,0:T(8,128)} %bitcast.44), custom_call_target="tpu_custom_call" | custom-call | tf_op jit(solution)/shard_map/gates/pallas_call | solution.py:383
  110.4 0.1 copy.20
  110.5 0.1 copy.21
  110.6 0.0 collective-permute-done.3
  110.6 0.2 fusion.21
  110.9 0.8 fusion.11.after_ref
  111.7 50.9 %all-to-all-done.1 = bf16[128,18,8,128]{3,2,1,0:T(8,128)(2,1)} async-done(((bf16[128,18,8,128]{3,2,1,0:T(8,128)(2,1)}), bf16[128,18,8,128]{3,2,1,0:T(8,128)(2,1)}, u32[]{:S(2)}, u32[]{:S(2)}) %all-to-all-start.1) | async-done | bytes 4718624 | tf_op jit(solution)/shard_map/all_to_all | solution.py:504
  162.6 4.8 %combine.1 = bf16[128,1792]{1,0:T(8,128)(2,1)} custom-call(bf16[64,36,8,128]{3,2,1,0:T(8,128)(2,1)} %bitcast.6.back_ref, bf16[256,1280]{1,0:T(8,128)(2,1)} %gates.1.gates_ref, bf16[1,128,512]{2,1,0:T(8,128)(2,1)} %fusion.11.after_ref), custom_call_target="tpu_custom_call" | custom-call | tf_op jit(solution)/shard_map/combine/pallas_call | solution.py:435
  (1 shorter events, 0.0 us)
Async XLA Ops:
  0.6 104.7 %copy-start = (bf16[1,1024,512]{2,1,0:T(8,128)(2,1)S(1)}, bf16[1,1024,512]{2,1,0:T(8,128)(2,1)}, u32[]{:S(2)}) copy-start(bf16[1,1024,512]{2,1,0:T(8,128)(2,1)} %param.19) | copy-start | bytes 3145732
  4.8 70.7 %all-to-all-start = ((bf16[64,35,8,128]{3,2,1,0:T(8,128)(2,1)}), bf16[64,35,8,128]{3,2,1,0:T(8,128)(2,1)}, u32[]{:S(2)}, u32[]{:S(2)}) async-start(bf16[64,35,8,128]{3,2,1,0:T(8,128)(2,1)} %dispatch.1), calls=%async_computation | async-start | bytes 9175040 | tf_op jit(solution)/shard_map/all_to_all | solution.py:495
  19.3 7.1 %collective-permute-start = (bf16[3584,512]{1,0:T(8,128)(2,1)S(1)}, bf16[3584,512]{1,0:T(8,128)(2,1)S(1)}, u32[]{:S(2)}, u32[]{:S(2)}) collective-permute-start(bf16[3584,512]{1,0:T(8,128)(2,1)S(1)} %dynamic-slice_bitcast_fusion.2), channel_id=1, source_target_pairs={{0,1},{1,0},{2,3},{3,2},{4,5},{5,4},{6,7},{7,6},{8,9},{9,8},{10,11... | collective-permute-start | bytes 11010056 | tf_op jit(solution)/shard_map/ppermute | solution.py:498
  22.7 9.0 %collective-permute-start.1 = (bf16[3584,512]{1,0:T(8,128)(2,1)S(1)}, bf16[3584,512]{1,0:T(8,128)(2,1)S(1)}, u32[]{:S(2)}, u32[]{:S(2)}) collective-permute-start(bf16[3584,512]{1,0:T(8,128)(2,1)S(1)} %dynamic-slice_bitcast_fusion.1), channel_id=1, source_target_pairs={{0,1},{1,0},{2,3},{3,2},{4,5},{5,4},{6,7},{7,6},{8,9},{9,8},{10,11... | collective-permute-start | bytes 11010056 | tf_op jit(solution)/shard_map/ppermute | solution.py:498
  25.0 12.0 %collective-permute-start.2 = (bf16[512,3584]{1,0:T(8,128)(2,1)S(1)}, bf16[512,3584]{1,0:T(8,128)(2,1)}, u32[]{:S(2)}, u32[]{:S(2)}) collective-permute-start(bf16[512,3584]{1,0:T(8,128)(2,1)S(1)} %dynamic-slice_bitcast_fusion), channel_id=1, source_target_pairs={{0,1},{1,0},{2,3},{3,2},{4,5},{5,4},{6,7},{7,6},{8,9},{9,8},{10,11... | collective-permute-start | bytes 11010056 | tf_op jit(solution)/shard_map/ppermute | solution.py:498
  26.4 5.3 %copy-start.4 = (bf16[3584,512]{1,0:T(8,128)(2,1)}, bf16[3584,512]{1,0:T(8,128)(2,1)S(1)}, u32[]{:S(2)}) copy-start(bf16[3584,512]{1,0:T(8,128)(2,1)S(1)} %collective-permute-done.in_far_ref) | copy-start | bytes 11010052
  31.7 1.8 %copy-start.5 = (bf16[3584,512]{1,0:T(8,128)(2,1)}, bf16[3584,512]{1,0:T(8,128)(2,1)S(1)}, u32[]{:S(2)}) copy-start(bf16[3584,512]{1,0:T(8,128)(2,1)S(1)} %collective-permute-done.1.up_far_ref) | copy-start | bytes 11010052
  95.0 10.1 %copy-start.2 = (bf16[1,64,1024]{2,1,0:T(8,128)(2,1)S(1)}, bf16[1,64,1024]{2,1,0:T(8,128)(2,1)}, u32[]{:S(2)}) copy-start(bf16[1,64,1024]{2,1,0:T(8,128)(2,1)} %param.20) | copy-start | bytes 393220
  95.0 10.1 %copy-start.3 = (bf16[1,128,64]{1,2,0:T(8,128)(2,1)S(1)}, bf16[1,128,64]{1,2,0:T(8,128)(2,1)}, u32[]{:S(2)}) copy-start(bf16[1,128,64]{1,2,0:T(8,128)(2,1)} %param.18) | copy-start | bytes 49156
  95.0 10.3 %copy-start.1 = (bf16[1,128,512]{2,1,0:T(8,128)(2,1)S(1)}, bf16[1,128,512]{2,1,0:T(8,128)(2,1)}, u32[]{:S(2)}) copy-start(bf16[1,128,512]{2,1,0:T(8,128)(2,1)} %param.17) | copy-start | bytes 393220
  95.0 67.6 %all-to-all-start.1 = ((bf16[128,18,8,128]{3,2,1,0:T(8,128)(2,1)}), bf16[128,18,8,128]{3,2,1,0:T(8,128)(2,1)}, u32[]{:S(2)}, u32[]{:S(2)}) async-start(bf16[128,18,8,128]{3,2,1,0:T(8,128)(2,1)} %bitcast.38), calls=%async_computation.1 | async-start | bytes 9437184 | tf_op jit(solution)/shard_map/all_to_all | solution.py:504
  106.8 3.9 %collective-permute-start.3 = (f32[1,128,640]{2,1,0:T(8,128)S(1)}, f32[1,128,640]{2,1,0:T(8,128)S(1)}, u32[]{:S(2)}, u32[]{:S(2)}) collective-permute-start(f32[1,128,640]{2,1,0:T(8,128)S(1)} %pad_maximum_fusion), channel_id=1, source_target_pairs={{0,1},{1,0},{2,3},{3,2},{4,5},{5,4},{6,7},{7,6},{8,9},{9,8},{10,11... | collective-permute-start | bytes 983048 | tf_op jit(solution)/shard_map/ppermute | solution.py:469
